TPU v7x, 128 devices: a whole 4x4x4 slice. The times are simulated.
128 devices in a mesh: inp: 32 (over z, x, core), head: 4 (over y).
Axes of the slice: x: 4, y: 4, z: 4, core: 2. Of those that a mesh axis runs over, the one named last changes fastest.
Arguments:
- inputs: bfloat16 [262144, 256], P('inp'), may hold values from -6 to 6
- input_modality: int32 [2048], P('inp'), may hold values from 0 to 2
- queries: bfloat16 [262144, 256], P(('inp', 'head')), may hold values from -6 to 6
- query_modality: int32 [2048], P(('inp', 'head')), may hold values from 0 to 2
- modality_embed: float32 [3, 256], replicated, may hold values from -3 to 3
- latents: float32 [512, 1024], replicated, may hold values from -6 to 6
- ln_in_gain: float32 [256], replicated, may hold values from 0.1 to 1.9
- ln_lat_gain: float32 [1024], replicated, may hold values from 0.1 to 1.9
- enc_wq: bfloat16 [1024, 1024], P(None, 'head'), may hold values from -0.75 to 0.75
- enc_wkv: bfloat16 [2, 256, 1024], P(None, None, 'head'), may hold values from -0.375 to 0.375
- enc_bias: float32 [3, 16, 512], P(None, 'head'), may hold values from -4 to 320, as said below
- enc_wo: bfloat16 [1024, 1024], P('head'), may hold values from -0.1875 to 0.1875
- self_gain: float32 [1024], replicated, may hold values from 0.1 to 1.9
- self_wqkv: bfloat16 [3, 1024, 1024], P(None, None, 'head'), may hold values from -0.1875 to 0.1875
- self_bias: float32 [16, 512, 512], P('head', 'inp'), may hold values from -4 to 320, as said below
- self_wo: bfloat16 [1024, 1024], P('head'), may hold values from -0.1875 to 0.1875
- mlp_gain: float32 [1024], replicated, may hold values from 0.1 to 1.9
- mlp_w1: bfloat16 [1024, 4096], P(None, 'head'), may hold values from -0.1875 to 0.1875
- mlp_w2: bfloat16 [4096, 1024], P('head'), may hold values from -0.09375 to 0.09375
- dec_gain: float32 [1024], replicated, may hold values from 0.1 to 1.9
- dec_wkv: bfloat16 [2, 1024, 1024], replicated, may hold values from -0.1875 to 0.1875
- query_gain: float32 [256], replicated, may hold values from 0.1 to 1.9
- dec_wq: bfloat16 [256, 1024], replicated, may hold values from -0.375 to 0.375
- dec_bias: float32 [3, 16, 512], replicated, may hold values from -4 to 320, as said below
- dec_wo: bfloat16 [1024, 256], replicated, may hold values from -0.375 to 0.375
Outputs:
- decoded: float32 [262144, 256], P(('inp', 'head'))
Inputs may be any that keep to these rules, and one draw needn't show every extreme that they name: `enc_bias`: score biases. `self_bias`: score biases. `dec_bias`: score biases.
All inputs are finite; a program needn't handle non-finite values.
Results may differ from a plain program's by a relative error of at most 0.017.
Values may be sent and summed in bfloat16 or wider, within the bound.
No kernel may reach another device: no remote copies, remote signals or barrier semaphores. Data moves between devices by JAX's collectives and lax.ppermute only.
A program may use at most 192 MiB of HBM per device.

v0:
```python
import functools
import math

import jax
import jax.numpy as jnp
from jax import lax
from jax.experimental import pallas as pl
from jax.experimental.pallas import tpu as pltpu
from jax.sharding import PartitionSpec as P

HSZ = 64
MODS = 3
MBLK = 128
EPSILON = 1e-05
LOG2E = 1.4426950408889634
SCALE2 = LOG2E / math.sqrt(HSZ)
NEG_FLOOR = -1e30
BF = jnp.bfloat16
F32 = jnp.float32
MIB = 2**20
EXTRA = 128


def dot(a, b):
    return jnp.dot(a, b, preferred_element_type=F32)


def dot_nt(a, b):
    return lax.dot_general(a, b, (((1,), (1,)), ((), ())), preferred_element_type=F32)


def layer_norm(values, gain):
    centered = values - jnp.mean(values, axis=-1, keepdims=True)
    variance = jnp.mean(centered * centered, axis=-1, keepdims=True)
    return centered * lax.rsqrt(variance + EPSILON) * gain


def three_parts(values):
    high = values.astype(BF)
    rest = values - high.astype(F32)
    mid = rest.astype(BF)
    low = (rest - mid.astype(F32)).astype(BF)
    return high.astype(F32), mid.astype(F32), low.astype(F32)


def bias_rows(bias, rows):
    index = lax.broadcasted_iota(jnp.int32, (rows, bias.shape[1]), 0)
    block = jnp.zeros((rows, bias.shape[1]), F32)
    for part, piece in enumerate(three_parts(bias)):
        for mod in range(MODS):
            block = jnp.where(index == MODS * part + mod, piece[mod : mod + 1, :], block)
    return block


def modality_hot(mod, shape, dim):
    index = lax.broadcasted_iota(jnp.int32, shape, dim)
    hit = (index == mod) | (index == mod + MODS) | (index == mod + 2 * MODS)
    return jnp.where(hit, 1.0, 0.0).astype(BF)


def embed_norm(mod_ref, first, x_ref, table_ref, gain, n_ref):
    for b in range(x_ref.shape[0] // MBLK):
        rows = slice(b * MBLK, (b + 1) * MBLK)
        mod = mod_ref[first + b]
        embedded = x_ref[rows, :].astype(F32) + table_ref[pl.ds(mod, 1), :]
        n_ref[rows, :] = layer_norm(embedded, gain).astype(BF)


def encode_kernel(
    heads,
    mod_ref,
    x_ref,
    table_ref,
    gain_ref,
    lat_ref,
    lat_gain_ref,
    wq_ref,
    wkv_ref,
    bias_ref,
    out_ref,
    qx_ref,
    wvt_ref,
    n_ref,
    hot_ref,
    m_ref,
    acc_ref,
):
    step = pl.program_id(0)
    blocks = x_ref.shape[0] // MBLK
    lat_count = lat_ref.shape[0]

    @pl.when(step == 0)
    def _():
        normed = layer_norm(lat_ref[...], lat_gain_ref[...]).astype(BF)
        query = (dot(normed, wq_ref[...]) * SCALE2).T
        qx_ref[...] = jnp.zeros(qx_ref.shape, BF)
        for h in range(heads):
            half = (h % 2) * HSZ
            qx_ref[h, half : half + HSZ, :] = query[h * HSZ : (h + 1) * HSZ, :].astype(BF)
            qx_ref[h, 128:144, :] = bias_rows(bias_ref[:, h, :] * LOG2E, 16).astype(BF)
        wvt_ref[...] = wkv_ref[1].T
        m_ref[...] = jnp.full(m_ref.shape, NEG_FLOOR, F32)
        acc_ref[...] = jnp.zeros(acc_ref.shape, F32)

    embed_norm(mod_ref, step * blocks, x_ref, table_ref, gain_ref[...], n_ref)
    for b in range(blocks):
        mod = mod_ref[step * blocks + b]
        hot_ref[b * MBLK : (b + 1) * MBLK, :] = modality_hot(mod, (MBLK, 128), 1)
    normed = n_ref[...]
    hot = hot_ref[...]
    keys = dot(normed, wkv_ref[0]).astype(BF)
    values_t = dot_nt(wvt_ref[...], normed).astype(BF)
    ones = jnp.ones((HSZ, x_ref.shape[0]), BF)
    for h in range(heads):
        pair = (h // 2) * 128
        left = jnp.concatenate([keys[:, pair : pair + 128], hot], axis=1)
        scores = dot(left, qx_ref[h])
        old = m_ref[h]
        new = jnp.maximum(old, jnp.max(scores, axis=0, keepdims=True))
        m_ref[h] = new
        weights = jnp.exp2(scores - new).astype(BF)
        values_h = jnp.concatenate([values_t[h * HSZ : (h + 1) * HSZ, :], ones], axis=0)
        acc_ref[h] = acc_ref[h] * jnp.exp2(old - new) + dot(values_h, weights)

    @pl.when(step == pl.num_programs(0) - 1)
    def _():
        index = lax.broadcasted_iota(jnp.int32, (EXTRA, lat_count), 0)
        extra = jnp.zeros((EXTRA, lat_count), F32)
        pieces = []
        for h in range(heads):
            acc = acc_ref[h]
            total = acc[HSZ : HSZ + 1, :]
            pieces.append(acc[:HSZ, :] / total)
            for part, piece in enumerate(three_parts(m_ref[h] + jnp.log2(total))):
                extra = jnp.where(index == heads * part + h, piece, extra)
        out_ref[...] = jnp.concatenate(pieces + [extra], axis=0).T.astype(BF)


def encode(inputs, input_modality, table, gain, latents, lat_gain, wq, wkv, bias):
    points, width = inputs.shape
    heads = bias.shape[1]
    lat_count, lat_width = latents.shape
    cols = heads * HSZ
    tile = math.gcd(points, 1024)
    whole = lambda *shape: pl.BlockSpec(shape, lambda i, mod: (0,) * len(shape))
    return pl.pallas_call(
        functools.partial(encode_kernel, heads),
        grid_spec=pltpu.PrefetchScalarGridSpec(
            num_scalar_prefetch=1,
            grid=(points // tile,),
            in_specs=[
                pl.BlockSpec((tile, width), lambda i, mod: (i, 0)),
                whole(MODS, width),
                whole(1, width),
                whole(lat_count, lat_width),
                whole(1, lat_width),
                whole(lat_width, cols),
                whole(2, width, cols),
                whole(MODS, heads, lat_count),
            ],
            out_specs=whole(lat_count, cols + EXTRA),
            scratch_shapes=[
                pltpu.VMEM((heads, 256, lat_count), BF),
                pltpu.VMEM((cols, width), BF),
                pltpu.VMEM((tile, width), BF),
                pltpu.VMEM((tile, 128), BF),
                pltpu.VMEM((heads, 1, lat_count), F32),
                pltpu.VMEM((heads, 128, lat_count), F32),
            ],
        ),
        out_shape=jax.ShapeDtypeStruct((lat_count, cols + EXTRA), BF),
        compiler_params=pltpu.CompilerParams(vmem_limit_bytes=48 * MIB),
        name="encode",
    )(input_modality, inputs, table, gain, latents, lat_gain, wq, wkv, bias)


def small_call(kernel, name, outs, *args):
    return pl.pallas_call(
        kernel,
        out_shape=outs,
        in_specs=[pl.BlockSpec(memory_space=pltpu.VMEM)] * len(args),
        out_specs=jax.tree.map(lambda _: pl.BlockSpec(memory_space=pltpu.VMEM), outs),
        compiler_params=pltpu.CompilerParams(vmem_limit_bytes=24 * MIB),
        name=name,
    )(*args)


def merge_kernel(heads, part_ref, wo_ref, out_ref):
    cols = heads * HSZ
    extra = part_ref[:, :, cols:].astype(F32)
    sources, rows, _ = extra.shape
    lse = extra[:, :, :heads]
    for part in range(1, 3):
        lse = lse + extra[:, :, heads * part : heads * (part + 1)]
    top = jnp.max(lse, axis=0, keepdims=True)
    factor = jnp.exp2(lse - top)
    factor = factor / jnp.sum(factor, axis=0, keepdims=True)
    lane = lax.broadcasted_iota(jnp.int32, (sources, rows, cols), 2)
    spread = jnp.zeros((sources, rows, cols), F32)
    for h in range(heads):
        spread = jnp.where(lane // HSZ == h, factor[:, :, h : h + 1], spread)
    attended = jnp.sum(part_ref[:, :, :cols].astype(F32) * spread, axis=0)
    out_ref[...] = dot(attended.astype(BF), wo_ref[...])


def project_kernel(a_ref, b_ref, c_ref, d_ref, lat_ref, gain_ref, w_ref, lat_out, q_out, kv_out):
    lat = lat_ref[...] + ((a_ref[...] + b_ref[...]) + (c_ref[...] + d_ref[...]))
    lat_out[...] = lat
    normed = layer_norm(lat, gain_ref[...]).astype(BF)
    cols = w_ref.shape[2]
    q_out[...] = (dot(normed, w_ref[0]) * SCALE2).astype(BF)
    kv_out[:, :cols] = dot(normed, w_ref[1]).astype(BF)
    kv_out[:, cols:] = dot(normed, w_ref[2]).astype(BF)


def attend_kernel(heads, q_ref, kv_ref, bias_ref, wo_ref, out_ref):
    cols = heads * HSZ
    query = q_ref[...]
    rows = query.shape[0]
    keys = kv_ref[:, :cols]
    values = kv_ref[:, cols:]
    lane = lax.broadcasted_iota(jnp.int32, (rows, cols), 1) // HSZ
    mixed = jnp.zeros((rows, cols), F32)
    for h in range(heads):
        own = jnp.where(lane == h, query.astype(F32), 0.0).astype(BF)
        scores = dot_nt(own, keys) + bias_ref[h] * LOG2E
        weights = jnp.exp2(scores - jnp.max(scores, axis=1, keepdims=True))
        total = jnp.sum(weights, axis=1, keepdims=True)
        mixed = jnp.where(lane == h, dot(weights.astype(BF), values) / total, mixed)
    out_ref[...] = dot(mixed.astype(BF), wo_ref[...])


def mlp_kernel(a_ref, b_ref, c_ref, d_ref, lat_ref, gain_ref, w1_ref, w2_ref, lat_out, out_ref):
    lat = lat_ref[...] + ((a_ref[...] + b_ref[...]) + (c_ref[...] + d_ref[...]))
    lat_out[...] = lat
    normed = layer_norm(lat, gain_ref[...]).astype(BF)
    hidden = jax.nn.gelu(dot(normed, w1_ref[...]), approximate=True).astype(BF)
    out_ref[...] = dot(hidden, w2_ref[...])


def last_kernel(a_ref, b_ref, c_ref, d_ref, lat_ref, gain_ref, out_ref):
    lat = lat_ref[...] + ((a_ref[...] + b_ref[...]) + (c_ref[...] + d_ref[...]))
    out_ref[...] = layer_norm(lat, gain_ref[...]).astype(BF)


def query_kernel(
    heads,
    mod_ref,
    x_ref,
    table_ref,
    gain_ref,
    wq_ref,
    bias_ref,
    wo_ref,
    qt_ref,
    hot_ref,
    bias_out,
    wot_ref,
    wqt_ref,
    n_ref,
):
    step = pl.program_id(0)
    blocks = x_ref.shape[0] // MBLK

    @pl.when(step == 0)
    def _():
        wqt_ref[...] = wq_ref[...].T
        wot_ref[...] = wo_ref[...].T
        for h in range(heads):
            bias_out[h] = bias_rows(bias_ref[:, h, :] * LOG2E, 128).T.astype(BF)

    embed_norm(mod_ref, step * blocks, x_ref, table_ref, gain_ref[...], n_ref)
    for b in range(blocks):
        mod = mod_ref[step * blocks + b]
        hot_ref[:, b * MBLK : (b + 1) * MBLK] = modality_hot(mod, (128, MBLK), 0)
    qt_ref[...] = (dot_nt(wqt_ref[...], n_ref[...]) * SCALE2).astype(BF)


def prepare_queries(queries, query_modality, table, gain, wq, bias, wo):
    count, width = queries.shape
    heads, lat_count = bias.shape[1:]
    cols = heads * HSZ
    tile = math.gcd(count, 512)
    whole = lambda *shape: pl.BlockSpec(shape, lambda i, mod: (0,) * len(shape))
    return pl.pallas_call(
        functools.partial(query_kernel, heads),
        grid_spec=pltpu.PrefetchScalarGridSpec(
            num_scalar_prefetch=1,
            grid=(count // tile,),
            in_specs=[
                pl.BlockSpec((tile, width), lambda i, mod: (i, 0)),
                whole(MODS, width),
                whole(1, width),
                whole(width, cols),
                whole(MODS, heads, lat_count),
                whole(cols, width),
            ],
            out_specs=[
                pl.BlockSpec((cols, tile), lambda i, mod: (0, i)),
                pl.BlockSpec((128, tile), lambda i, mod: (0, i)),
                whole(heads, lat_count, 128),
                whole(width, cols),
            ],
            scratch_shapes=[
                pltpu.VMEM((cols, width), BF),
                pltpu.VMEM((tile, width), BF),
            ],
        ),
        out_shape=[
            jax.ShapeDtypeStruct((cols, count), BF),
            jax.ShapeDtypeStruct((128, count), BF),
            jax.ShapeDtypeStruct((heads, lat_count, 128), BF),
            jax.ShapeDtypeStruct((width, cols), BF),
        ],
        compiler_params=pltpu.CompilerParams(vmem_limit_bytes=32 * MIB),
        name="queries",
    )(query_modality, queries, table, gain, wq, bias, wo)


def decode_kernel(
    heads,
    mod_ref,
    x_ref,
    table_ref,
    lat_ref,
    wkv_ref,
    bias_ref,
    qt_ref,
    hot_ref,
    wot_ref,
    out_ref,
    kx_ref,
    vx_ref,
    mix_ref,
):
    step = pl.program_id(0)
    blocks = x_ref.shape[0] // MBLK
    lat_count = lat_ref.shape[0]

    @pl.when(step == 0)
    def _():
        normed = lat_ref[...]
        ones = jnp.ones((HSZ, lat_count), BF)
        lane = lax.broadcasted_iota(jnp.int32, (lat_count, 128), 1) // HSZ
        for pair in range(heads // 2):
            cols = slice(pair * 128, (pair + 1) * 128)
            keys = dot(normed, wkv_ref[0, :, cols])
            values = dot(normed, wkv_ref[1, :, cols]).T.astype(BF)
            for half in range(2):
                h = 2 * pair + half
                kx_ref[h, :, :128] = jnp.where(lane == half, keys, 0.0).astype(BF)
                kx_ref[h, :, 128:] = bias_ref[h]
                vx_ref[h, :HSZ, :] = values[half * HSZ : (half + 1) * HSZ, :]
                vx_ref[h, HSZ:, :] = ones

    hot = hot_ref[...]
    for h in range(heads):
        pair = (h // 2) * 128
        right = jnp.concatenate([qt_ref[pair : pair + 128, :], hot], axis=0)
        scores = dot(kx_ref[h], right)
        weights = jnp.exp2(scores - jnp.max(scores, axis=0, keepdims=True)).astype(BF)
        mixed = dot(vx_ref[h], weights)
        mix_ref[h * HSZ : (h + 1) * HSZ, :] = (mixed[:HSZ, :] / mixed[HSZ:, :]).astype(BF)
    decoded = dot(wot_ref[...], mix_ref[...]).T
    for b in range(blocks):
        rows = slice(b * MBLK, (b + 1) * MBLK)
        mod = mod_ref[step * blocks + b]
        embedded = x_ref[rows, :].astype(F32) + table_ref[pl.ds(mod, 1), :]
        out_ref[rows, :] = embedded + decoded[rows, :]


def decode(queries, query_modality, table, normed, wkv, prepared):
    queries_t, hot, bias, wo_t = prepared
    count, width = queries.shape
    heads, lat_count = bias.shape[:2]
    cols = heads * HSZ
    tile = math.gcd(count, 512)
    whole = lambda *shape: pl.BlockSpec(shape, lambda i, mod: (0,) * len(shape))
    return pl.pallas_call(
        functools.partial(decode_kernel, heads),
        grid_spec=pltpu.PrefetchScalarGridSpec(
            num_scalar_prefetch=1,
            grid=(count // tile,),
            in_specs=[
                pl.BlockSpec((tile, width), lambda i, mod: (i, 0)),
                whole(MODS, width),
                whole(lat_count, normed.shape[1]),
                whole(*wkv.shape),
                whole(heads, lat_count, 128),
                pl.BlockSpec((cols, tile), lambda i, mod: (0, i)),
                pl.BlockSpec((128, tile), lambda i, mod: (0, i)),
                whole(width, cols),
            ],
            out_specs=pl.BlockSpec((tile, width), lambda i, mod: (i, 0)),
            scratch_shapes=[
                pltpu.VMEM((heads, lat_count, 256), BF),
                pltpu.VMEM((heads, 128, lat_count), BF),
                pltpu.VMEM((cols, tile), BF),
            ],
        ),
        out_shape=jax.ShapeDtypeStruct((count, width), F32),
        compiler_params=pltpu.CompilerParams(vmem_limit_bytes=56 * MIB),
        name="decode",
    )(query_modality, queries, table, normed, wkv, bias, queries_t, hot, wo_t)


def share(rows):
    copies = jnp.broadcast_to(rows[None], (lax.axis_size("inp"),) + rows.shape)
    return lax.all_to_all(copies, "inp", 0, 0)


def head_parts(part):
    size = lax.axis_size("head")
    moved = [
        lax.ppermute(part, "head", [(i, (i + k) % size) for i in range(size)])
        for k in range(1, size)
    ]
    return [part] + moved


def body(
    inputs,
    input_modality,
    queries,
    query_modality,
    modality_embed,
    latents,
    ln_in_gain,
    ln_lat_gain,
    enc_wq,
    enc_wkv,
    enc_bias,
    enc_wo,
    self_gain,
    self_wqkv,
    self_bias,
    self_wo,
    mlp_gain,
    mlp_w1,
    mlp_w2,
    dec_gain,
    dec_wkv,
    query_gain,
    dec_wq,
    dec_bias,
    dec_wo,
):
    lat_count, width = latents.shape
    lat_rows = lat_count // lax.axis_size("inp")
    row_first = lax.axis_index("inp") * lat_rows
    heads = enc_bias.shape[1]
    cols = heads * HSZ
    row = lambda v: v.reshape(1, -1)
    shape = jax.ShapeDtypeStruct

    own = encode(
        inputs,
        input_modality,
        modality_embed,
        row(ln_in_gain),
        latents,
        row(ln_lat_gain),
        enc_wq,
        enc_wkv,
        enc_bias,
    )
    parts = lax.all_to_all(own.reshape(-1, lat_rows, own.shape[1]), "inp", 0, 0)
    enc_part = small_call(
        functools.partial(merge_kernel, heads), "merge", shape((lat_rows, width), F32), parts, enc_wo
    )
    prepared = prepare_queries(
        queries, query_modality, modality_embed, row(query_gain), dec_wq, dec_bias, dec_wo
    )
    latent_rows = lax.dynamic_slice_in_dim(latents, row_first, lat_rows, 0)
    lat_one, self_q, self_kv = small_call(
        project_kernel,
        "project",
        [
            shape((lat_rows, width), F32),
            shape((lat_rows, cols), BF),
            shape((lat_rows, 2 * cols), BF),
        ],
        *head_parts(enc_part),
        latent_rows,
        row(self_gain),
        self_wqkv,
    )
    all_kv = share(self_kv).reshape(lat_count, 2 * cols)
    self_part = small_call(
        functools.partial(attend_kernel, heads),
        "attend",
        shape((lat_rows, width), F32),
        self_q,
        all_kv,
        self_bias,
        self_wo,
    )
    lat_two, mlp_part = small_call(
        mlp_kernel,
        "mlp",
        [shape((lat_rows, width), F32), shape((lat_rows, width), F32)],
        *head_parts(self_part),
        lat_one,
        row(mlp_gain),
        mlp_w1,
        mlp_w2,
    )
    normed = small_call(
        last_kernel,
        "last",
        shape((lat_rows, width), BF),
        *head_parts(mlp_part),
        lat_two,
        row(dec_gain),
    )
    all_normed = share(normed).reshape(lat_count, width)
    return decode(queries, query_modality, modality_embed, all_normed, dec_wkv, prepared)


def solution(mesh):
    placed = (
        P("inp", None),
        P("inp"),
        P(("inp", "head"), None),
        P(("inp", "head")),
        P(),
        P(),
        P(),
        P(),
        P(None, "head"),
        P(None, None, "head"),
        P(None, "head", None),
        P("head", None),
        P(),
        P(None, None, "head"),
        P("head", "inp", None),
        P("head", None),
        P(),
        P(None, "head"),
        P("head", None),
        P(),
        P(),
        P(),
        P(),
        P(),
        P(),
    )
    return jax.shard_map(
        body, mesh=mesh, in_specs=placed, out_specs=P(("inp", "head"), None), check_vma=False
    )
```

profile of v0, /device:TPU:1, one launch (start us, length us, event | category | flops | bytes accessed | tf_op | source)
XLA Modules:
  0.0 176.7 jit_solution(15407963757326306151)
XLA Ops:
  0.0 1.6 copy-done.2
  1.6 1.0 copy-done.7
  2.6 0.9 copy-done.14
  3.6 0.7 copy-done.17
  4.3 0.7 copy-done.19
  5.0 0.7 copy-done.20
  5.7 0.7 copy-done.25
  6.4 0.7 copy-done.27
  7.0 38.9 %encode.1 = bf16[512,384]{1,0:T(8,128)(2,1)} custom-call(s32[64]{0:T(128)S(1)} %copy-done.27, bf16[8192,256]{1,0:T(8,128)(2,1)} %x_ref.3, f32[3,256]{1,0:T(4,128)S(1)} %copy-done.17, f32[1,256]{1,0:T(1,128)S(1)} %bitcast.14, f32[512,1024]{1,0:T(8,128)S(1)} %copy-done.2, f32[1,1024]{1,0:T(1,128)S(1)} %bitcast.10, bf16[1024,256]{1,0:T(8,128)(2,1)S(1)} %copy-done.7, ...), custom_call_target="tpu_custom_call" | custom-call | tf_op jit(solution)/shard_map/encode/pallas_call | solution.py:146
  45.9 9.6 %all-to-all-start = ((bf16[32,16,384]{2,1,0:T(8,128)(2,1)}), bf16[32,16,384]{2,1,0:T(8,128)(2,1)S(1)}, u32[]{:S(2)}, u32[]{:S(2)}) async-start(bf16[32,16,384]{2,1,0:T(8,128)(2,1)} %bitcast.2), calls=%async_computation | async-start | bytes 786432 | tf_op jit(solution)/shard_map/all_to_all | solution.py:467
  55.5 0.0 copy-start.10
  55.5 0.0 copy-start.15
  55.5 10.1 %all-to-all-done.part_ref = bf16[32,16,384]{2,1,0:T(8,128)(2,1)S(1)} async-done(((bf16[32,16,384]{2,1,0:T(8,128)(2,1)}), bf16[32,16,384]{2,1,0:T(8,128)(2,1)S(1)}, u32[]{:S(2)}, u32[]{:S(2)}) %all-to-all-start) | async-done | bytes 393248 | tf_op jit(solution)/shard_map/all_to_all | solution.py:467
  65.7 0.0 copy-done.11
  65.7 0.7 merge.1.a_ref
  66.4 2.7 %collective-permute-start.2 = (f32[16,1024]{1,0:T(8,128)S(1)}, f32[16,1024]{1,0:T(8,128)S(1)}, u32[]{:S(2)}, u32[]{:S(2)}) collective-permute-start(f32[16,1024]{1,0:T(8,128)S(1)} %merge.1.a_ref), channel_id=1, source_target_pairs={{0,3},{1,0},{2,1},{3,2},{4,7},{5,4},{6,5},{7,6},{8,11},{9,8},{10,9... | collective-permute-start | bytes 196616 | tf_op jit(solution)/shard_map/ppermute | solution.py:415
  69.1 0.3 collective-permute-start.1
  69.4 0.7 collective-permute-start
  70.1 0.8 constant_dynamic-slice_fusion.lat_ref
  71.0 0.0 collective-permute-done.2.d_ref
  71.0 2.8 %collective-permute-done.1.c_ref = f32[16,1024]{1,0:T(8,128)S(1)} collective-permute-done((f32[16,1024]{1,0:T(8,128)S(1)}, f32[16,1024]{1,0:T(8,128)S(1)}, u32[]{:S(2)}, u32[]{:S(2)}) %collective-permute-start.1) | collective-permute-done | bytes 65568 | tf_op jit(solution)/shard_map/ppermute | solution.py:415
  73.8 1.7 collective-permute-done.b_ref
  75.5 0.0 copy-done.21
  75.5 0.0 copy-done.6
  75.5 0.0 copy-start.22
  75.5 0.5 project.1
  76.0 0.1 broadcast_in_dim.4
  76.1 16.1 %all_to_all.15 = bf16[32,16,512]{2,1,0:T(8,128)(2,1)S(1)} all-to-all(bf16[32,16,512]{2,1,0:T(8,128)(2,1)S(1)} %broadcast_in_dim.4), channel_id=1, replica_groups=mesh['inp'=32,'head'=4] {'inp'}, dimensions={0} | all-to-all | bytes 1048576 | tf_op jit(solution)/shard_map/all_to_all | solution.py:409
  92.2 0.0 copy-done.10
  92.2 0.0 copy-done.15
  92.2 1.5 attend.1.a_ref
  93.6 0.3 collective-permute-start.5
  93.9 0.3 collective-permute-start.4
  94.3 0.8 collective-permute-start.3
  95.1 1.6 collective-permute-done.5.d_ref
  96.8 1.8 %collective-permute-done.4.c_ref = f32[16,1024]{1,0:T(8,128)S(1)} collective-permute-done((f32[16,1024]{1,0:T(8,128)S(1)}, f32[16,1024]{1,0:T(8,128)S(1)}, u32[]{:S(2)}, u32[]{:S(2)}) %collective-permute-start.4) | collective-permute-done | bytes 65568 | tf_op jit(solution)/shard_map/ppermute | solution.py:415
  98.6 1.8 %collective-permute-done.3.b_ref = f32[16,1024]{1,0:T(8,128)S(1)} collective-permute-done((f32[16,1024]{1,0:T(8,128)S(1)}, f32[16,1024]{1,0:T(8,128)S(1)}, u32[]{:S(2)}, u32[]{:S(2)}) %collective-permute-start.3) | collective-permute-done | bytes 65568 | tf_op jit(solution)/shard_map/ppermute | solution.py:415
  100.4 0.0 copy-done.3
  100.4 0.0 copy-done.4
  100.4 0.0 copy-done.22
  100.4 0.0 copy-start.23
  100.4 0.9 mlp.1
  101.3 0.0 copy-start.16
  101.3 0.0 copy-start.18
  101.3 0.0 copy-start.24
  101.3 0.0 copy-start.26
  101.3 0.7 collective-permute-start.8
  102.0 0.5 collective-permute-start.7
  102.5 0.3 collective-permute-start.6
  102.9 1.6 collective-permute-done.8.d_ref
  104.5 2.2 %collective-permute-done.7.c_ref = f32[16,1024]{1,0:T(8,128)S(1)} collective-permute-done((f32[16,1024]{1,0:T(8,128)S(1)}, f32[16,1024]{1,0:T(8,128)S(1)}, u32[]{:S(2)}, u32[]{:S(2)}) %collective-permute-start.7) | collective-permute-done | bytes 65568 | tf_op jit(solution)/shard_map/ppermute | solution.py:415
  106.7 0.7 collective-permute-done.6.b_ref
  107.4 0.2 last.1
  107.6 1.1 broadcast_in_dim.5
  108.7 7.0 %all-to-all-start.2 = ((bf16[32,16,1024]{2,1,0:T(8,128)(2,1)}), bf16[32,16,1024]{2,1,0:T(8,128)(2,1)S(1)}, u32[]{:S(2)}, u32[]{:S(2)}) async-start(bf16[32,16,1024]{2,1,0:T(8,128)(2,1)} %broadcast_in_dim.5), calls=%async_computation.2 | async-start | bytes 2097152 | tf_op jit(solution)/shard_map/all_to_all | solution.py:409
  115.7 5.0 %queries.1 = (bf16[1024,2048]{1,0:T(8,128)(2,1)S(1)}, bf16[128,2048]{1,0:T(8,128)(2,1)S(1)}, bf16[16,512,128]{2,1,0:T(8,128)(2,1)S(1)}, bf16[256,1024]{1,0:T(8,128)(2,1)S(1)}) custom-call(s32[16]{0:T(128)S(1)} %copy-done.24, bf16[2048,256]{1,0:T(8,128)(2,1)S(1)} %copy-done.1, f32[3,256]{1,0:T(4,128)S(1)} %copy-done.18, f32[1,256]{1,0:T(1,128)S(1)} %bitcast.15, ...), custom_call_target="tpu_custom_call" | custom-call | tf_op jit(solution)/shard_map/queries/pallas_call | solution.py:285
  120.7 0.0 copy-start
  120.8 2.0 %copy-done = bf16[1024,2048]{1,0:T(8,128)(2,1)} copy-done((bf16[1024,2048]{1,0:T(8,128)(2,1)}, bf16[1024,2048]{1,0:T(8,128)(2,1)S(1)}, u32[]{:S(2)}) %copy-start) | copy-done | bytes 4194328
  122.7 1.4 copy-done.5
  124.1 0.8 copy-done.12
  125.0 0.8 copy-done.13
  125.8 7.1 %all-to-all-done.2 = bf16[32,16,1024]{2,1,0:T(8,128)(2,1)S(1)} async-done(((bf16[32,16,1024]{2,1,0:T(8,128)(2,1)}), bf16[32,16,1024]{2,1,0:T(8,128)(2,1)S(1)}, u32[]{:S(2)}, u32[]{:S(2)}) %all-to-all-start.2) | async-done | bytes 1048608 | tf_op jit(solution)/shard_map/all_to_all | solution.py:409
  132.9 1.0 copy-done.28
  133.9 42.8 %decode.1 = f32[2048,256]{1,0:T(8,128)} custom-call(s32[16]{0:T(128)} %mod_ref.5, bf16[2048,256]{1,0:T(8,128)(2,1)} %x_ref.5, f32[3,256]{1,0:T(4,128)} %table_ref.5, bf16[512,1024]{1,0:T(8,128)(2,1)} %bitcast.16, bf16[2,1024,1024]{2,1,0:T(8,128)(2,1)} %wkv_ref.3, bf16[16,512,128]{2,1,0:T(8,128)(2,1)} %copy-done.5, bf16[1024,2048]{1,0:T(8,128)(2,1)} %copy-done, ...), custom_call_target="tpu_custom_call" | custom-call | tf_op jit(solution)/shard_map/decode/pallas_call | solution.py:379
  (28 shorter events, 0.0 us)
Async XLA Ops:
  0.0 1.6 copy-start.2
  1.6 1.0 copy-start.7
  2.6 0.9 copy-start.14
  3.6 0.7 copy-start.17
  4.3 0.7 copy-start.19
  5.0 0.7 copy-start.20
  5.7 0.7 copy-start.25
  6.4 0.7 copy-start.27
  7.0 58.6 %copy-start.11 = (bf16[256,1024]{1,0:T(8,128)(2,1)S(1)}, bf16[256,1024]{1,0:T(8,128)(2,1)}, u32[]{:S(2)}) copy-start(bf16[256,1024]{1,0:T(8,128)(2,1)} %wo_ref.3) | copy-start | bytes 1572868
  7.0 68.5 %copy-start.21 = (f32[1024]{0:T(1024)S(1)}, f32[1024]{0:T(1024)}, u32[]{:S(2)}) copy-start(f32[1024]{0:T(1024)} %param.37) | copy-start | bytes 12292
  45.9 29.6 %copy-start.6 = (bf16[3,1024,256]{2,1,0:T(8,128)(2,1)S(1)}, bf16[3,1024,256]{2,1,0:T(8,128)(2,1)}, u32[]{:S(2)}) copy-start(bf16[3,1024,256]{2,1,0:T(8,128)(2,1)} %w_ref.1) | copy-start | bytes 4718596
  45.9 19.8 %all-to-all-start = ((bf16[32,16,384]{2,1,0:T(8,128)(2,1)}), bf16[32,16,384]{2,1,0:T(8,128)(2,1)S(1)}, u32[]{:S(2)}, u32[]{:S(2)}) async-start(bf16[32,16,384]{2,1,0:T(8,128)(2,1)} %bitcast.2), calls=%async_computation | async-start | bytes 786432 | tf_op jit(solution)/shard_map/all_to_all | solution.py:467
  55.5 36.7 %copy-start.10 = (bf16[256,1024]{1,0:T(8,128)(2,1)S(1)}, bf16[256,1024]{1,0:T(8,128)(2,1)}, u32[]{:S(2)}) copy-start(bf16[256,1024]{1,0:T(8,128)(2,1)} %wo_ref.4) | copy-start | bytes 1572868
  55.5 36.6 %copy-start.15 = (f32[4,16,512]{2,1,0:T(8,128)S(1)}, f32[4,16,512]{2,1,0:T(8,128)}, u32[]{:S(2)}) copy-start(f32[4,16,512]{2,1,0:T(8,128)} %bias_ref.4) | copy-start | bytes 393220
  66.4 4.6 %collective-permute-start.2 = (f32[16,1024]{1,0:T(8,128)S(1)}, f32[16,1024]{1,0:T(8,128)S(1)}, u32[]{:S(2)}, u32[]{:S(2)}) collective-permute-start(f32[16,1024]{1,0:T(8,128)S(1)} %merge.1.a_ref), channel_id=1, source_target_pairs={{0,3},{1,0},{2,1},{3,2},{4,7},{5,4},{6,5},{7,6},{8,11},{9,8},{10,9... | collective-permute-start | bytes 196616 | tf_op jit(solution)/shard_map/ppermute | solution.py:415
  69.1 4.7 %collective-permute-start.1 = (f32[16,1024]{1,0:T(8,128)S(1)}, f32[16,1024]{1,0:T(8,128)S(1)}, u32[]{:S(2)}, u32[]{:S(2)}) collective-permute-start(f32[16,1024]{1,0:T(8,128)S(1)} %merge.1.a_ref), channel_id=1, source_target_pairs={{0,2},{1,3},{2,0},{3,1},{4,6},{5,7},{6,4},{7,5},{8,10},{9,11},{10,... | collective-permute-start | bytes 196616 | tf_op jit(solution)/shard_map/ppermute | solution.py:415
  69.4 6.0 %collective-permute-start = (f32[16,1024]{1,0:T(8,128)S(1)}, f32[16,1024]{1,0:T(8,128)S(1)}, u32[]{:S(2)}, u32[]{:S(2)}) collective-permute-start(f32[16,1024]{1,0:T(8,128)S(1)} %merge.1.a_ref), channel_id=1, source_target_pairs={{0,1},{1,2},{2,3},{3,0},{4,5},{5,6},{6,7},{7,4},{8,9},{9,10},{10,1... | collective-permute-start | bytes 196616 | tf_op jit(solution)/shard_map/ppermute | solution.py:415
  75.5 24.9 %copy-start.3 = (bf16[1024,1024]{1,0:T(8,128)(2,1)S(1)}, bf16[1024,1024]{1,0:T(8,128)(2,1)}, u32[]{:S(2)}) copy-start(bf16[1024,1024]{1,0:T(8,128)(2,1)} %w1_ref.1) | copy-start | bytes 6291460
  75.5 24.9 %copy-start.4 = (bf16[1024,1024]{1,0:T(8,128)(2,1)S(1)}, bf16[1024,1024]{1,0:T(8,128)(2,1)}, u32[]{:S(2)}) copy-start(bf16[1024,1024]{1,0:T(8,128)(2,1)} %w2_ref.1) | copy-start | bytes 6291460
  75.5 24.9 %copy-start.22 = (f32[1024]{0:T(1024)S(1)}, f32[1024]{0:T(1024)}, u32[]{:S(2)}) copy-start(f32[1024]{0:T(1024)} %param.41) | copy-start | bytes 12292
  93.6 3.1 %collective-permute-start.5 = (f32[16,1024]{1,0:T(8,128)S(1)}, f32[16,1024]{1,0:T(8,128)S(1)}, u32[]{:S(2)}, u32[]{:S(2)}) collective-permute-start(f32[16,1024]{1,0:T(8,128)S(1)} %attend.1.a_ref), channel_id=1, source_target_pairs={{0,3},{1,0},{2,1},{3,2},{4,7},{5,4},{6,5},{7,6},{8,11},{9,8},{10,9... | collective-permute-start | bytes 196616 | tf_op jit(solution)/shard_map/ppermute | solution.py:415
  93.9 4.6 %collective-permute-start.4 = (f32[16,1024]{1,0:T(8,128)S(1)}, f32[16,1024]{1,0:T(8,128)S(1)}, u32[]{:S(2)}, u32[]{:S(2)}) collective-permute-start(f32[16,1024]{1,0:T(8,128)S(1)} %attend.1.a_ref), channel_id=1, source_target_pairs={{0,2},{1,3},{2,0},{3,1},{4,6},{5,7},{6,4},{7,5},{8,10},{9,11},{10,... | collective-permute-start | bytes 196616 | tf_op jit(solution)/shard_map/ppermute | solution.py:415
  94.3 6.1 %collective-permute-start.3 = (f32[16,1024]{1,0:T(8,128)S(1)}, f32[16,1024]{1,0:T(8,128)S(1)}, u32[]{:S(2)}, u32[]{:S(2)}) collective-permute-start(f32[16,1024]{1,0:T(8,128)S(1)} %attend.1.a_ref), channel_id=1, source_target_pairs={{0,1},{1,2},{2,3},{3,0},{4,5},{5,6},{6,7},{7,4},{8,9},{9,10},{10,1... | collective-permute-start | bytes 196616 | tf_op jit(solution)/shard_map/ppermute | solution.py:415
  100.4 6.9 %copy-start.23 = (f32[1024]{0:T(1024)S(1)}, f32[1024]{0:T(1024)}, u32[]{:S(2)}) copy-start(f32[1024]{0:T(1024)} %param.44) | copy-start | bytes 12292
  101.3 14.3 %copy-start.1 = (bf16[2048,256]{1,0:T(8,128)(2,1)S(1)}, bf16[2048,256]{1,0:T(8,128)(2,1)}, u32[]{:S(2)}) copy-start(bf16[2048,256]{1,0:T(8,128)(2,1)} %x_ref.5) | copy-start | bytes 3145732
  101.3 14.4 %copy-start.8 = (bf16[256,1024]{1,0:T(8,128)(2,1)S(1)}, bf16[256,1024]{1,0:T(8,128)(2,1)}, u32[]{:S(2)}) copy-start(bf16[256,1024]{1,0:T(8,128)(2,1)} %wq_ref.3) | copy-start | bytes 1572868
  101.3 14.4 %copy-start.9 = (bf16[1024,256]{1,0:T(8,128)(2,1)S(1)}, bf16[1024,256]{1,0:T(8,128)(2,1)}, u32[]{:S(2)}) copy-start(bf16[1024,256]{1,0:T(8,128)(2,1)} %wo_ref.5) | copy-start | bytes 1572868
  101.3 14.4 %copy-start.16 = (f32[3,16,512]{2,1,0:T(8,128)S(1)}, f32[3,16,512]{2,1,0:T(8,128)}, u32[]{:S(2)}) copy-start(f32[3,16,512]{2,1,0:T(8,128)} %bias_ref.5) | copy-start | bytes 294916
  101.3 14.4 %copy-start.18 = (f32[3,256]{1,0:T(4,128)S(1)}, f32[3,256]{1,0:T(4,128)}, u32[]{:S(2)}) copy-start(f32[3,256]{1,0:T(4,128)} %table_ref.5) | copy-start | bytes 9220
  101.3 14.4 %copy-start.24 = (s32[16]{0:T(128)S(1)}, s32[16]{0:T(128)}, u32[]{:S(2)}) copy-start(s32[16]{0:T(128)} %mod_ref.5) | copy-start | bytes 196
  101.3 14.4 %copy-start.26 = (f32[256]{0:T(256)S(1)}, f32[256]{0:T(256)}, u32[]{:S(2)}) copy-start(f32[256]{0:T(256)} %param.46) | copy-start | bytes 3076
  101.3 3.2 %collective-permute-start.8 = (f32[16,1024]{1,0:T(8,128)S(1)}, f32[16,1024]{1,0:T(8,128)S(1)}, u32[]{:S(2)}, u32[]{:S(2)}) collective-permute-start(f32[16,1024]{1,0:T(8,128)S(1)} %get-tuple-element.17.a_ref), channel_id=1, source_target_pairs={{0,3},{1,0},{2,1},{3,2},{4,7},{5,4},{6,5},{7,6},{8,11},{9,8},{10,9... | collective-permute-start | bytes 196616 | tf_op jit(solution)/shard_map/ppermute | solution.py:415
  102.0 4.7 %collective-permute-start.7 = (f32[16,1024]{1,0:T(8,128)S(1)}, f32[16,1024]{1,0:T(8,128)S(1)}, u32[]{:S(2)}, u32[]{:S(2)}) collective-permute-start(f32[16,1024]{1,0:T(8,128)S(1)} %get-tuple-element.17.a_ref), channel_id=1, source_target_pairs={{0,2},{1,3},{2,0},{3,1},{4,6},{5,7},{6,4},{7,5},{8,10},{9,11},{10,... | collective-permute-start | bytes 196616 | tf_op jit(solution)/shard_map/ppermute | solution.py:415
  102.5 4.8 %collective-permute-start.6 = (f32[16,1024]{1,0:T(8,128)S(1)}, f32[16,1024]{1,0:T(8,128)S(1)}, u32[]{:S(2)}, u32[]{:S(2)}) collective-permute-start(f32[16,1024]{1,0:T(8,128)S(1)} %get-tuple-element.17.a_ref), channel_id=1, source_target_pairs={{0,1},{1,2},{2,3},{3,0},{4,5},{5,6},{6,7},{7,4},{8,9},{9,10},{10,1... | collective-permute-start | bytes 196616 | tf_op jit(solution)/shard_map/ppermute | solution.py:415
  108.7 24.2 %all-to-all-start.2 = ((bf16[32,16,1024]{2,1,0:T(8,128)(2,1)}), bf16[32,16,1024]{2,1,0:T(8,128)(2,1)S(1)}, u32[]{:S(2)}, u32[]{:S(2)}) async-start(bf16[32,16,1024]{2,1,0:T(8,128)(2,1)} %broadcast_in_dim.5), calls=%async_computation.2 | async-start | bytes 2097152 | tf_op jit(solution)/shard_map/all_to_all | solution.py:409
  120.7 2.0 %copy-start = (bf16[1024,2048]{1,0:T(8,128)(2,1)}, bf16[1024,2048]{1,0:T(8,128)(2,1)S(1)}, u32[]{:S(2)}) copy-start(bf16[1024,2048]{1,0:T(8,128)(2,1)S(1)} %get-tuple-element.20.qt_ref) | copy-start | bytes 12582916
  122.7 1.4 copy-start.5
  124.1 0.8 copy-start.12
  124.9 0.8 copy-start.13
  132.9 1.0 copy-start.28
where the time goes:
time: 177 us
  Pallas kernels  90.4 us (51%)
  waiting for transfers between devices  31.5 us (18%)
  starting transfers between devices  23.3 us (13%)
  blocking collectives  16.1 us (9%)
  local copies, waits for them, and re-layouts  15.1 us (9%)
    pallas_call x1, Pallas kernels, decode(): pl.pallas_call(functools.partial(decode_kernel, heads), grid_spec=pltpu.P...  42.8 us
    pallas_call x1, Pallas kernels, encode(): pl.pallas_call(functools.partial(encode_kernel, heads), grid_spec=pltpu.P...  38.9 us
    all_to_all x1, blocking collectives, share(): return lax.all_to_all(copies, 'inp', 0, 0)  16.1 us
    ppermute x9, waiting for transfers between devices, head_parts(): lax.ppermute(part, 'head', [(i, (i + k) % size) for i in range(size)])  14.2 us
    unnamed x58, local copies, waits for them, and re-layouts  13.1 us
    all_to_all x1, waiting for transfers between devices, body(): parts = lax.all_to_all(own.reshape(-1, lat_rows, own.shape[1]), 'inp', 0, 0)  10.1 us
    all_to_all x1, starting transfers between devices, body(): parts = lax.all_to_all(own.reshape(-1, lat_rows, own.shape[1]), 'inp', 0, 0)  9.6 us
    all_to_all x1, waiting for transfers between devices, share(): return lax.all_to_all(copies, 'inp', 0, 0)  7.14 us
  transfers between devices with their start and end apart: 11, of which 10 were waited for; matrix products, arithmetic and copies ran while one was open for 0% of the time, Pallas kernels for 3%

commit v1 on v0

--- a/solution.py
+++ b/solution.py
@@ -19,6 +19,7 @@
 F32 = jnp.float32
 MIB = 2**20
 EXTRA = 128
+SMALL_TOTAL = 2.0**-95
 
 
 def dot(a, b):
@@ -55,21 +56,26 @@
 def modality_hot(mod, shape, dim):
     index = lax.broadcasted_iota(jnp.int32, shape, dim)
     hit = (index == mod) | (index == mod + MODS) | (index == mod + 2 * MODS)
-    return jnp.where(hit, 1.0, 0.0).astype(BF)
-
-
-def embed_norm(mod_ref, first, x_ref, table_ref, gain, n_ref):
-    for b in range(x_ref.shape[0] // MBLK):
-        rows = slice(b * MBLK, (b + 1) * MBLK)
-        mod = mod_ref[first + b]
-        embedded = x_ref[rows, :].astype(F32) + table_ref[pl.ds(mod, 1), :]
-        n_ref[rows, :] = layer_norm(embedded, gain).astype(BF)
+    return hit, index
+
+
+def head_sums(count, lanes):
+    row = lax.broadcasted_iota(jnp.int32, (count * HSZ, lanes), 0) // HSZ
+    lane = lax.broadcasted_iota(jnp.int32, (count * HSZ, lanes), 1) // (lanes // count)
+    return jnp.where(row == lane, 1.0, 0.0).astype(BF)
+
+
+def embed_norm(mod_ref, first, b, x_ref, table_ref, gain):
+    embedded = x_ref[b * MBLK : (b + 1) * MBLK, :].astype(F32)
+    embedded = embedded + table_ref[pl.ds(mod_ref[first + b], 1), :]
+    return layer_norm(embedded, gain).astype(BF)
 
 
 def encode_kernel(
     heads,
     mod_ref,
     x_ref,
+    next_ref,
     table_ref,
     gain_ref,
     lat_ref,
@@ -79,15 +85,49 @@
     bias_ref,
     out_ref,
     qx_ref,
+    norm_ref,
     wvt_ref,
     n_ref,
     hot_ref,
+    k_ref,
+    vt_ref,
+    p_ref,
+    part_ref,
+    shift_ref,
     m_ref,
     acc_ref,
 ):
     step = pl.program_id(0)
-    blocks = x_ref.shape[0] // MBLK
+    last = pl.num_programs(0) - 1
+    points = x_ref.shape[0]
+    blocks = points // MBLK
     lat_count = lat_ref.shape[0]
+    slot = lax.rem(step, 2)
+    row16 = lax.broadcasted_iota(jnp.int32, (16, lat_count), 0)
+    gain = gain_ref[...]
+
+    def project(at, into):
+        normed = n_ref[...]
+        keys = dot(normed, wkv_ref[0])
+        k_ref[into] = keys.astype(BF)
+        vt_ref[into] = dot_nt(wvt_ref[...], normed).astype(BF)
+        lengths = dot((keys * keys).astype(BF), head_sums(heads, 128))
+        longest = jnp.sqrt(jnp.max(lengths, axis=0, keepdims=True))
+        present = [jnp.bool_(False)] * MODS
+        for b in range(blocks):
+            mod = mod_ref[at * blocks + b]
+            hit, index = modality_hot(mod, (MBLK, 128), 1)
+            hit = jnp.where(hit | (index == 16), 1.0, 0.0)
+            hot_ref[into, b * MBLK : (b + 1) * MBLK, :] = hit.astype(BF)
+            present = [p | (mod == m) for m, p in enumerate(present)]
+        for h in range(heads):
+            bound = jnp.full((1, lat_count), NEG_FLOOR, F32)
+            for m in range(MODS):
+                held = jnp.where(present[m], bias_ref[m, h : h + 1, :] * LOG2E, NEG_FLOOR)
+                bound = jnp.maximum(bound, held)
+            lane = h * (128 // heads)
+            bound = bound + norm_ref[h : h + 1, :] * longest[:, lane : lane + 1]
+            shift_ref[into, h] = bound.astype(BF).astype(F32)
 
     @pl.when(step == 0)
     def _():
@@ -96,33 +136,66 @@
         qx_ref[...] = jnp.zeros(qx_ref.shape, BF)
         for h in range(heads):
             half = (h % 2) * HSZ
-            qx_ref[h, half : half + HSZ, :] = query[h * HSZ : (h + 1) * HSZ, :].astype(BF)
+            own = query[h * HSZ : (h + 1) * HSZ, :]
+            qx_ref[h, half : half + HSZ, :] = own.astype(BF)
             qx_ref[h, 128:144, :] = bias_rows(bias_ref[:, h, :] * LOG2E, 16).astype(BF)
+            norm_ref[h : h + 1, :] = jnp.sqrt(jnp.sum(own * own, axis=0, keepdims=True))
         wvt_ref[...] = wkv_ref[1].T
         m_ref[...] = jnp.full(m_ref.shape, NEG_FLOOR, F32)
         acc_ref[...] = jnp.zeros(acc_ref.shape, F32)
-
-    embed_norm(mod_ref, step * blocks, x_ref, table_ref, gain_ref[...], n_ref)
-    for b in range(blocks):
-        mod = mod_ref[step * blocks + b]
-        hot_ref[b * MBLK : (b + 1) * MBLK, :] = modality_hot(mod, (MBLK, 128), 1)
-    normed = n_ref[...]
-    hot = hot_ref[...]
-    keys = dot(normed, wkv_ref[0]).astype(BF)
-    values_t = dot_nt(wvt_ref[...], normed).astype(BF)
-    ones = jnp.ones((HSZ, x_ref.shape[0]), BF)
+        for b in range(blocks):
+            n_ref[b * MBLK : (b + 1) * MBLK, :] = embed_norm(
+                mod_ref, 0, b, x_ref, table_ref, gain
+            )
+        project(0, 0)
+
+    following = jnp.minimum(step + 1, last)
+    hot = hot_ref[slot]
+    ones = jnp.ones((HSZ, points), BF)
     for h in range(heads):
-        pair = (h // 2) * 128
-        left = jnp.concatenate([keys[:, pair : pair + 128], hot], axis=1)
-        scores = dot(left, qx_ref[h])
+        qx_ref[h, 144:160, :] = jnp.where(row16 == 0, -shift_ref[slot, h], 0.0).astype(BF)
+    per_head = -(-blocks // heads)
+    for h in range(heads + 1):
+        if h < heads:
+            pair = (h // 2) * 128
+            left = jnp.concatenate([k_ref[slot, :, pair : pair + 128], hot], axis=1)
+            p_ref[h % 2] = jnp.exp2(dot(left, qx_ref[h])).astype(BF)
+        if h > 0:
+            values_h = vt_ref[slot, (h - 1) * HSZ : h * HSZ, :]
+            values_h = jnp.concatenate([values_h, ones], axis=0)
+            part_ref[h - 1] = dot(values_h, p_ref[(h - 1) % 2])
+        for b in range(h * per_head, min((h + 1) * per_head, blocks)):
+            n_ref[b * MBLK : (b + 1) * MBLK, :] = embed_norm(
+                mod_ref, following * blocks, b, next_ref, table_ref, gain
+            )
+    project(following, 1 - slot)
+    least = jnp.min(part_ref[:, HSZ : HSZ + 1, :])
+
+    @pl.when(least < SMALL_TOTAL)
+    def _():
+        def exact(h, _):
+            pair = pl.multiple_of((h // 2) * 128, 128)
+            qx_ref[h, 144:160, :] = jnp.zeros((16, lat_count), BF)
+            left = jnp.concatenate([k_ref[slot, :, pl.ds(pair, 128)], hot_ref[slot]], axis=1)
+            scores = dot(left, qx_ref[h])
+            top = jnp.max(scores, axis=0, keepdims=True)
+            weights = jnp.exp2(scores - top).astype(BF)
+            values_h = vt_ref[slot, pl.ds(pl.multiple_of(h * HSZ, HSZ), HSZ), :]
+            values_h = jnp.concatenate([values_h, jnp.ones((HSZ, points), BF)], axis=0)
+            part_ref[h] = dot(values_h, weights)
+            shift_ref[slot, h] = top
+            return 0
+
+        lax.fori_loop(0, heads, exact, 0)
+
+    for h in range(heads):
         old = m_ref[h]
-        new = jnp.maximum(old, jnp.max(scores, axis=0, keepdims=True))
+        own = shift_ref[slot, h]
+        new = jnp.maximum(old, own)
         m_ref[h] = new
-        weights = jnp.exp2(scores - new).astype(BF)
-        values_h = jnp.concatenate([values_t[h * HSZ : (h + 1) * HSZ, :], ones], axis=0)
-        acc_ref[h] = acc_ref[h] * jnp.exp2(old - new) + dot(values_h, weights)
-
-    @pl.when(step == pl.num_programs(0) - 1)
+        acc_ref[h] = acc_ref[h] * jnp.exp2(old - new) + part_ref[h] * jnp.exp2(own - new)
+
+    @pl.when(step == last)
     def _():
         index = lax.broadcasted_iota(jnp.int32, (EXTRA, lat_count), 0)
         extra = jnp.zeros((EXTRA, lat_count), F32)
@@ -142,14 +215,16 @@
     lat_count, lat_width = latents.shape
     cols = heads * HSZ
     tile = math.gcd(points, 1024)
+    steps = points // tile
     whole = lambda *shape: pl.BlockSpec(shape, lambda i, mod: (0,) * len(shape))
     return pl.pallas_call(
         functools.partial(encode_kernel, heads),
         grid_spec=pltpu.PrefetchScalarGridSpec(
             num_scalar_prefetch=1,
-            grid=(points // tile,),
+            grid=(steps,),
             in_specs=[
-                pl.BlockSpec((tile, width), lambda i, mod: (i, 0)),
+                pl.BlockSpec((tile, width), lambda i, mod: (0, 0)),
+                pl.BlockSpec((tile, width), lambda i, mod: (jnp.minimum(i + 1, steps - 1), 0)),
                 whole(MODS, width),
                 whole(1, width),
                 whole(lat_count, lat_width),
@@ -161,17 +236,23 @@
             out_specs=whole(lat_count, cols + EXTRA),
             scratch_shapes=[
                 pltpu.VMEM((heads, 256, lat_count), BF),
+                pltpu.VMEM((heads, lat_count), F32),
                 pltpu.VMEM((cols, width), BF),
                 pltpu.VMEM((tile, width), BF),
-                pltpu.VMEM((tile, 128), BF),
+                pltpu.VMEM((2, tile, 128), BF),
+                pltpu.VMEM((2, tile, cols), BF),
+                pltpu.VMEM((2, cols, tile), BF),
+                pltpu.VMEM((2, tile, lat_count), BF),
+                pltpu.VMEM((heads, 128, lat_count), F32),
+                pltpu.VMEM((2, heads, 1, lat_count), F32),
                 pltpu.VMEM((heads, 1, lat_count), F32),
                 pltpu.VMEM((heads, 128, lat_count), F32),
             ],
         ),
         out_shape=jax.ShapeDtypeStruct((lat_count, cols + EXTRA), BF),
-        compiler_params=pltpu.CompilerParams(vmem_limit_bytes=48 * MIB),
+        compiler_params=pltpu.CompilerParams(vmem_limit_bytes=58 * MIB),
         name="encode",
-    )(input_modality, inputs, table, gain, latents, lat_gain, wq, wkv, bias)
+    )(input_modality, inputs, inputs, table, gain, latents, lat_gain, wq, wkv, bias)
 
 
 def small_call(kernel, name, outs, *args):
@@ -254,26 +335,43 @@
     wo_ref,
     qt_ref,
     hot_ref,
+    norm_ref,
+    top_ref,
     bias_out,
     wot_ref,
     wqt_ref,
+    bmax_ref,
     n_ref,
 ):
     step = pl.program_id(0)
     blocks = x_ref.shape[0] // MBLK
+    lat_count = bias_ref.shape[2]
 
     @pl.when(step == 0)
     def _():
         wqt_ref[...] = wq_ref[...].T
         wot_ref[...] = wo_ref[...].T
+        lane = lax.broadcasted_iota(jnp.int32, (lat_count, 128), 1)
         for h in range(heads):
-            bias_out[h] = bias_rows(bias_ref[:, h, :] * LOG2E, 128).T.astype(BF)
-
-    embed_norm(mod_ref, step * blocks, x_ref, table_ref, gain_ref[...], n_ref)
+            columns = bias_rows(bias_ref[:, h, :] * LOG2E, 128).T
+            bias_out[h] = jnp.where(lane == 16 + h, 1.0, columns).astype(BF)
+        for m in range(MODS):
+            top = jnp.max(bias_ref[m] * LOG2E, axis=1, keepdims=True)
+            bmax_ref[m] = jnp.broadcast_to(top, (heads, MBLK))
+
     for b in range(blocks):
+        n_ref[b * MBLK : (b + 1) * MBLK, :] = embed_norm(
+            mod_ref, step * blocks, b, x_ref, table_ref, gain_ref[...]
+        )
         mod = mod_ref[step * blocks + b]
-        hot_ref[:, b * MBLK : (b + 1) * MBLK] = modality_hot(mod, (128, MBLK), 0)
-    qt_ref[...] = (dot_nt(wqt_ref[...], n_ref[...]) * SCALE2).astype(BF)
+        hit, _ = modality_hot(mod, (16, MBLK), 0)
+        hot_ref[:, b * MBLK : (b + 1) * MBLK] = jnp.where(hit, 1.0, 0.0).astype(BF)
+        top_ref[:, b * MBLK : (b + 1) * MBLK] = bmax_ref[mod]
+    query = dot_nt(wqt_ref[...], n_ref[...]) * SCALE2
+    qt_ref[...] = query.astype(BF)
+    for h in range(heads):
+        own = query[h * HSZ : (h + 1) * HSZ, :]
+        norm_ref[h : h + 1, :] = jnp.sqrt(jnp.sum(own * own, axis=0, keepdims=True))
 
 
 def prepare_queries(queries, query_modality, table, gain, wq, bias, wo):
@@ -282,6 +380,7 @@
     cols = heads * HSZ
     tile = math.gcd(count, 512)
     whole = lambda *shape: pl.BlockSpec(shape, lambda i, mod: (0,) * len(shape))
+    tiled = lambda rows: pl.BlockSpec((rows, tile), lambda i, mod: (0, i))
     return pl.pallas_call(
         functools.partial(query_kernel, heads),
         grid_spec=pltpu.PrefetchScalarGridSpec(
@@ -296,23 +395,28 @@
                 whole(cols, width),
             ],
             out_specs=[
-                pl.BlockSpec((cols, tile), lambda i, mod: (0, i)),
-                pl.BlockSpec((128, tile), lambda i, mod: (0, i)),
+                tiled(cols),
+                tiled(16),
+                tiled(heads),
+                tiled(heads),
                 whole(heads, lat_count, 128),
                 whole(width, cols),
             ],
             scratch_shapes=[
                 pltpu.VMEM((cols, width), BF),
+                pltpu.VMEM((MODS, heads, MBLK), F32),
                 pltpu.VMEM((tile, width), BF),
             ],
         ),
         out_shape=[
             jax.ShapeDtypeStruct((cols, count), BF),
-            jax.ShapeDtypeStruct((128, count), BF),
+            jax.ShapeDtypeStruct((16, count), BF),
+            jax.ShapeDtypeStruct((heads, count), F32),
+            jax.ShapeDtypeStruct((heads, count), F32),
             jax.ShapeDtypeStruct((heads, lat_count, 128), BF),
             jax.ShapeDtypeStruct((width, cols), BF),
         ],
-        compiler_params=pltpu.CompilerParams(vmem_limit_bytes=32 * MIB),
+        compiler_params=pltpu.CompilerParams(vmem_limit_bytes=28 * MIB),
         name="queries",
     )(query_modality, queries, table, gain, wq, bias, wo)
 
@@ -326,15 +430,21 @@
     wkv_ref,
     bias_ref,
     qt_ref,
-    hot_ref,
+    onehot_ref,
+    norm_ref,
+    top_ref,
     wot_ref,
     out_ref,
     kx_ref,
     vx_ref,
+    long_ref,
+    hot_ref,
+    p_ref,
     mix_ref,
 ):
     step = pl.program_id(0)
-    blocks = x_ref.shape[0] // MBLK
+    tile = x_ref.shape[0]
+    blocks = tile // MBLK
     lat_count = lat_ref.shape[0]
 
     @pl.when(step == 0)
@@ -342,25 +452,55 @@
         normed = lat_ref[...]
         ones = jnp.ones((HSZ, lat_count), BF)
         lane = lax.broadcasted_iota(jnp.int32, (lat_count, 128), 1) // HSZ
+        sums = head_sums(2, 128)
         for pair in range(heads // 2):
             cols = slice(pair * 128, (pair + 1) * 128)
             keys = dot(normed, wkv_ref[0, :, cols])
-            values = dot(normed, wkv_ref[1, :, cols]).T.astype(BF)
+            values = dot(normed, wkv_ref[1, :, cols]).astype(BF).T
+            lengths = dot((keys * keys).astype(BF), sums)
+            longest = jnp.sqrt(jnp.max(lengths, axis=0, keepdims=True))
             for half in range(2):
                 h = 2 * pair + half
                 kx_ref[h, :, :128] = jnp.where(lane == half, keys, 0.0).astype(BF)
                 kx_ref[h, :, 128:] = bias_ref[h]
                 vx_ref[h, :HSZ, :] = values[half * HSZ : (half + 1) * HSZ, :]
                 vx_ref[h, HSZ:, :] = ones
-
+                long_ref[h : h + 1, :] = jnp.broadcast_to(
+                    longest[:, half * HSZ : half * HSZ + 1], (1, 128)
+                )
+        hot_ref[...] = jnp.zeros(hot_ref.shape, BF)
+
+    bound = norm_ref[...] * long_ref[:, :1] + top_ref[...]
+    hot_ref[:16, :] = onehot_ref[...]
+    hot_ref[16 : 16 + heads, :] = (-bound).astype(BF)
     hot = hot_ref[...]
-    for h in range(heads):
-        pair = (h // 2) * 128
-        right = jnp.concatenate([qt_ref[pair : pair + 128, :], hot], axis=0)
-        scores = dot(kx_ref[h], right)
-        weights = jnp.exp2(scores - jnp.max(scores, axis=0, keepdims=True)).astype(BF)
-        mixed = dot(vx_ref[h], weights)
-        mix_ref[h * HSZ : (h + 1) * HSZ, :] = (mixed[:HSZ, :] / mixed[HSZ:, :]).astype(BF)
+    least = jnp.full((1, tile), 1.0, F32)
+    for h in range(heads + 1):
+        if h < heads:
+            pair = (h // 2) * 128
+            right = jnp.concatenate([qt_ref[pair : pair + 128, :], hot], axis=0)
+            p_ref[h % 2] = jnp.exp2(dot(kx_ref[h], right)).astype(BF)
+        if h > 0:
+            mixed = dot(vx_ref[h - 1], p_ref[(h - 1) % 2])
+            least = jnp.minimum(least, mixed[HSZ : HSZ + 1, :])
+            mix_ref[(h - 1) * HSZ : h * HSZ, :] = (mixed[:HSZ, :] / mixed[HSZ:, :]).astype(BF)
+
+    @pl.when(jnp.min(least) < SMALL_TOTAL)
+    def _():
+        hot_ref[16 : 16 + heads, :] = jnp.zeros((heads, tile), BF)
+
+        def exact(h, _):
+            pair = pl.multiple_of((h // 2) * 128, 128)
+            right = jnp.concatenate([qt_ref[pl.ds(pair, 128), :], hot_ref[...]], axis=0)
+            scores = dot(kx_ref[h], right)
+            top = jnp.max(scores, axis=0, keepdims=True)
+            mixed = dot(vx_ref[h], jnp.exp2(scores - top).astype(BF))
+            mixed = (mixed[:HSZ, :] / mixed[HSZ:, :]).astype(BF)
+            mix_ref[pl.ds(pl.multiple_of(h * HSZ, HSZ), HSZ), :] = mixed
+            return 0
+
+        lax.fori_loop(0, heads, exact, 0)
+
     decoded = dot(wot_ref[...], mix_ref[...]).T
     for b in range(blocks):
         rows = slice(b * MBLK, (b + 1) * MBLK)
@@ -370,12 +510,13 @@
 
 
 def decode(queries, query_modality, table, normed, wkv, prepared):
-    queries_t, hot, bias, wo_t = prepared
+    queries_t, hot, norms, tops, bias, wo_t = prepared
     count, width = queries.shape
     heads, lat_count = bias.shape[:2]
     cols = heads * HSZ
     tile = math.gcd(count, 512)
-    whole = lambda *shape: pl.BlockSpec(shape, lambda i, mod: (0,) * len(shape))
+    held = pl.BlockSpec(memory_space=pltpu.VMEM)
+    tiled = lambda rows: pl.BlockSpec((rows, tile), lambda i, mod: (0, i))
     return pl.pallas_call(
         functools.partial(decode_kernel, heads),
         grid_spec=pltpu.PrefetchScalarGridSpec(
@@ -383,25 +524,30 @@
             grid=(count // tile,),
             in_specs=[
                 pl.BlockSpec((tile, width), lambda i, mod: (i, 0)),
-                whole(MODS, width),
-                whole(lat_count, normed.shape[1]),
-                whole(*wkv.shape),
-                whole(heads, lat_count, 128),
-                pl.BlockSpec((cols, tile), lambda i, mod: (0, i)),
-                pl.BlockSpec((128, tile), lambda i, mod: (0, i)),
-                whole(width, cols),
+                held,
+                held,
+                held,
+                held,
+                tiled(cols),
+                tiled(16),
+                tiled(heads),
+                tiled(heads),
+                held,
             ],
             out_specs=pl.BlockSpec((tile, width), lambda i, mod: (i, 0)),
             scratch_shapes=[
                 pltpu.VMEM((heads, lat_count, 256), BF),
                 pltpu.VMEM((heads, 128, lat_count), BF),
+                pltpu.VMEM((heads, 128), F32),
+                pltpu.VMEM((128, tile), BF),
+                pltpu.VMEM((2, lat_count, tile), BF),
                 pltpu.VMEM((cols, tile), BF),
             ],
         ),
         out_shape=jax.ShapeDtypeStruct((count, width), F32),
-        compiler_params=pltpu.CompilerParams(vmem_limit_bytes=56 * MIB),
+        compiler_params=pltpu.CompilerParams(vmem_limit_bytes=32 * MIB),
         name="decode",
-    )(query_modality, queries, table, normed, wkv, bias, queries_t, hot, wo_t)
+    )(query_modality, queries, table, normed, wkv, bias, queries_t, hot, norms, tops, wo_t)
 
 
 def share(rows):

time: 177 us -> 180 us (1.017)
  Pallas kernels: 90.4 us -> 93.9 us
    pallas_call x1, Pallas kernels: 38.9 us -> 60.7 us  [encode(): pl.pallas_call(functools.partial(encode_kernel, heads), grid_spec=pltpu.P...]
    pallas_call x1, Pallas kernels: 42.8 us -> 24.2 us  [decode(): pl.pallas_call(functools.partial(decode_kernel, heads), grid_spec=pltpu.P...]
    unnamed x58 -> x50, local copies, waits for them, and re-layouts: 13.1 us -> 12.6 us
where the time goes in v1:
time: 180 us
  Pallas kernels  93.9 us (52%)
  waiting for transfers between devices  31.6 us (18%)
  starting transfers between devices  23.1 us (13%)
  blocking collectives  16.1 us (9%)
  local copies, waits for them, and re-layouts  14.7 us (8%)
    pallas_call x1, Pallas kernels, encode(): pl.pallas_call(functools.partial(encode_kernel, heads), grid_spec=pltpu.P...  60.7 us
    pallas_call x1, Pallas kernels, decode(): pl.pallas_call(functools.partial(decode_kernel, heads), grid_spec=pltpu.P...  24.2 us
    all_to_all x1, blocking collectives, share(): return lax.all_to_all(copies, 'inp', 0, 0)  16.1 us
    ppermute x9, waiting for transfers between devices, head_parts(): lax.ppermute(part, 'head', [(i, (i + k) % size) for i in range(size)])  14.2 us
    unnamed x50, local copies, waits for them, and re-layouts  12.6 us
    all_to_all x1, waiting for transfers between devices, body(): parts = lax.all_to_all(own.reshape(-1, lat_rows, own.shape[1]), 'inp', 0, 0)  10.1 us
    all_to_all x1, starting transfers between devices, body(): parts = lax.all_to_all(own.reshape(-1, lat_rows, own.shape[1]), 'inp', 0, 0)  9.56 us
    all_to_all x1, waiting for transfers between devices, share(): return lax.all_to_all(copies, 'inp', 0, 0)  7.25 us
  transfers between devices with their start and end apart: 11, of which 10 were waited for; matrix products, arithmetic and copies ran while one was open for 0% of the time, Pallas kernels for 3%

profile of v1, /device:TPU:1, one launch (start us, length us, event | category | flops | bytes accessed | tf_op | source)
XLA Modules:
  0.0 179.7 jit_solution(3066827978295955851)
XLA Ops:
  0.0 60.7 %encode.1 = bf16[512,384]{1,0:T(8,128)(2,1)} custom-call(s32[64]{0:T(128)} %mod_ref.3, bf16[8192,256]{1,0:T(8,128)(2,1)} %next_ref.1, bf16[8192,256]{1,0:T(8,128)(2,1)} %next_ref.1, f32[3,256]{1,0:T(4,128)} %table_ref.5, f32[1,256]{1,0:T(1,128)} %bitcast.17, f32[512,1024]{1,0:T(8,128)} %lat_ref.1, f32[1,1024]{1,0:T(1,128)} %bitcast.16, ...), custom_call_target="tpu_custom_call" | custom-call | tf_op jit(solution)/shard_map/encode/pallas_call | solution.py:220
  60.7 9.6 %all-to-all-start = ((bf16[32,16,384]{2,1,0:T(8,128)(2,1)}), bf16[32,16,384]{2,1,0:T(8,128)(2,1)S(1)}, u32[]{:S(2)}, u32[]{:S(2)}) async-start(bf16[32,16,384]{2,1,0:T(8,128)(2,1)} %bitcast.15), calls=%async_computation | async-start | bytes 786432 | tf_op jit(solution)/shard_map/all_to_all | solution.py:613
  70.3 0.0 copy-start.13
  70.3 0.0 copy-start.15
  70.3 10.1 %all-to-all-done.part_ref = bf16[32,16,384]{2,1,0:T(8,128)(2,1)S(1)} async-done(((bf16[32,16,384]{2,1,0:T(8,128)(2,1)}), bf16[32,16,384]{2,1,0:T(8,128)(2,1)S(1)}, u32[]{:S(2)}, u32[]{:S(2)}) %all-to-all-start) | async-done | bytes 393248 | tf_op jit(solution)/shard_map/all_to_all | solution.py:613
  80.4 0.0 copy-done.14
  80.4 0.7 merge.1.a_ref
  81.1 2.8 %collective-permute-start.2 = (f32[16,1024]{1,0:T(8,128)S(1)}, f32[16,1024]{1,0:T(8,128)S(1)}, u32[]{:S(2)}, u32[]{:S(2)}) collective-permute-start(f32[16,1024]{1,0:T(8,128)S(1)} %merge.1.a_ref), channel_id=1, source_target_pairs={{0,3},{1,0},{2,1},{3,2},{4,7},{5,4},{6,5},{7,6},{8,11},{9,8},{10,9... | collective-permute-start | bytes 196616 | tf_op jit(solution)/shard_map/ppermute | solution.py:561
  83.9 0.3 collective-permute-start.1
  84.2 0.7 collective-permute-start
  84.9 0.8 constant_dynamic-slice_fusion.lat_ref
  85.8 0.0 collective-permute-done.2.d_ref
  85.8 2.8 %collective-permute-done.1.c_ref = f32[16,1024]{1,0:T(8,128)S(1)} collective-permute-done((f32[16,1024]{1,0:T(8,128)S(1)}, f32[16,1024]{1,0:T(8,128)S(1)}, u32[]{:S(2)}, u32[]{:S(2)}) %collective-permute-start.1) | collective-permute-done | bytes 65568 | tf_op jit(solution)/shard_map/ppermute | solution.py:561
  88.6 1.7 collective-permute-done.b_ref
  90.3 0.0 copy-done.20
  90.3 0.0 copy-done.8
  90.3 0.0 copy-start.21
  90.3 0.5 project.1
  90.8 0.1 broadcast_in_dim.4
  90.9 16.1 %all_to_all.15 = bf16[32,16,512]{2,1,0:T(8,128)(2,1)S(1)} all-to-all(bf16[32,16,512]{2,1,0:T(8,128)(2,1)S(1)} %broadcast_in_dim.4), channel_id=1, replica_groups=mesh['inp'=32,'head'=4] {'inp'}, dimensions={0} | all-to-all | bytes 1048576 | tf_op jit(solution)/shard_map/all_to_all | solution.py:555
  107.0 0.0 copy-done.13
  107.0 0.0 copy-done.15
  107.0 1.5 attend.1.a_ref
  108.4 0.3 collective-permute-start.5
  108.7 0.3 collective-permute-start.4
  109.1 0.8 collective-permute-start.3
  109.9 1.6 collective-permute-done.5.d_ref
  111.6 1.8 collective-permute-done.4.c_ref
  113.4 1.8 %collective-permute-done.3.b_ref = f32[16,1024]{1,0:T(8,128)S(1)} collective-permute-done((f32[16,1024]{1,0:T(8,128)S(1)}, f32[16,1024]{1,0:T(8,128)S(1)}, u32[]{:S(2)}, u32[]{:S(2)}) %collective-permute-start.3) | collective-permute-done | bytes 65568 | tf_op jit(solution)/shard_map/ppermute | solution.py:561
  115.2 0.0 copy-done.6
  115.2 0.0 copy-done.7
  115.2 0.0 copy-done.21
  115.2 0.0 copy-start.22
  115.2 0.8 mlp.1
  116.1 0.0 copy-start.16
  116.1 0.0 copy-start.19
  116.1 0.0 copy-start.23
  116.1 0.0 copy-start.24
  116.1 0.7 collective-permute-start.8
  116.8 0.5 collective-permute-start.7
  117.3 0.3 collective-permute-start.6
  117.7 1.6 collective-permute-done.8.d_ref
  119.3 2.2 %collective-permute-done.7.c_ref = f32[16,1024]{1,0:T(8,128)S(1)} collective-permute-done((f32[16,1024]{1,0:T(8,128)S(1)}, f32[16,1024]{1,0:T(8,128)S(1)}, u32[]{:S(2)}, u32[]{:S(2)}) %collective-permute-start.7) | collective-permute-done | bytes 65568 | tf_op jit(solution)/shard_map/ppermute | solution.py:561
  121.5 0.7 collective-permute-done.6.b_ref
  122.2 0.0 copy-done.22
  122.2 0.2 last.1
  122.4 1.1 broadcast_in_dim.5
  123.5 6.8 %all-to-all-start.2 = ((bf16[32,16,1024]{2,1,0:T(8,128)(2,1)}), bf16[32,16,1024]{2,1,0:T(8,128)(2,1)S(1)}, u32[]{:S(2)}, u32[]{:S(2)}) async-start(bf16[32,16,1024]{2,1,0:T(8,128)(2,1)} %broadcast_in_dim.5), calls=%async_computation.2 | async-start | bytes 2097152 | tf_op jit(solution)/shard_map/all_to_all | solution.py:555
  130.3 0.0 copy-done.3
  130.3 0.0 copy-done.9
  130.3 0.0 copy-done.10
  130.3 0.0 copy-done.16
  130.4 5.2 %queries.1 = (bf16[1024,2048]{1,0:T(8,128)(2,1)S(1)}, bf16[16,2048]{1,0:T(8,128)(2,1)S(1)}, f32[16,2048]{1,0:T(8,128)S(1)}, f32[16,2048]{1,0:T(8,128)S(1)}, bf16...) custom-call(s32[16]{0:T(128)S(1)} %copy-done.23, bf16[2048,256]{1,0:T(8,128)(2,1)S(1)} %copy-done.3, ...), custom_call_target="tpu_custom_call" | custom-call | tf_op jit(solution)/shard_map/queries/pallas_call | solution.py:384
  135.6 2.0 %copy-done.1 = bf16[1024,2048]{1,0:T(8,128)(2,1)} copy-done((bf16[1024,2048]{1,0:T(8,128)(2,1)}, bf16[1024,2048]{1,0:T(8,128)(2,1)S(1)}, u32[]{:S(2)}) %copy-start.1) | copy-done | bytes 4194328
  137.6 1.3 copy-done.4
  138.9 0.8 copy-done.11
  139.7 0.6 copy-done.17
  140.3 7.2 %all-to-all-done.2 = bf16[32,16,1024]{2,1,0:T(8,128)(2,1)S(1)} async-done(((bf16[32,16,1024]{2,1,0:T(8,128)(2,1)}), bf16[32,16,1024]{2,1,0:T(8,128)(2,1)S(1)}, u32[]{:S(2)}, u32[]{:S(2)}) %all-to-all-start.2) | async-done | bytes 1048608 | tf_op jit(solution)/shard_map/all_to_all | solution.py:555
  147.6 2.2 %copy-done = bf16[2,1024,1024]{2,1,0:T(8,128)(2,1)S(1)} copy-done((bf16[2,1024,1024]{2,1,0:T(8,128)(2,1)S(1)}, bf16[2,1024,1024]{2,1,0:T(8,128)(2,1)}, u32[]{:S(2)}) %copy-start) | copy-done | bytes 4194328
  149.8 2.2 %copy-done.2 = bf16[1024,2048]{1,0:T(8,128)(2,1)S(1)} copy-done((bf16[1024,2048]{1,0:T(8,128)(2,1)S(1)}, bf16[1024,2048]{1,0:T(8,128)(2,1)}, u32[]{:S(2)}) %copy-start.2) | copy-done | bytes 4194328
  151.9 1.6 copy-done.5
  153.5 1.0 copy-done.12
  154.6 0.8 copy-done.18
  155.4 24.2 %decode.1 = f32[2048,256]{1,0:T(8,128)} custom-call(s32[16]{0:T(128)S(1)} %copy-done.23, bf16[2048,256]{1,0:T(8,128)(2,1)S(1)} %copy-done.3, f32[3,256]{1,0:T(4,128)S(1)} %copy-done.19, bf16[512,1024]{1,0:T(8,128)(2,1)S(1)} %bitcast.9, bf16[2,1024,1024]{2,1,0:T(8,128)(2,1)S(1)} %copy-done, bf16[16,512,128]{2,1,0:T(8,128)(2,1)S(1)} %copy-done.5, ...), custom_call_target="tpu_custom_call" | custom-call | tf_op jit(solution)/shard_map/decode/pallas_call | solution.py:520
  (20 shorter events, 0.0 us)
Async XLA Ops:
  0.0 80.4 %copy-start.14 = (bf16[256,1024]{1,0:T(8,128)(2,1)S(1)}, bf16[256,1024]{1,0:T(8,128)(2,1)}, u32[]{:S(2)}) copy-start(bf16[256,1024]{1,0:T(8,128)(2,1)} %wo_ref.3) | copy-start | bytes 1572868
  0.0 90.3 %copy-start.20 = (f32[1024]{0:T(1024)S(1)}, f32[1024]{0:T(1024)}, u32[]{:S(2)}) copy-start(f32[1024]{0:T(1024)} %param.37) | copy-start | bytes 12292
  60.7 29.6 %copy-start.8 = (bf16[3,1024,256]{2,1,0:T(8,128)(2,1)S(1)}, bf16[3,1024,256]{2,1,0:T(8,128)(2,1)}, u32[]{:S(2)}) copy-start(bf16[3,1024,256]{2,1,0:T(8,128)(2,1)} %w_ref.1) | copy-start | bytes 4718596
  60.7 19.7 %all-to-all-start = ((bf16[32,16,384]{2,1,0:T(8,128)(2,1)}), bf16[32,16,384]{2,1,0:T(8,128)(2,1)S(1)}, u32[]{:S(2)}, u32[]{:S(2)}) async-start(bf16[32,16,384]{2,1,0:T(8,128)(2,1)} %bitcast.15), calls=%async_computation | async-start | bytes 786432 | tf_op jit(solution)/shard_map/all_to_all | solution.py:613
  70.3 36.7 %copy-start.13 = (bf16[256,1024]{1,0:T(8,128)(2,1)S(1)}, bf16[256,1024]{1,0:T(8,128)(2,1)}, u32[]{:S(2)}) copy-start(bf16[256,1024]{1,0:T(8,128)(2,1)} %wo_ref.4) | copy-start | bytes 1572868
  70.3 36.7 %copy-start.15 = (f32[4,16,512]{2,1,0:T(8,128)S(1)}, f32[4,16,512]{2,1,0:T(8,128)}, u32[]{:S(2)}) copy-start(f32[4,16,512]{2,1,0:T(8,128)} %bias_ref.4) | copy-start | bytes 393220
  81.1 4.6 %collective-permute-start.2 = (f32[16,1024]{1,0:T(8,128)S(1)}, f32[16,1024]{1,0:T(8,128)S(1)}, u32[]{:S(2)}, u32[]{:S(2)}) collective-permute-start(f32[16,1024]{1,0:T(8,128)S(1)} %merge.1.a_ref), channel_id=1, source_target_pairs={{0,3},{1,0},{2,1},{3,2},{4,7},{5,4},{6,5},{7,6},{8,11},{9,8},{10,9... | collective-permute-start | bytes 196616 | tf_op jit(solution)/shard_map/ppermute | solution.py:561
  83.9 4.7 %collective-permute-start.1 = (f32[16,1024]{1,0:T(8,128)S(1)}, f32[16,1024]{1,0:T(8,128)S(1)}, u32[]{:S(2)}, u32[]{:S(2)}) collective-permute-start(f32[16,1024]{1,0:T(8,128)S(1)} %merge.1.a_ref), channel_id=1, source_target_pairs={{0,2},{1,3},{2,0},{3,1},{4,6},{5,7},{6,4},{7,5},{8,10},{9,11},{10,... | collective-permute-start | bytes 196616 | tf_op jit(solution)/shard_map/ppermute | solution.py:561
  84.2 6.0 %collective-permute-start = (f32[16,1024]{1,0:T(8,128)S(1)}, f32[16,1024]{1,0:T(8,128)S(1)}, u32[]{:S(2)}, u32[]{:S(2)}) collective-permute-start(f32[16,1024]{1,0:T(8,128)S(1)} %merge.1.a_ref), channel_id=1, source_target_pairs={{0,1},{1,2},{2,3},{3,0},{4,5},{5,6},{6,7},{7,4},{8,9},{9,10},{10,1... | collective-permute-start | bytes 196616 | tf_op jit(solution)/shard_map/ppermute | solution.py:561
  90.3 24.9 %copy-start.6 = (bf16[1024,1024]{1,0:T(8,128)(2,1)S(1)}, bf16[1024,1024]{1,0:T(8,128)(2,1)}, u32[]{:S(2)}) copy-start(bf16[1024,1024]{1,0:T(8,128)(2,1)} %w1_ref.1) | copy-start | bytes 6291460
  90.3 24.9 %copy-start.7 = (bf16[1024,1024]{1,0:T(8,128)(2,1)S(1)}, bf16[1024,1024]{1,0:T(8,128)(2,1)}, u32[]{:S(2)}) copy-start(bf16[1024,1024]{1,0:T(8,128)(2,1)} %w2_ref.1) | copy-start | bytes 6291460
  90.3 24.9 %copy-start.21 = (f32[1024]{0:T(1024)S(1)}, f32[1024]{0:T(1024)}, u32[]{:S(2)}) copy-start(f32[1024]{0:T(1024)} %param.41) | copy-start | bytes 12292
  108.4 3.1 %collective-permute-start.5 = (f32[16,1024]{1,0:T(8,128)S(1)}, f32[16,1024]{1,0:T(8,128)S(1)}, u32[]{:S(2)}, u32[]{:S(2)}) collective-permute-start(f32[16,1024]{1,0:T(8,128)S(1)} %attend.1.a_ref), channel_id=1, source_target_pairs={{0,3},{1,0},{2,1},{3,2},{4,7},{5,4},{6,5},{7,6},{8,11},{9,8},{10,9... | collective-permute-start | bytes 196616 | tf_op jit(solution)/shard_map/ppermute | solution.py:561
  108.7 4.6 %collective-permute-start.4 = (f32[16,1024]{1,0:T(8,128)S(1)}, f32[16,1024]{1,0:T(8,128)S(1)}, u32[]{:S(2)}, u32[]{:S(2)}) collective-permute-start(f32[16,1024]{1,0:T(8,128)S(1)} %attend.1.a_ref), channel_id=1, source_target_pairs={{0,2},{1,3},{2,0},{3,1},{4,6},{5,7},{6,4},{7,5},{8,10},{9,11},{10,... | collective-permute-start | bytes 196616 | tf_op jit(solution)/shard_map/ppermute | solution.py:561
  109.1 6.1 %collective-permute-start.3 = (f32[16,1024]{1,0:T(8,128)S(1)}, f32[16,1024]{1,0:T(8,128)S(1)}, u32[]{:S(2)}, u32[]{:S(2)}) collective-permute-start(f32[16,1024]{1,0:T(8,128)S(1)} %attend.1.a_ref), channel_id=1, source_target_pairs={{0,1},{1,2},{2,3},{3,0},{4,5},{5,6},{6,7},{7,4},{8,9},{9,10},{10,1... | collective-permute-start | bytes 196616 | tf_op jit(solution)/shard_map/ppermute | solution.py:561
  115.2 6.9 %copy-start.22 = (f32[1024]{0:T(1024)S(1)}, f32[1024]{0:T(1024)}, u32[]{:S(2)}) copy-start(f32[1024]{0:T(1024)} %param.44) | copy-start | bytes 12292
  116.1 14.2 %copy-start.3 = (bf16[2048,256]{1,0:T(8,128)(2,1)S(1)}, bf16[2048,256]{1,0:T(8,128)(2,1)}, u32[]{:S(2)}) copy-start(bf16[2048,256]{1,0:T(8,128)(2,1)} %x_ref.5) | copy-start | bytes 3145732
  116.1 14.2 %copy-start.9 = (bf16[256,1024]{1,0:T(8,128)(2,1)S(1)}, bf16[256,1024]{1,0:T(8,128)(2,1)}, u32[]{:S(2)}) copy-start(bf16[256,1024]{1,0:T(8,128)(2,1)} %wq_ref.3) | copy-start | bytes 1572868
  116.1 14.2 %copy-start.10 = (bf16[1024,256]{1,0:T(8,128)(2,1)S(1)}, bf16[1024,256]{1,0:T(8,128)(2,1)}, u32[]{:S(2)}) copy-start(bf16[1024,256]{1,0:T(8,128)(2,1)} %wo_ref.5) | copy-start | bytes 1572868
  116.1 14.2 %copy-start.16 = (f32[3,16,512]{2,1,0:T(8,128)S(1)}, f32[3,16,512]{2,1,0:T(8,128)}, u32[]{:S(2)}) copy-start(f32[3,16,512]{2,1,0:T(8,128)} %bias_ref.5) | copy-start | bytes 294916
  116.1 14.2 %copy-start.19 = (f32[3,256]{1,0:T(4,128)S(1)}, f32[3,256]{1,0:T(4,128)}, u32[]{:S(2)}) copy-start(f32[3,256]{1,0:T(4,128)} %table_ref.5) | copy-start | bytes 9220
  116.1 14.2 %copy-start.23 = (s32[16]{0:T(128)S(1)}, s32[16]{0:T(128)}, u32[]{:S(2)}) copy-start(s32[16]{0:T(128)} %mod_ref.5) | copy-start | bytes 196
  116.1 14.2 %copy-start.24 = (f32[256]{0:T(256)S(1)}, f32[256]{0:T(256)}, u32[]{:S(2)}) copy-start(f32[256]{0:T(256)} %param.46) | copy-start | bytes 3076
  116.1 3.2 %collective-permute-start.8 = (f32[16,1024]{1,0:T(8,128)S(1)}, f32[16,1024]{1,0:T(8,128)S(1)}, u32[]{:S(2)}, u32[]{:S(2)}) collective-permute-start(f32[16,1024]{1,0:T(8,128)S(1)} %get-tuple-element.19.a_ref), channel_id=1, source_target_pairs={{0,3},{1,0},{2,1},{3,2},{4,7},{5,4},{6,5},{7,6},{8,11},{9,8},{10,9... | collective-permute-start | bytes 196616 | tf_op jit(solution)/shard_map/ppermute | solution.py:561
  116.8 4.7 %collective-permute-start.7 = (f32[16,1024]{1,0:T(8,128)S(1)}, f32[16,1024]{1,0:T(8,128)S(1)}, u32[]{:S(2)}, u32[]{:S(2)}) collective-permute-start(f32[16,1024]{1,0:T(8,128)S(1)} %get-tuple-element.19.a_ref), channel_id=1, source_target_pairs={{0,2},{1,3},{2,0},{3,1},{4,6},{5,7},{6,4},{7,5},{8,10},{9,11},{10,... | collective-permute-start | bytes 196616 | tf_op jit(solution)/shard_map/ppermute | solution.py:561
  117.3 4.8 %collective-permute-start.6 = (f32[16,1024]{1,0:T(8,128)S(1)}, f32[16,1024]{1,0:T(8,128)S(1)}, u32[]{:S(2)}, u32[]{:S(2)}) collective-permute-start(f32[16,1024]{1,0:T(8,128)S(1)} %get-tuple-element.19.a_ref), channel_id=1, source_target_pairs={{0,1},{1,2},{2,3},{3,0},{4,5},{5,6},{6,7},{7,4},{8,9},{9,10},{10,1... | collective-permute-start | bytes 196616 | tf_op jit(solution)/shard_map/ppermute | solution.py:561
  123.5 24.1 %all-to-all-start.2 = ((bf16[32,16,1024]{2,1,0:T(8,128)(2,1)}), bf16[32,16,1024]{2,1,0:T(8,128)(2,1)S(1)}, u32[]{:S(2)}, u32[]{:S(2)}) async-start(bf16[32,16,1024]{2,1,0:T(8,128)(2,1)} %broadcast_in_dim.5), calls=%async_computation.2 | async-start | bytes 2097152 | tf_op jit(solution)/shard_map/all_to_all | solution.py:555
  135.6 2.0 %copy-start.1 = (bf16[1024,2048]{1,0:T(8,128)(2,1)}, bf16[1024,2048]{1,0:T(8,128)(2,1)S(1)}, u32[]{:S(2)}) copy-start(bf16[1024,2048]{1,0:T(8,128)(2,1)S(1)} %get-tuple-element.22.qt_ref) | copy-start | bytes 12582916
  137.6 1.3 copy-start.4
  138.9 0.8 copy-start.11
  139.7 0.6 copy-start.17
  147.6 2.2 %copy-start = (bf16[2,1024,1024]{2,1,0:T(8,128)(2,1)S(1)}, bf16[2,1024,1024]{2,1,0:T(8,128)(2,1)}, u32[]{:S(2)}) copy-start(bf16[2,1024,1024]{2,1,0:T(8,128)(2,1)} %wkv_ref.3) | copy-start | bytes 12582916
  149.8 2.2 %copy-start.2 = (bf16[1024,2048]{1,0:T(8,128)(2,1)S(1)}, bf16[1024,2048]{1,0:T(8,128)(2,1)}, u32[]{:S(2)}) copy-start(bf16[1024,2048]{1,0:T(8,128)(2,1)} %copy-done.1) | copy-start | bytes 12582916
  151.9 1.6 copy-start.5
  153.5 1.0 copy-start.12
  154.6 0.8 copy-start.18

commit v2 on v1

--- a/solution.py
+++ b/solution.py
@@ -71,9 +71,29 @@
     return layer_norm(embedded, gain).astype(BF)
 
 
+def part_rows(core, all_ref, own_ref, other_ref):
+    for held, refs in enumerate(((own_ref, other_ref), (other_ref, own_ref))):
+
+        @pl.when(core == held)
+        def _():
+            for block in range(all_ref.shape[0] // 16):
+                rows = slice(block // 2 * 16, block // 2 * 16 + 16)
+                refs[block % 2][rows, :] = all_ref[block * 16 : block * 16 + 16, :]
+
+
+def join_rows(core, own_ref, other_ref, all_ref):
+    for held, refs in enumerate(((own_ref, other_ref), (other_ref, own_ref))):
+
+        @pl.when(core == held)
+        def _():
+            for block in range(all_ref.shape[0] // 16):
+                all_ref[block * 16 : block * 16 + 16, :] = refs[block % 2][block // 2]
+
+
 def encode_kernel(
     heads,
     mod_ref,
+    core_ref,
     x_ref,
     next_ref,
     table_ref,
@@ -83,7 +103,8 @@
     wq_ref,
     wkv_ref,
     bias_ref,
-    out_ref,
+    keep_ref,
+    send_ref,
     qx_ref,
     norm_ref,
     wvt_ref,
@@ -96,6 +117,7 @@
     shift_ref,
     m_ref,
     acc_ref,
+    out_ref,
 ):
     step = pl.program_id(0)
     last = pl.num_programs(0) - 1
@@ -207,24 +229,25 @@
             for part, piece in enumerate(three_parts(m_ref[h] + jnp.log2(total))):
                 extra = jnp.where(index == heads * part + h, piece, extra)
         out_ref[...] = jnp.concatenate(pieces + [extra], axis=0).T.astype(BF)
-
-
-def encode(inputs, input_modality, table, gain, latents, lat_gain, wq, wkv, bias):
+        part_rows(core_ref[0], out_ref, keep_ref, send_ref)
+
+
+def encode(core, inputs, input_modality, table, gain, latents, lat_gain, wq, wkv, bias):
     points, width = inputs.shape
     heads = bias.shape[1]
     lat_count, lat_width = latents.shape
     cols = heads * HSZ
     tile = math.gcd(points, 1024)
     steps = points // tile
-    whole = lambda *shape: pl.BlockSpec(shape, lambda i, mod: (0,) * len(shape))
+    whole = lambda *shape: pl.BlockSpec(shape, lambda i, *_: (0,) * len(shape))
     return pl.pallas_call(
         functools.partial(encode_kernel, heads),
         grid_spec=pltpu.PrefetchScalarGridSpec(
-            num_scalar_prefetch=1,
+            num_scalar_prefetch=2,
             grid=(steps,),
             in_specs=[
-                pl.BlockSpec((tile, width), lambda i, mod: (0, 0)),
-                pl.BlockSpec((tile, width), lambda i, mod: (jnp.minimum(i + 1, steps - 1), 0)),
+                pl.BlockSpec((tile, width), lambda i, *_: (0, 0)),
+                pl.BlockSpec((tile, width), lambda i, *_: (jnp.minimum(i + 1, steps - 1), 0)),
                 whole(MODS, width),
                 whole(1, width),
                 whole(lat_count, lat_width),
@@ -233,7 +256,7 @@
                 whole(2, width, cols),
                 whole(MODS, heads, lat_count),
             ],
-            out_specs=whole(lat_count, cols + EXTRA),
+            out_specs=[whole(lat_count // 2, cols + EXTRA)] * 2,
             scratch_shapes=[
                 pltpu.VMEM((heads, 256, lat_count), BF),
                 pltpu.VMEM((heads, lat_count), F32),
@@ -247,39 +270,68 @@
                 pltpu.VMEM((2, heads, 1, lat_count), F32),
                 pltpu.VMEM((heads, 1, lat_count), F32),
                 pltpu.VMEM((heads, 128, lat_count), F32),
+                pltpu.VMEM((lat_count, cols + EXTRA), BF),
             ],
         ),
-        out_shape=jax.ShapeDtypeStruct((lat_count, cols + EXTRA), BF),
+        out_shape=[jax.ShapeDtypeStruct((lat_count // 2, cols + EXTRA), BF)] * 2,
         compiler_params=pltpu.CompilerParams(vmem_limit_bytes=58 * MIB),
         name="encode",
-    )(input_modality, inputs, inputs, table, gain, latents, lat_gain, wq, wkv, bias)
-
-
-def small_call(kernel, name, outs, *args):
+    )(input_modality, core, inputs, inputs, table, gain, latents, lat_gain, wq, wkv, bias)
+
+
+def small_call(kernel, name, outs, *args, scratch=()):
+    space = lambda a: pltpu.SMEM if a.dtype == jnp.int32 else pltpu.VMEM
     return pl.pallas_call(
         kernel,
         out_shape=outs,
-        in_specs=[pl.BlockSpec(memory_space=pltpu.VMEM)] * len(args),
+        in_specs=[pl.BlockSpec(memory_space=space(a)) for a in args],
+        scratch_shapes=list(scratch),
         out_specs=jax.tree.map(lambda _: pl.BlockSpec(memory_space=pltpu.VMEM), outs),
         compiler_params=pltpu.CompilerParams(vmem_limit_bytes=24 * MIB),
         name=name,
     )(*args)
 
 
+def log_totals(heads, extra):
+    lse = extra[..., :heads]
+    for part in range(1, 3):
+        lse = lse + extra[..., heads * part : heads * (part + 1)]
+    return lse
+
+
+def per_head(heads, factor, shape):
+    lane = lax.broadcasted_iota(jnp.int32, shape, len(shape) - 1) // HSZ
+    spread = jnp.zeros(shape, F32)
+    for h in range(heads):
+        spread = jnp.where(lane == h, factor[..., h : h + 1], spread)
+    return spread
+
+
+def pair_kernel(heads, a_ref, b_ref, out_ref):
+    cols = heads * HSZ
+    rows = a_ref.shape[0]
+    first = log_totals(heads, a_ref[:, cols:].astype(F32))
+    second = log_totals(heads, b_ref[:, cols:].astype(F32))
+    top = jnp.maximum(first, second)
+    first, second = jnp.exp2(first - top), jnp.exp2(second - top)
+    total = first + second
+    joint = a_ref[:, :cols].astype(F32) * per_head(heads, first / total, (rows, cols))
+    joint = joint + b_ref[:, :cols].astype(F32) * per_head(heads, second / total, (rows, cols))
+    out_ref[:, :cols] = joint.astype(BF)
+    lane = lax.broadcasted_iota(jnp.int32, (rows, EXTRA), 1)
+    extra = jnp.zeros((rows, EXTRA), F32)
+    for part, piece in enumerate(three_parts(top + jnp.log2(total))):
+        for h in range(heads):
+            extra = jnp.where(lane == heads * part + h, piece[:, h : h + 1], extra)
+    out_ref[:, cols:] = extra.astype(BF)
+
+
 def merge_kernel(heads, part_ref, wo_ref, out_ref):
     cols = heads * HSZ
-    extra = part_ref[:, :, cols:].astype(F32)
-    sources, rows, _ = extra.shape
-    lse = extra[:, :, :heads]
-    for part in range(1, 3):
-        lse = lse + extra[:, :, heads * part : heads * (part + 1)]
-    top = jnp.max(lse, axis=0, keepdims=True)
-    factor = jnp.exp2(lse - top)
+    lse = log_totals(heads, part_ref[:, :, cols:].astype(F32))
+    factor = jnp.exp2(lse - jnp.max(lse, axis=0, keepdims=True))
     factor = factor / jnp.sum(factor, axis=0, keepdims=True)
-    lane = lax.broadcasted_iota(jnp.int32, (sources, rows, cols), 2)
-    spread = jnp.zeros((sources, rows, cols), F32)
-    for h in range(heads):
-        spread = jnp.where(lane // HSZ == h, factor[:, :, h : h + 1], spread)
+    spread = per_head(heads, factor, part_ref.shape[:2] + (cols,))
     attended = jnp.sum(part_ref[:, :, :cols].astype(F32) * spread, axis=0)
     out_ref[...] = dot(attended.astype(BF), wo_ref[...])
 
@@ -290,11 +342,15 @@
     normed = layer_norm(lat, gain_ref[...]).astype(BF)
     cols = w_ref.shape[2]
     q_out[...] = (dot(normed, w_ref[0]) * SCALE2).astype(BF)
-    kv_out[:, :cols] = dot(normed, w_ref[1]).astype(BF)
-    kv_out[:, cols:] = dot(normed, w_ref[2]).astype(BF)
-
-
-def attend_kernel(heads, q_ref, kv_ref, bias_ref, wo_ref, out_ref):
+    keys = dot(normed, w_ref[1]).astype(BF)
+    values = dot(normed, w_ref[2]).astype(BF)
+    for copy in range(kv_out.shape[0]):
+        kv_out[copy, :, :cols] = keys
+        kv_out[copy, :, cols:] = values
+
+
+def attend_kernel(heads, core_ref, q_ref, own_ref, other_ref, bias_ref, wo_ref, out_ref, kv_ref):
+    join_rows(core_ref[0], own_ref, other_ref, kv_ref)
     cols = heads * HSZ
     query = q_ref[...]
     rows = query.shape[0]
@@ -321,7 +377,9 @@
 
 def last_kernel(a_ref, b_ref, c_ref, d_ref, lat_ref, gain_ref, out_ref):
     lat = lat_ref[...] + ((a_ref[...] + b_ref[...]) + (c_ref[...] + d_ref[...]))
-    out_ref[...] = layer_norm(lat, gain_ref[...]).astype(BF)
+    normed = layer_norm(lat, gain_ref[...]).astype(BF)
+    for copy in range(out_ref.shape[0]):
+        out_ref[copy] = normed
 
 
 def query_kernel(
@@ -416,7 +474,7 @@
             jax.ShapeDtypeStruct((heads, lat_count, 128), BF),
             jax.ShapeDtypeStruct((width, cols), BF),
         ],
-        compiler_params=pltpu.CompilerParams(vmem_limit_bytes=28 * MIB),
+        compiler_params=pltpu.CompilerParams(vmem_limit_bytes=58 * MIB),
         name="queries",
     )(query_modality, queries, table, gain, wq, bias, wo)
 
@@ -424,9 +482,11 @@
 def decode_kernel(
     heads,
     mod_ref,
+    core_ref,
     x_ref,
     table_ref,
-    lat_ref,
+    own_ref,
+    other_ref,
     wkv_ref,
     bias_ref,
     qt_ref,
@@ -435,6 +495,7 @@
     top_ref,
     wot_ref,
     out_ref,
+    lat_ref,
     kx_ref,
     vx_ref,
     long_ref,
@@ -449,6 +510,7 @@
 
     @pl.when(step == 0)
     def _():
+        join_rows(core_ref[0], own_ref, other_ref, lat_ref)
         normed = lat_ref[...]
         ones = jnp.ones((HSZ, lat_count), BF)
         lane = lax.broadcasted_iota(jnp.int32, (lat_count, 128), 1) // HSZ
@@ -509,33 +571,36 @@
         out_ref[rows, :] = embedded + decoded[rows, :]
 
 
-def decode(queries, query_modality, table, normed, wkv, prepared):
+def decode(core, queries, query_modality, table, own, other, wkv, prepared):
     queries_t, hot, norms, tops, bias, wo_t = prepared
     count, width = queries.shape
     heads, lat_count = bias.shape[:2]
     cols = heads * HSZ
     tile = math.gcd(count, 512)
-    held = pl.BlockSpec(memory_space=pltpu.VMEM)
-    tiled = lambda rows: pl.BlockSpec((rows, tile), lambda i, mod: (0, i))
+    lat_width = wkv.shape[1]
+    whole = lambda a: pl.BlockSpec(a.shape, lambda i, *_: (0,) * a.ndim)
+    tiled = lambda rows: pl.BlockSpec((rows, tile), lambda i, *_: (0, i))
     return pl.pallas_call(
         functools.partial(decode_kernel, heads),
         grid_spec=pltpu.PrefetchScalarGridSpec(
-            num_scalar_prefetch=1,
+            num_scalar_prefetch=2,
             grid=(count // tile,),
             in_specs=[
-                pl.BlockSpec((tile, width), lambda i, mod: (i, 0)),
-                held,
-                held,
-                held,
-                held,
+                pl.BlockSpec((tile, width), lambda i, *_: (i, 0)),
+                whole(table),
+                whole(own),
+                whole(other),
+                whole(wkv),
+                whole(bias),
                 tiled(cols),
                 tiled(16),
                 tiled(heads),
                 tiled(heads),
-                held,
+                whole(wo_t),
             ],
-            out_specs=pl.BlockSpec((tile, width), lambda i, mod: (i, 0)),
+            out_specs=pl.BlockSpec((tile, width), lambda i, *_: (i, 0)),
             scratch_shapes=[
+                pltpu.VMEM((lat_count, lat_width), BF),
                 pltpu.VMEM((heads, lat_count, 256), BF),
                 pltpu.VMEM((heads, 128, lat_count), BF),
                 pltpu.VMEM((heads, 128), F32),
@@ -545,14 +610,19 @@
             ],
         ),
         out_shape=jax.ShapeDtypeStruct((count, width), F32),
-        compiler_params=pltpu.CompilerParams(vmem_limit_bytes=32 * MIB),
+        compiler_params=pltpu.CompilerParams(vmem_limit_bytes=58 * MIB),
         name="decode",
-    )(query_modality, queries, table, normed, wkv, bias, queries_t, hot, norms, tops, wo_t)
-
-
-def share(rows):
-    copies = jnp.broadcast_to(rows[None], (lax.axis_size("inp"),) + rows.shape)
-    return lax.all_to_all(copies, "inp", 0, 0)
+    )(query_modality, core, queries, table, own, other, wkv, bias, queries_t, hot, norms, tops, wo_t)
+
+
+def trade(parts):
+    size = lax.axis_size("inp")
+    groups = [list(range(core, size, 2)) for core in range(2)]
+    return lax.all_to_all(parts, "inp", 0, 0, axis_index_groups=groups)
+
+
+def other_core(rows):
+    return lax.ppermute(rows, "inp", [(i, i ^ 1) for i in range(lax.axis_size("inp"))])
 
 
 def head_parts(part):
@@ -599,7 +669,10 @@
     row = lambda v: v.reshape(1, -1)
     shape = jax.ShapeDtypeStruct
 
-    own = encode(
+    core = (lax.axis_index("inp") % 2).astype(jnp.int32).reshape(1)
+    chips = lax.axis_size("inp") // 2
+    keep, send = encode(
+        core,
         inputs,
         input_modality,
         modality_embed,
@@ -610,12 +683,21 @@
         enc_wkv,
         enc_bias,
     )
-    parts = lax.all_to_all(own.reshape(-1, lat_rows, own.shape[1]), "inp", 0, 0)
+    joint = small_call(
+        functools.partial(pair_kernel, heads),
+        "pair",
+        shape(keep.shape, BF),
+        keep,
+        other_core(send),
+    )
+    joint, early = lax.optimization_barrier((joint, queries))
+    parts = trade(joint.reshape(chips, lat_rows, joint.shape[1]))
+    prepared = prepare_queries(
+        early, query_modality, modality_embed, row(query_gain), dec_wq, dec_bias, dec_wo
+    )
+    parts, prepared = lax.optimization_barrier((parts, prepared))
     enc_part = small_call(
         functools.partial(merge_kernel, heads), "merge", shape((lat_rows, width), F32), parts, enc_wo
-    )
-    prepared = prepare_queries(
-        queries, query_modality, modality_embed, row(query_gain), dec_wq, dec_bias, dec_wo
     )
     latent_rows = lax.dynamic_slice_in_dim(latents, row_first, lat_rows, 0)
     lat_one, self_q, self_kv = small_call(
@@ -624,22 +706,25 @@
         [
             shape((lat_rows, width), F32),
             shape((lat_rows, cols), BF),
-            shape((lat_rows, 2 * cols), BF),
+            shape((chips, lat_rows, 2 * cols), BF),
         ],
         *head_parts(enc_part),
         latent_rows,
         row(self_gain),
         self_wqkv,
     )
-    all_kv = share(self_kv).reshape(lat_count, 2 * cols)
+    own_kv = trade(self_kv)
     self_part = small_call(
         functools.partial(attend_kernel, heads),
         "attend",
         shape((lat_rows, width), F32),
+        core,
         self_q,
-        all_kv,
+        own_kv,
+        other_core(own_kv),
         self_bias,
         self_wo,
+        scratch=[pltpu.VMEM((lat_count, 2 * cols), BF)],
     )
     lat_two, mlp_part = small_call(
         mlp_kernel,
@@ -654,13 +739,15 @@
     normed = small_call(
         last_kernel,
         "last",
-        shape((lat_rows, width), BF),
+        shape((chips, lat_rows, width), BF),
         *head_parts(mlp_part),
         lat_two,
         row(dec_gain),
     )
-    all_normed = share(normed).reshape(lat_count, width)
-    return decode(queries, query_modality, modality_embed, all_normed, dec_wkv, prepared)
+    own = trade(normed)
+    return decode(
+        core, queries, query_modality, modality_embed, own, other_core(own), dec_wkv, prepared
+    )
 
 
 def solution(mesh):

time: 180 us -> 173 us (0.961)
  waiting for transfers between devices: 31.6 us -> 16.7 us
  local copies, waits for them, and re-layouts: 14.7 us -> 2.61 us
  blocking collectives: 16.1 us -> 25.7 us
  Pallas kernels: 93.9 us -> 102 us
    all_to_all x2 -> x1, waiting for transfers between devices: 17.4 us -> 0.01 us  [trade(): return lax.all_to_all(parts, 'inp', 0, 0, axis_index_groups=groups)]
    unnamed x50 -> x24, local copies, waits for them, and re-layouts: 12.6 us -> 1.77 us
    ppermute x0 -> x3, starting transfers between devices: none -> 9.81 us  [other_core(): lax.ppermute(rows, 'inp', [(i, i ^ 1) for i in range(lax.axis_size('inp'))])]
    all_to_all x1 -> x2, blocking collectives: 16.1 us -> 25.7 us  [trade(): return lax.all_to_all(parts, 'inp', 0, 0, axis_index_groups=groups)]
    all_to_all x2 -> x1, starting transfers between devices: 16.3 us -> 7.67 us  [trade(): return lax.all_to_all(parts, 'inp', 0, 0, axis_index_groups=groups)]
    ppermute x0 -> x3, waiting for transfers between devices: none -> 3.98 us  [other_core(): lax.ppermute(rows, 'inp', [(i, i ^ 1) for i in range(lax.axis_size('inp'))])]
    pallas_call x1, Pallas kernels: 24.2 us -> 28 us  [decode(): pl.pallas_call(functools.partial(decode_kernel, heads), grid_spec=pltpu.P...]
    pallas_call x1, Pallas kernels: 5.24 us -> 8.95 us  [prepare_queries(): pl.pallas_call(functools.partial(query_kernel, heads), grid_spec=pltpu.Pr...]
  transfers between devices with their start and end apart: 11 -> 13, of which waited for: 10 -> 11; matrix products, arithmetic and copies ran while one was open for 0% -> 0% of each run, Pallas kernels for 3% -> 5%
where the time goes in v2:
time: 173 us; the launch traced here: 172 us
  Pallas kernels  102 us (59%)
  blocking collectives  25.7 us (15%)
  starting transfers between devices  24.7 us (14%)
  waiting for transfers between devices  16.7 us (10%)
  local copies, waits for them, and re-layouts  2.61 us (2%)
    pallas_call x1, Pallas kernels, encode(): pl.pallas_call(functools.partial(encode_kernel, heads), grid_spec=pltpu.P...  60.4 us
    pallas_call x1, Pallas kernels, decode(): pl.pallas_call(functools.partial(decode_kernel, heads), grid_spec=pltpu.P...  28 us
    all_to_all x2, blocking collectives, trade(): return lax.all_to_all(parts, 'inp', 0, 0, axis_index_groups=groups)  25.7 us
    ppermute x9, waiting for transfers between devices, head_parts(): lax.ppermute(part, 'head', [(i, (i + k) % size) for i in range(size)])  12.7 us
    ppermute x3, starting transfers between devices, other_core(): lax.ppermute(rows, 'inp', [(i, i ^ 1) for i in range(lax.axis_size('inp'))])  9.81 us
    pallas_call x1, Pallas kernels, prepare_queries(): pl.pallas_call(functools.partial(query_kernel, heads), grid_spec=pltpu.Pr...  8.95 us
    all_to_all x1, starting transfers between devices, trade(): return lax.all_to_all(parts, 'inp', 0, 0, axis_index_groups=groups)  7.67 us
    ppermute x9, starting transfers between devices, head_parts(): lax.ppermute(part, 'head', [(i, (i + k) % size) for i in range(size)])  7.21 us
  transfers between devices with their start and end apart: 13, of which 11 were waited for; matrix products, arithmetic and copies ran while one was open for 0% of the time, Pallas kernels for 5%

profile of v2, /device:TPU:1, one launch (start us, length us, event | category | flops | bytes accessed | tf_op | source)
XLA Modules:
  0.0 172.3 jit_solution(17898526107197098682)
XLA Ops:
  0.0 0.0 copy-start.7
  0.0 60.4 %encode.1 = (bf16[256,384]{1,0:T(8,128)(2,1)}, bf16[256,384]{1,0:T(8,128)(2,1)}) custom-call(s32[64]{0:T(128)} %mod_ref.3, s32[1]{0:T(128)} %bitcast.core_ref, bf16[8192,256]{1,0:T(8,128)(2,1)} %next_ref.1, bf16[8192,256]{1,0:T(8,128)(2,1)} %next_ref.1, f32[3,256]{1,0:T(4,128)} %table_ref.5, f32[1,256]{1,0:T(1,128)} %bitcast.12, f32[512,1024]{1,0:T(8,128)} %lat_ref.1, ...), custom_call_target="tpu_custom_call" | custom-call | tf_op jit(solution)/shard_map/encode/pallas_call | solution.py:243
  60.4 0.0 copy-start.3
  60.4 0.0 copy-start.2
  60.4 1.5 collective-permute-start
  61.9 1.3 collective-permute-done.b_ref
  63.2 0.0 copy-start.5
  63.2 0.9 copy-done.5
  64.2 1.5 pair.1
  65.6 7.7 %all-to-all-start = ((bf16[16,16,384]{2,1,0:T(8,128)(2,1)}), bf16[16,16,384]{2,1,0:T(8,128)(2,1)S(1)}, u32[]{:S(2)}, u32[]{:S(2)}) async-start(bf16[16,16,384]{2,1,0:T(8,128)(2,1)} %bitcast.3), calls=%async_computation | async-start | bytes 393216 | tf_op jit(solution)/shard_map/all_to_all | solution.py:621
  73.3 0.0 copy-start.4
  73.3 8.9 %queries.1 = (bf16[1024,2048]{1,0:T(8,128)(2,1)}, bf16[16,2048]{1,0:T(8,128)(2,1)}, f32[16,2048]{1,0:T(8,128)}, f32[16,2048]{1,0:T(8,128)}, bf16[16,512,128]{2,1,0:T(8,128)(2,1)}, /*index=5*/bf16[256,1024]{1,0:T(8,128)(2,1)}) custom-call(s32[16]{0:T(128)} %mod_ref.5, bf16[2048,256]{1,0:T(8,128)(2,1)} %x_ref.4, f32[3,256]{1,0:T(4,128)} %table_ref.5, ...), custom_call_target="tpu_custom_call" | custom-call | tf_op jit(solution)/shard_map/queries/pallas_call | solution.py:442
  82.2 0.0 copy-start.6
  82.3 0.0 all-to-all-done.part_ref
  82.3 0.0 copy-done.3
  82.3 0.0 copy-start.1
  82.3 0.5 merge.1.a_ref
  82.8 0.0 copy-start
  82.8 0.0 copy-start.8
  82.8 2.8 %collective-permute-start.3 = (f32[16,1024]{1,0:T(8,128)S(1)}, f32[16,1024]{1,0:T(8,128)S(1)}, u32[]{:S(2)}, u32[]{:S(2)}) collective-permute-start(f32[16,1024]{1,0:T(8,128)S(1)} %merge.1.a_ref), channel_id=1, source_target_pairs={{0,3},{1,0},{2,1},{3,2},{4,7},{5,4},{6,5},{7,6},{8,11},{9,8},{10,9... | collective-permute-start | bytes 196616 | tf_op jit(solution)/shard_map/ppermute | solution.py:631
  85.6 0.4 collective-permute-start.2
  86.0 0.7 collective-permute-start.1
  86.6 0.8 constant_dynamic-slice_fusion.lat_ref
  87.5 0.0 collective-permute-done.3.d_ref
  87.5 2.8 %collective-permute-done.2.c_ref = f32[16,1024]{1,0:T(8,128)S(1)} collective-permute-done((f32[16,1024]{1,0:T(8,128)S(1)}, f32[16,1024]{1,0:T(8,128)S(1)}, u32[]{:S(2)}, u32[]{:S(2)}) %collective-permute-start.2) | collective-permute-done | bytes 65568 | tf_op jit(solution)/shard_map/ppermute | solution.py:631
  90.3 0.6 collective-permute-done.1.b_ref
  90.9 0.0 copy-done.7
  90.9 0.0 copy-done.2
  90.9 0.5 project.1
  91.4 14.1 %all_to_all.15.own_ref = bf16[16,16,512]{2,1,0:T(8,128)(2,1)S(1)} all-to-all(bf16[16,16,512]{2,1,0:T(8,128)(2,1)S(1)} %get-tuple-element.39), channel_id=1, replica_groups={{0,8,16,24,32,40,48,56,64,72,80,88,96,104,112,120},{4,12,20,28,36,44,52..., dimensions={0} | all-to-all | bytes 524288 | tf_op jit(solution)/shard_map/all_to_all | solution.py:621
  105.5 3.7 %collective-permute-start.4 = (bf16[16,16,512]{2,1,0:T(8,128)(2,1)S(1)}, bf16[16,16,512]{2,1,0:T(8,128)(2,1)S(1)}, u32[]{:S(2)}, u32[]{:S(2)}) collective-permute-start(bf16[16,16,512]{2,1,0:T(8,128)(2,1)S(1)} %all_to_all.15.own_ref), channel_id=1, source_target_pairs={{0,4},{4,0},{8,12},{12,8},{16,20},{20,16},{24,28},{28,24},{32,36},... | collective-permute-start | bytes 786440 | tf_op jit(solution)/shard_map/ppermute | solution.py:625
  109.2 1.2 collective-permute-done.4.other_ref
  110.4 0.0 copy-done.4
  110.4 0.0 copy-done.6
  110.4 1.5 attend.1.a_ref
  111.9 0.3 collective-permute-start.7
  112.2 0.8 collective-permute-start.6
  113.0 0.8 collective-permute-start.5
  113.8 1.2 collective-permute-done.7.d_ref
  115.0 1.8 %collective-permute-done.6.c_ref = f32[16,1024]{1,0:T(8,128)S(1)} collective-permute-done((f32[16,1024]{1,0:T(8,128)S(1)}, f32[16,1024]{1,0:T(8,128)S(1)}, u32[]{:S(2)}, u32[]{:S(2)}) %collective-permute-start.6) | collective-permute-done | bytes 65568 | tf_op jit(solution)/shard_map/ppermute | solution.py:631
  116.8 1.9 %collective-permute-done.5.b_ref = f32[16,1024]{1,0:T(8,128)S(1)} collective-permute-done((f32[16,1024]{1,0:T(8,128)S(1)}, f32[16,1024]{1,0:T(8,128)S(1)}, u32[]{:S(2)}, u32[]{:S(2)}) %collective-permute-start.5) | collective-permute-done | bytes 65568 | tf_op jit(solution)/shard_map/ppermute | solution.py:631
  118.8 0.0 copy-done.1
  118.8 0.0 copy-done
  118.8 0.0 copy-done.8
  118.8 0.0 copy-start.9
  118.8 0.8 mlp.1
  119.6 0.5 collective-permute-start.10
  120.1 0.6 collective-permute-start.9
  120.7 0.4 collective-permute-start.8
  121.1 1.6 collective-permute-done.10.d_ref
  122.7 2.0 %collective-permute-done.9.c_ref = f32[16,1024]{1,0:T(8,128)S(1)} collective-permute-done((f32[16,1024]{1,0:T(8,128)S(1)}, f32[16,1024]{1,0:T(8,128)S(1)}, u32[]{:S(2)}, u32[]{:S(2)}) %collective-permute-start.9) | collective-permute-done | bytes 65568 | tf_op jit(solution)/shard_map/ppermute | solution.py:631
  124.7 0.7 collective-permute-done.8.b_ref
  125.4 0.0 copy-done.9
  125.4 0.2 last.1
  125.7 11.6 %all_to_all.16.own_ref = bf16[16,16,1024]{2,1,0:T(8,128)(2,1)S(1)} all-to-all(bf16[16,16,1024]{2,1,0:T(8,128)(2,1)S(1)} %last.1), channel_id=1, replica_groups={{0,8,16,24,32,40,48,56,64,72,80,88,96,104,112,120},{4,12,20,28,36,44,52..., dimensions={0} | all-to-all | bytes 1048576 | tf_op jit(solution)/shard_map/all_to_all | solution.py:621
  137.3 0.0 copy-start.10
  137.3 4.6 %collective-permute-start.11 = (bf16[16,16,1024]{2,1,0:T(8,128)(2,1)S(1)}, bf16[16,16,1024]{2,1,0:T(8,128)(2,1)S(1)}, u32[]{:S(2)}, u32[]{:S(2)}) collective-permute-start(bf16[16,16,1024]{2,1,0:T(8,128)(2,1)S(1)} %all_to_all.16.own_ref), channel_id=1, source_target_pairs={{0,4},{4,0},{8,12},{12,8},{16,20},{20,16},{24,28},{28,24},{32,36},... | collective-permute-start | bytes 1572872 | tf_op jit(solution)/shard_map/ppermute | solution.py:625
  141.9 1.5 collective-permute-done.11.other_ref
  143.4 0.0 copy-done.10
  143.4 0.0 copy-start.11
  143.4 0.8 copy-done.11
  144.2 28.0 %decode.1 = f32[2048,256]{1,0:T(8,128)} custom-call(s32[16]{0:T(128)} %mod_ref.5, s32[1]{0:T(128)} %bitcast.core_ref, bf16[2048,256]{1,0:T(8,128)(2,1)} %x_ref.4, f32[3,256]{1,0:T(4,128)} %table_ref.5, bf16[16,16,1024]{2,1,0:T(8,128)(2,1)} %copy-done.10, bf16[16,16,1024]{2,1,0:T(8,128)(2,1)} %copy-done.11, bf16[2,1024,1024]{2,1,0:T(8,128)(2,1)} %wkv_ref.3, ...), custom_call_target="tpu_custom_call" | custom-call | tf_op jit(solution)/shard_map/decode/pallas_call | solution.py:583
Async XLA Ops:
  0.0 90.9 %copy-start.7 = (f32[1024]{0:T(1024)S(1)}, f32[1024]{0:T(1024)}, u32[]{:S(2)}) copy-start(f32[1024]{0:T(1024)} %param.37) | copy-start | bytes 12292
  60.4 21.9 %copy-start.3 = (bf16[256,1024]{1,0:T(8,128)(2,1)S(1)}, bf16[256,1024]{1,0:T(8,128)(2,1)}, u32[]{:S(2)}) copy-start(bf16[256,1024]{1,0:T(8,128)(2,1)} %wo_ref.4) | copy-start | bytes 1572868
  60.4 30.5 %copy-start.2 = (bf16[3,1024,256]{2,1,0:T(8,128)(2,1)S(1)}, bf16[3,1024,256]{2,1,0:T(8,128)(2,1)}, u32[]{:S(2)}) copy-start(bf16[3,1024,256]{2,1,0:T(8,128)(2,1)} %w_ref.1) | copy-start | bytes 4718596
  60.4 2.8 %collective-permute-start = (bf16[256,384]{1,0:T(8,128)(2,1)}, bf16[256,384]{1,0:T(8,128)(2,1)S(1)}, u32[]{:S(2)}, u32[]{:S(2)}) collective-permute-start(bf16[256,384]{1,0:T(8,128)(2,1)} %get-tuple-element.28), channel_id=1, source_target_pairs={{0,4},{4,0},{8,12},{12,8},{16,20},{20,16},{24,28},{28,24},{32,36},... | collective-permute-start | bytes 589832 | tf_op jit(solution)/shard_map/ppermute | solution.py:625
  63.2 0.9 copy-start.5
  65.6 16.7 %all-to-all-start = ((bf16[16,16,384]{2,1,0:T(8,128)(2,1)}), bf16[16,16,384]{2,1,0:T(8,128)(2,1)S(1)}, u32[]{:S(2)}, u32[]{:S(2)}) async-start(bf16[16,16,384]{2,1,0:T(8,128)(2,1)} %bitcast.3), calls=%async_computation | async-start | bytes 393216 | tf_op jit(solution)/shard_map/all_to_all | solution.py:621
  73.3 37.1 %copy-start.4 = (bf16[256,1024]{1,0:T(8,128)(2,1)S(1)}, bf16[256,1024]{1,0:T(8,128)(2,1)}, u32[]{:S(2)}) copy-start(bf16[256,1024]{1,0:T(8,128)(2,1)} %wo_ref.5) | copy-start | bytes 1572868
  82.2 28.1 %copy-start.6 = (f32[4,16,512]{2,1,0:T(8,128)S(1)}, f32[4,16,512]{2,1,0:T(8,128)}, u32[]{:S(2)}) copy-start(f32[4,16,512]{2,1,0:T(8,128)} %bias_ref.5) | copy-start | bytes 393220
  82.3 36.5 %copy-start.1 = (bf16[1024,1024]{1,0:T(8,128)(2,1)S(1)}, bf16[1024,1024]{1,0:T(8,128)(2,1)}, u32[]{:S(2)}) copy-start(bf16[1024,1024]{1,0:T(8,128)(2,1)} %w2_ref.1) | copy-start | bytes 6291460
  82.8 35.9 %copy-start = (bf16[1024,1024]{1,0:T(8,128)(2,1)S(1)}, bf16[1024,1024]{1,0:T(8,128)(2,1)}, u32[]{:S(2)}) copy-start(bf16[1024,1024]{1,0:T(8,128)(2,1)} %w1_ref.1) | copy-start | bytes 6291460
  82.8 35.9 %copy-start.8 = (f32[1024]{0:T(1024)S(1)}, f32[1024]{0:T(1024)}, u32[]{:S(2)}) copy-start(f32[1024]{0:T(1024)} %param.41) | copy-start | bytes 12292
  82.8 4.7 %collective-permute-start.3 = (f32[16,1024]{1,0:T(8,128)S(1)}, f32[16,1024]{1,0:T(8,128)S(1)}, u32[]{:S(2)}, u32[]{:S(2)}) collective-permute-start(f32[16,1024]{1,0:T(8,128)S(1)} %merge.1.a_ref), channel_id=1, source_target_pairs={{0,3},{1,0},{2,1},{3,2},{4,7},{5,4},{6,5},{7,6},{8,11},{9,8},{10,9... | collective-permute-start | bytes 196616 | tf_op jit(solution)/shard_map/ppermute | solution.py:631
  85.6 4.7 %collective-permute-start.2 = (f32[16,1024]{1,0:T(8,128)S(1)}, f32[16,1024]{1,0:T(8,128)S(1)}, u32[]{:S(2)}, u32[]{:S(2)}) collective-permute-start(f32[16,1024]{1,0:T(8,128)S(1)} %merge.1.a_ref), channel_id=1, source_target_pairs={{0,2},{1,3},{2,0},{3,1},{4,6},{5,7},{6,4},{7,5},{8,10},{9,11},{10,... | collective-permute-start | bytes 196616 | tf_op jit(solution)/shard_map/ppermute | solution.py:631
  86.0 5.0 %collective-permute-start.1 = (f32[16,1024]{1,0:T(8,128)S(1)}, f32[16,1024]{1,0:T(8,128)S(1)}, u32[]{:S(2)}, u32[]{:S(2)}) collective-permute-start(f32[16,1024]{1,0:T(8,128)S(1)} %merge.1.a_ref), channel_id=1, source_target_pairs={{0,1},{1,2},{2,3},{3,0},{4,5},{5,6},{6,7},{7,4},{8,9},{9,10},{10,1... | collective-permute-start | bytes 196616 | tf_op jit(solution)/shard_map/ppermute | solution.py:631
  105.5 4.8 %collective-permute-start.4 = (bf16[16,16,512]{2,1,0:T(8,128)(2,1)S(1)}, bf16[16,16,512]{2,1,0:T(8,128)(2,1)S(1)}, u32[]{:S(2)}, u32[]{:S(2)}) collective-permute-start(bf16[16,16,512]{2,1,0:T(8,128)(2,1)S(1)} %all_to_all.15.own_ref), channel_id=1, source_target_pairs={{0,4},{4,0},{8,12},{12,8},{16,20},{20,16},{24,28},{28,24},{32,36},... | collective-permute-start | bytes 786440 | tf_op jit(solution)/shard_map/ppermute | solution.py:625
  111.9 3.1 %collective-permute-start.7 = (f32[16,1024]{1,0:T(8,128)S(1)}, f32[16,1024]{1,0:T(8,128)S(1)}, u32[]{:S(2)}, u32[]{:S(2)}) collective-permute-start(f32[16,1024]{1,0:T(8,128)S(1)} %attend.1.a_ref), channel_id=1, source_target_pairs={{0,3},{1,0},{2,1},{3,2},{4,7},{5,4},{6,5},{7,6},{8,11},{9,8},{10,9... | collective-permute-start | bytes 196616 | tf_op jit(solution)/shard_map/ppermute | solution.py:631
  112.2 4.6 %collective-permute-start.6 = (f32[16,1024]{1,0:T(8,128)S(1)}, f32[16,1024]{1,0:T(8,128)S(1)}, u32[]{:S(2)}, u32[]{:S(2)}) collective-permute-start(f32[16,1024]{1,0:T(8,128)S(1)} %attend.1.a_ref), channel_id=1, source_target_pairs={{0,2},{1,3},{2,0},{3,1},{4,6},{5,7},{6,4},{7,5},{8,10},{9,11},{10,... | collective-permute-start | bytes 196616 | tf_op jit(solution)/shard_map/ppermute | solution.py:631
  113.0 5.7 %collective-permute-start.5 = (f32[16,1024]{1,0:T(8,128)S(1)}, f32[16,1024]{1,0:T(8,128)S(1)}, u32[]{:S(2)}, u32[]{:S(2)}) collective-permute-start(f32[16,1024]{1,0:T(8,128)S(1)} %attend.1.a_ref), channel_id=1, source_target_pairs={{0,1},{1,2},{2,3},{3,0},{4,5},{5,6},{6,7},{7,4},{8,9},{9,10},{10,1... | collective-permute-start | bytes 196616 | tf_op jit(solution)/shard_map/ppermute | solution.py:631
  118.8 6.7 %copy-start.9 = (f32[1024]{0:T(1024)S(1)}, f32[1024]{0:T(1024)}, u32[]{:S(2)}) copy-start(f32[1024]{0:T(1024)} %param.44) | copy-start | bytes 12292
  119.6 3.1 %collective-permute-start.10 = (f32[16,1024]{1,0:T(8,128)S(1)}, f32[16,1024]{1,0:T(8,128)S(1)}, u32[]{:S(2)}, u32[]{:S(2)}) collective-permute-start(f32[16,1024]{1,0:T(8,128)S(1)} %get-tuple-element.41.a_ref), channel_id=1, source_target_pairs={{0,3},{1,0},{2,1},{3,2},{4,7},{5,4},{6,5},{7,6},{8,11},{9,8},{10,9... | collective-permute-start | bytes 196616 | tf_op jit(solution)/shard_map/ppermute | solution.py:631
  120.1 4.6 %collective-permute-start.9 = (f32[16,1024]{1,0:T(8,128)S(1)}, f32[16,1024]{1,0:T(8,128)S(1)}, u32[]{:S(2)}, u32[]{:S(2)}) collective-permute-start(f32[16,1024]{1,0:T(8,128)S(1)} %get-tuple-element.41.a_ref), channel_id=1, source_target_pairs={{0,2},{1,3},{2,0},{3,1},{4,6},{5,7},{6,4},{7,5},{8,10},{9,11},{10,... | collective-permute-start | bytes 196616 | tf_op jit(solution)/shard_map/ppermute | solution.py:631
  120.7 4.7 %collective-permute-start.8 = (f32[16,1024]{1,0:T(8,128)S(1)}, f32[16,1024]{1,0:T(8,128)S(1)}, u32[]{:S(2)}, u32[]{:S(2)}) collective-permute-start(f32[16,1024]{1,0:T(8,128)S(1)} %get-tuple-element.41.a_ref), channel_id=1, source_target_pairs={{0,1},{1,2},{2,3},{3,0},{4,5},{5,6},{6,7},{7,4},{8,9},{9,10},{10,1... | collective-permute-start | bytes 196616 | tf_op jit(solution)/shard_map/ppermute | solution.py:631
  137.3 6.1 %copy-start.10 = (bf16[16,16,1024]{2,1,0:T(8,128)(2,1)}, bf16[16,16,1024]{2,1,0:T(8,128)(2,1)S(1)}, u32[]{:S(2)}) copy-start(bf16[16,16,1024]{2,1,0:T(8,128)(2,1)S(1)} %all_to_all.16.own_ref) | copy-start | bytes 1572868
  137.3 6.1 %collective-permute-start.11 = (bf16[16,16,1024]{2,1,0:T(8,128)(2,1)S(1)}, bf16[16,16,1024]{2,1,0:T(8,128)(2,1)S(1)}, u32[]{:S(2)}, u32[]{:S(2)}) collective-permute-start(bf16[16,16,1024]{2,1,0:T(8,128)(2,1)S(1)} %all_to_all.16.own_ref), channel_id=1, source_target_pairs={{0,4},{4,0},{8,12},{12,8},{16,20},{20,16},{24,28},{28,24},{32,36},... | collective-permute-start | bytes 1572872 | tf_op jit(solution)/shard_map/ppermute | solution.py:625
  143.4 0.8 copy-start.11

commit v3 on v2

--- a/solution.py
+++ b/solution.py
@@ -172,25 +172,31 @@
         project(0, 0)
 
     following = jnp.minimum(step + 1, last)
-    hot = hot_ref[slot]
-    ones = jnp.ones((HSZ, points), BF)
-    for h in range(heads):
-        qx_ref[h, 144:160, :] = jnp.where(row16 == 0, -shift_ref[slot, h], 0.0).astype(BF)
-    per_head = -(-blocks // heads)
-    for h in range(heads + 1):
-        if h < heads:
-            pair = (h // 2) * 128
-            left = jnp.concatenate([k_ref[slot, :, pair : pair + 128], hot], axis=1)
-            p_ref[h % 2] = jnp.exp2(dot(left, qx_ref[h])).astype(BF)
-        if h > 0:
-            values_h = vt_ref[slot, (h - 1) * HSZ : h * HSZ, :]
-            values_h = jnp.concatenate([values_h, ones], axis=0)
-            part_ref[h - 1] = dot(values_h, p_ref[(h - 1) % 2])
-        for b in range(h * per_head, min((h + 1) * per_head, blocks)):
-            n_ref[b * MBLK : (b + 1) * MBLK, :] = embed_norm(
-                mod_ref, following * blocks, b, next_ref, table_ref, gain
-            )
-    project(following, 1 - slot)
+
+    def main(prepare):
+        hot = hot_ref[slot]
+        ones = jnp.ones((HSZ, points), BF)
+        for h in range(heads):
+            qx_ref[h, 144:160, :] = jnp.where(row16 == 0, -shift_ref[slot, h], 0.0).astype(BF)
+        per_head = -(-blocks // 2)
+        for h in range(heads + 1):
+            if h < heads:
+                pair = (h // 2) * 128
+                left = jnp.concatenate([k_ref[slot, :, pair : pair + 128], hot], axis=1)
+                p_ref[h % 2] = jnp.exp2(dot(left, qx_ref[h])).astype(BF)
+            if h > 0:
+                values_h = vt_ref[slot, (h - 1) * HSZ : h * HSZ, :]
+                values_h = jnp.concatenate([values_h, ones], axis=0)
+                part_ref[h - 1] = dot(values_h, p_ref[(h - 1) % 2])
+            for b in range(h * per_head, min((h + 1) * per_head, blocks) if prepare else 0):
+                n_ref[b * MBLK : (b + 1) * MBLK, :] = embed_norm(
+                    mod_ref, following * blocks, b, next_ref, table_ref, gain
+                )
+            if h == 2 and prepare:
+                project(following, 1 - slot)
+
+    pl.when(step < last)(functools.partial(main, True))
+    pl.when(step == last)(functools.partial(main, False))
     least = jnp.min(part_ref[:, HSZ : HSZ + 1, :])
 
     @pl.when(least < SMALL_TOTAL)
@@ -237,7 +243,7 @@
     heads = bias.shape[1]
     lat_count, lat_width = latents.shape
     cols = heads * HSZ
-    tile = math.gcd(points, 1024)
+    tile = math.gcd(points, 2048)
     steps = points // tile
     whole = lambda *shape: pl.BlockSpec(shape, lambda i, *_: (0,) * len(shape))
     return pl.pallas_call(
@@ -287,7 +293,7 @@
         in_specs=[pl.BlockSpec(memory_space=space(a)) for a in args],
         scratch_shapes=list(scratch),
         out_specs=jax.tree.map(lambda _: pl.BlockSpec(memory_space=pltpu.VMEM), outs),
-        compiler_params=pltpu.CompilerParams(vmem_limit_bytes=24 * MIB),
+        compiler_params=pltpu.CompilerParams(vmem_limit_bytes=14 * MIB),
         name=name,
     )(*args)
 
@@ -392,7 +398,6 @@
     bias_ref,
     wo_ref,
     qt_ref,
-    hot_ref,
     norm_ref,
     top_ref,
     bias_out,
@@ -409,10 +414,13 @@
     def _():
         wqt_ref[...] = wq_ref[...].T
         wot_ref[...] = wo_ref[...].T
-        lane = lax.broadcasted_iota(jnp.int32, (lat_count, 128), 1)
-        for h in range(heads):
-            columns = bias_rows(bias_ref[:, h, :] * LOG2E, 128).T
-            bias_out[h] = jnp.where(lane == 16 + h, 1.0, columns).astype(BF)
+        row = lax.broadcasted_iota(jnp.int32, (16, lat_count), 0)
+        for part in range(heads // 8):
+            block = []
+            for h in range(8 * part, 8 * part + 8):
+                rows = bias_rows(bias_ref[:, h, :] * LOG2E, 16)
+                block.append(jnp.where(row == 3 * MODS + part, 1.0, rows))
+            bias_out[part] = jnp.concatenate(block, axis=0).T.astype(BF)
         for m in range(MODS):
             top = jnp.max(bias_ref[m] * LOG2E, axis=1, keepdims=True)
             bmax_ref[m] = jnp.broadcast_to(top, (heads, MBLK))
@@ -422,8 +430,6 @@
             mod_ref, step * blocks, b, x_ref, table_ref, gain_ref[...]
         )
         mod = mod_ref[step * blocks + b]
-        hit, _ = modality_hot(mod, (16, MBLK), 0)
-        hot_ref[:, b * MBLK : (b + 1) * MBLK] = jnp.where(hit, 1.0, 0.0).astype(BF)
         top_ref[:, b * MBLK : (b + 1) * MBLK] = bmax_ref[mod]
     query = dot_nt(wqt_ref[...], n_ref[...]) * SCALE2
     qt_ref[...] = query.astype(BF)
@@ -454,10 +460,9 @@
             ],
             out_specs=[
                 tiled(cols),
-                tiled(16),
                 tiled(heads),
                 tiled(heads),
-                whole(heads, lat_count, 128),
+                whole(heads // 8, lat_count, 128),
                 whole(width, cols),
             ],
             scratch_shapes=[
@@ -468,10 +473,9 @@
         ),
         out_shape=[
             jax.ShapeDtypeStruct((cols, count), BF),
-            jax.ShapeDtypeStruct((16, count), BF),
             jax.ShapeDtypeStruct((heads, count), F32),
             jax.ShapeDtypeStruct((heads, count), F32),
-            jax.ShapeDtypeStruct((heads, lat_count, 128), BF),
+            jax.ShapeDtypeStruct((heads // 8, lat_count, 128), BF),
             jax.ShapeDtypeStruct((width, cols), BF),
         ],
         compiler_params=pltpu.CompilerParams(vmem_limit_bytes=58 * MIB),
@@ -490,7 +494,6 @@
     wkv_ref,
     bias_ref,
     qt_ref,
-    onehot_ref,
     norm_ref,
     top_ref,
     wot_ref,
@@ -513,28 +516,38 @@
         join_rows(core_ref[0], own_ref, other_ref, lat_ref)
         normed = lat_ref[...]
         ones = jnp.ones((HSZ, lat_count), BF)
-        lane = lax.broadcasted_iota(jnp.int32, (lat_count, 128), 1) // HSZ
-        sums = head_sums(2, 128)
-        for pair in range(heads // 2):
-            cols = slice(pair * 128, (pair + 1) * 128)
+        lane = lax.broadcasted_iota(jnp.int32, (lat_count, 128), 1)
+        sums = head_sums(4, 128)
+        for quad in range(heads // 4):
+            cols = slice(quad * 256, (quad + 1) * 256)
             keys = dot(normed, wkv_ref[0, :, cols])
             values = dot(normed, wkv_ref[1, :, cols]).astype(BF).T
             lengths = dot((keys * keys).astype(BF), sums)
             longest = jnp.sqrt(jnp.max(lengths, axis=0, keepdims=True))
-            for half in range(2):
-                h = 2 * pair + half
-                kx_ref[h, :, :128] = jnp.where(lane == half, keys, 0.0).astype(BF)
-                kx_ref[h, :, 128:] = bias_ref[h]
-                vx_ref[h, :HSZ, :] = values[half * HSZ : (half + 1) * HSZ, :]
+            for at in range(4):
+                h = 4 * quad + at
+                pair = keys[:, at // 2 * 128 : at // 2 * 128 + 128]
+                kx_ref[h, :, :128] = jnp.where(lane // HSZ == at % 2, pair, 0.0).astype(BF)
+                extra = jnp.where(lane // 16 == h % 8, bias_ref[h // 8].astype(F32), 0.0)
+                kx_ref[h, :, 128:] = extra.astype(BF)
+                vx_ref[h, :HSZ, :] = values[at * HSZ : (at + 1) * HSZ, :]
                 vx_ref[h, HSZ:, :] = ones
                 long_ref[h : h + 1, :] = jnp.broadcast_to(
-                    longest[:, half * HSZ : half * HSZ + 1], (1, 128)
+                    longest[:, at * 32 : at * 32 + 1], (1, 128)
                 )
-        hot_ref[...] = jnp.zeros(hot_ref.shape, BF)
 
     bound = norm_ref[...] * long_ref[:, :1] + top_ref[...]
-    hot_ref[:16, :] = onehot_ref[...]
-    hot_ref[16 : 16 + heads, :] = (-bound).astype(BF)
+    row = lax.broadcasted_iota(jnp.int32, (16, MBLK), 0)
+    for b in range(blocks):
+        hit, _ = modality_hot(mod_ref[step * blocks + b], (16, MBLK), 0)
+        onehot = jnp.where(hit, 1.0, 0.0)
+        lanes = slice(b * MBLK, (b + 1) * MBLK)
+        for group in range(8):
+            rows = onehot
+            for part in range(heads // 8):
+                own = bound[8 * part + group : 8 * part + group + 1, lanes]
+                rows = jnp.where(row == 3 * MODS + part, -own, rows)
+            hot_ref[16 * group : 16 * group + 16, lanes] = rows.astype(BF)
     hot = hot_ref[...]
     least = jnp.full((1, tile), 1.0, F32)
     for h in range(heads + 1):
@@ -549,7 +562,11 @@
 
     @pl.when(jnp.min(least) < SMALL_TOTAL)
     def _():
-        hot_ref[16 : 16 + heads, :] = jnp.zeros((heads, tile), BF)
+        for b in range(blocks):
+            hit, _ = modality_hot(mod_ref[step * blocks + b], (16, MBLK), 0)
+            onehot = jnp.where(hit, 1.0, 0.0).astype(BF)
+            for group in range(8):
+                hot_ref[16 * group : 16 * group + 16, b * MBLK : (b + 1) * MBLK] = onehot
 
         def exact(h, _):
             pair = pl.multiple_of((h // 2) * 128, 128)
@@ -572,13 +589,14 @@
 
 
 def decode(core, queries, query_modality, table, own, other, wkv, prepared):
-    queries_t, hot, norms, tops, bias, wo_t = prepared
+    queries_t, norms, tops, bias, wo_t = prepared
     count, width = queries.shape
-    heads, lat_count = bias.shape[:2]
-    cols = heads * HSZ
+    lat_count = bias.shape[1]
+    cols = queries_t.shape[0]
+    heads = cols // HSZ
     tile = math.gcd(count, 512)
     lat_width = wkv.shape[1]
-    whole = lambda a: pl.BlockSpec(a.shape, lambda i, *_: (0,) * a.ndim)
+    held = pl.BlockSpec(memory_space=pltpu.VMEM)
     tiled = lambda rows: pl.BlockSpec((rows, tile), lambda i, *_: (0, i))
     return pl.pallas_call(
         functools.partial(decode_kernel, heads),
@@ -587,16 +605,15 @@
             grid=(count // tile,),
             in_specs=[
                 pl.BlockSpec((tile, width), lambda i, *_: (i, 0)),
-                whole(table),
-                whole(own),
-                whole(other),
-                whole(wkv),
-                whole(bias),
+                held,
+                held,
+                held,
+                held,
+                held,
                 tiled(cols),
-                tiled(16),
                 tiled(heads),
                 tiled(heads),
-                whole(wo_t),
+                held,
             ],
             out_specs=pl.BlockSpec((tile, width), lambda i, *_: (i, 0)),
             scratch_shapes=[
@@ -610,9 +627,9 @@
             ],
         ),
         out_shape=jax.ShapeDtypeStruct((count, width), F32),
-        compiler_params=pltpu.CompilerParams(vmem_limit_bytes=58 * MIB),
+        compiler_params=pltpu.CompilerParams(vmem_limit_bytes=32 * MIB),
         name="decode",
-    )(query_modality, core, queries, table, own, other, wkv, bias, queries_t, hot, norms, tops, wo_t)
+    )(query_modality, core, queries, table, own, other, wkv, bias, queries_t, norms, tops, wo_t)
 
 
 def trade(parts):

time: 173 us -> 160 us (0.925)
  Pallas kernels: 102 us -> 87.3 us
  local copies, waits for them, and re-layouts: 2.61 us -> 4.88 us
    pallas_call x1, Pallas kernels: 60.4 us -> 52.1 us  [encode(): pl.pallas_call(functools.partial(encode_kernel, heads), grid_spec=pltpu.P...]
    pallas_call x1, Pallas kernels: 28 us -> 22.2 us  [decode(): pl.pallas_call(functools.partial(decode_kernel, heads), grid_spec=pltpu.P...]
    unnamed x24 -> x38, local copies, waits for them, and re-layouts: 1.77 us -> 4 us
  transfers between devices with their start and end apart: 13 -> 13, of which waited for: 11 -> 11; matrix products, arithmetic and copies ran while one was open for 0% -> 1% of each run, Pallas kernels for 5% -> 5%
where the time goes in v3:
time: 160 us
  Pallas kernels  87.3 us (55%)
  blocking collectives  25.9 us (16%)
  starting transfers between devices  24.8 us (16%)
  waiting for transfers between devices  16.6 us (10%)
  local copies, waits for them, and re-layouts  4.88 us (3%)
    pallas_call x1, Pallas kernels, encode(): pl.pallas_call(functools.partial(encode_kernel, heads), grid_spec=pltpu.P...  52.1 us
    all_to_all x2, blocking collectives, trade(): return lax.all_to_all(parts, 'inp', 0, 0, axis_index_groups=groups)  25.9 us
    pallas_call x1, Pallas kernels, decode(): pl.pallas_call(functools.partial(decode_kernel, heads), grid_spec=pltpu.P...  22.2 us
    ppermute x9, waiting for transfers between devices, head_parts(): lax.ppermute(part, 'head', [(i, (i + k) % size) for i in range(size)])  12.6 us
    ppermute x3, starting transfers between devices, other_core(): lax.ppermute(rows, 'inp', [(i, i ^ 1) for i in range(lax.axis_size('inp'))])  9.8 us
    pallas_call x1, Pallas kernels, prepare_queries(): pl.pallas_call(functools.partial(query_kernel, heads), grid_spec=pltpu.Pr...  7.92 us
    all_to_all x1, starting transfers between devices, trade(): return lax.all_to_all(parts, 'inp', 0, 0, axis_index_groups=groups)  7.79 us
    ppermute x9, starting transfers between devices, head_parts(): lax.ppermute(part, 'head', [(i, (i + k) % size) for i in range(size)])  7.16 us
  transfers between devices with their start and end apart: 13, of which 11 were waited for; matrix products, arithmetic and copies ran while one was open for 1% of the time, Pallas kernels for 5%

profile of v3, /device:TPU:1, one launch (start us, length us, event | category | flops | bytes accessed | tf_op | source)
XLA Modules:
  0.0 159.6 jit_solution(6219880126084454243)
XLA Ops:
  0.0 52.1 %encode.1 = (bf16[256,384]{1,0:T(8,128)(2,1)}, bf16[256,384]{1,0:T(8,128)(2,1)}) custom-call(s32[64]{0:T(128)} %mod_ref.3, s32[1]{0:T(128)} %bitcast.core_ref, bf16[8192,256]{1,0:T(8,128)(2,1)} %next_ref.1, bf16[8192,256]{1,0:T(8,128)(2,1)} %next_ref.1, f32[3,256]{1,0:T(4,128)} %table_ref.5, f32[1,256]{1,0:T(1,128)} %bitcast.12, f32[512,1024]{1,0:T(8,128)} %lat_ref.1, ...), custom_call_target="tpu_custom_call" | custom-call | tf_op jit(solution)/shard_map/encode/pallas_call | solution.py:249
  52.1 0.0 copy-start.7
  52.1 1.5 collective-permute-start
  53.6 1.3 collective-permute-done.b_ref
  54.9 0.9 copy-done.10
  55.8 1.5 pair.1
  57.3 7.8 %all-to-all-start = ((bf16[16,16,384]{2,1,0:T(8,128)(2,1)}), bf16[16,16,384]{2,1,0:T(8,128)(2,1)S(1)}, u32[]{:S(2)}, u32[]{:S(2)}) async-start(bf16[16,16,384]{2,1,0:T(8,128)(2,1)} %bitcast.3), calls=%async_computation | async-start | bytes 393216 | tf_op jit(solution)/shard_map/all_to_all | solution.py:638
  65.1 0.0 copy-start.3
  65.1 7.9 %queries.1 = (bf16[1024,2048]{1,0:T(8,128)(2,1)}, f32[16,2048]{1,0:T(8,128)}, f32[16,2048]{1,0:T(8,128)}, bf16[2,512,128]{2,1,0:T(8,128)(2,1)}, bf16[256,1024]{1,0:T(8,128)(2,1)}) custom-call(s32[16]{0:T(128)} %mod_ref.5, bf16[2048,256]{1,0:T(8,128)(2,1)} %x_ref.4, f32[3,256]{1,0:T(4,128)} %table_ref.5, f32[1,256]{1,0:T(1,128)} %bitcast.13, ...), custom_call_target="tpu_custom_call" | custom-call | tf_op jit(solution)/shard_map/queries/pallas_call | solution.py:448
  73.0 0.0 all-to-all-done.part_ref
  73.0 0.0 copy-done.7
  73.0 0.0 copy-start.16
  73.1 0.0 copy-start.17
  73.1 0.0 copy-start.9
  73.1 0.5 merge.1.a_ref
  73.6 2.7 %collective-permute-start.3 = (f32[16,1024]{1,0:T(8,128)S(1)}, f32[16,1024]{1,0:T(8,128)S(1)}, u32[]{:S(2)}, u32[]{:S(2)}) collective-permute-start(f32[16,1024]{1,0:T(8,128)S(1)} %merge.1.a_ref), channel_id=1, source_target_pairs={{0,3},{1,0},{2,1},{3,2},{4,7},{5,4},{6,5},{7,6},{8,11},{9,8},{10,9... | collective-permute-start | bytes 196616 | tf_op jit(solution)/shard_map/ppermute | solution.py:648
  76.3 0.4 collective-permute-start.2
  76.7 0.7 collective-permute-start.1
  77.4 0.9 constant_dynamic-slice_fusion.lat_ref
  78.3 0.0 collective-permute-done.3.d_ref
  78.3 2.8 %collective-permute-done.2.c_ref = f32[16,1024]{1,0:T(8,128)S(1)} collective-permute-done((f32[16,1024]{1,0:T(8,128)S(1)}, f32[16,1024]{1,0:T(8,128)S(1)}, u32[]{:S(2)}, u32[]{:S(2)}) %collective-permute-start.2) | collective-permute-done | bytes 65568 | tf_op jit(solution)/shard_map/ppermute | solution.py:648
  81.0 0.6 collective-permute-done.1.b_ref
  81.7 0.0 copy-done.15
  81.7 1.4 copy-done.5
  83.1 0.5 project.1
  83.6 14.2 %all_to_all.15.own_ref = bf16[16,16,512]{2,1,0:T(8,128)(2,1)S(1)} all-to-all(bf16[16,16,512]{2,1,0:T(8,128)(2,1)S(1)} %get-tuple-element.36), channel_id=1, replica_groups={{0,8,16,24,32,40,48,56,64,72,80,88,96,104,112,120},{4,12,20,28,36,44,52..., dimensions={0} | all-to-all | bytes 524288 | tf_op jit(solution)/shard_map/all_to_all | solution.py:638
  97.8 3.7 %collective-permute-start.4 = (bf16[16,16,512]{2,1,0:T(8,128)(2,1)S(1)}, bf16[16,16,512]{2,1,0:T(8,128)(2,1)S(1)}, u32[]{:S(2)}, u32[]{:S(2)}) collective-permute-start(bf16[16,16,512]{2,1,0:T(8,128)(2,1)S(1)} %all_to_all.15.own_ref), channel_id=1, source_target_pairs={{0,4},{4,0},{8,12},{12,8},{16,20},{20,16},{24,28},{28,24},{32,36},... | collective-permute-start | bytes 786440 | tf_op jit(solution)/shard_map/ppermute | solution.py:642
  101.5 1.2 collective-permute-done.4.other_ref
  102.7 0.0 copy-done.13
  102.7 0.0 copy-done.8
  102.7 1.5 attend.1.a_ref
  104.2 0.3 collective-permute-start.7
  104.5 0.8 collective-permute-start.6
  105.3 0.8 collective-permute-start.5
  106.1 1.2 collective-permute-done.7.d_ref
  107.3 1.8 %collective-permute-done.6.c_ref = f32[16,1024]{1,0:T(8,128)S(1)} collective-permute-done((f32[16,1024]{1,0:T(8,128)S(1)}, f32[16,1024]{1,0:T(8,128)S(1)}, u32[]{:S(2)}, u32[]{:S(2)}) %collective-permute-start.6) | collective-permute-done | bytes 65568 | tf_op jit(solution)/shard_map/ppermute | solution.py:648
  109.1 1.9 %collective-permute-done.5.b_ref = f32[16,1024]{1,0:T(8,128)S(1)} collective-permute-done((f32[16,1024]{1,0:T(8,128)S(1)}, f32[16,1024]{1,0:T(8,128)S(1)}, u32[]{:S(2)}, u32[]{:S(2)}) %collective-permute-start.5) | collective-permute-done | bytes 65568 | tf_op jit(solution)/shard_map/ppermute | solution.py:648
  111.0 0.0 copy-done.3
  111.0 0.0 copy-done.16
  111.0 1.6 copy-done.4
  112.6 0.0 copy-start.14
  112.7 0.0 copy-start.18
  112.7 0.9 mlp.1
  113.5 0.5 collective-permute-start.10
  114.0 0.6 collective-permute-start.9
  114.6 0.4 collective-permute-start.8
  115.0 1.6 %collective-permute-done.10.d_ref = f32[16,1024]{1,0:T(8,128)S(1)} collective-permute-done((f32[16,1024]{1,0:T(8,128)S(1)}, f32[16,1024]{1,0:T(8,128)S(1)}, u32[]{:S(2)}, u32[]{:S(2)}) %collective-permute-start.10) | collective-permute-done | bytes 65568 | tf_op jit(solution)/shard_map/ppermute | solution.py:648
  116.6 2.0 %collective-permute-done.9.c_ref = f32[16,1024]{1,0:T(8,128)S(1)} collective-permute-done((f32[16,1024]{1,0:T(8,128)S(1)}, f32[16,1024]{1,0:T(8,128)S(1)}, u32[]{:S(2)}, u32[]{:S(2)}) %collective-permute-start.9) | collective-permute-done | bytes 65568 | tf_op jit(solution)/shard_map/ppermute | solution.py:648
  118.6 0.7 collective-permute-done.8.b_ref
  119.3 0.0 copy-done.17
  119.3 0.2 last.1
  119.5 11.6 %all_to_all.16.own_ref = bf16[16,16,1024]{2,1,0:T(8,128)(2,1)S(1)} all-to-all(bf16[16,16,1024]{2,1,0:T(8,128)(2,1)S(1)} %last.1), channel_id=1, replica_groups={{0,8,16,24,32,40,48,56,64,72,80,88,96,104,112,120},{4,12,20,28,36,44,52..., dimensions={0} | all-to-all | bytes 1048576 | tf_op jit(solution)/shard_map/all_to_all | solution.py:638
  131.2 4.6 %collective-permute-start.11 = (bf16[16,16,1024]{2,1,0:T(8,128)(2,1)S(1)}, bf16[16,16,1024]{2,1,0:T(8,128)(2,1)S(1)}, u32[]{:S(2)}, u32[]{:S(2)}) collective-permute-start(bf16[16,16,1024]{2,1,0:T(8,128)(2,1)S(1)} %all_to_all.16.own_ref), channel_id=1, source_target_pairs={{0,4},{4,0},{8,12},{12,8},{16,20},{20,16},{24,28},{28,24},{32,36},... | collective-permute-start | bytes 1572872 | tf_op jit(solution)/shard_map/ppermute | solution.py:642
  135.8 1.5 collective-permute-done.11.other_ref
  137.3 0.0 copy-done.9
  137.3 0.0 copy-done.12
  137.3 0.0 copy-done.2
  137.3 0.0 copy-done
  137.3 0.0 copy-done.1
  137.3 0.0 copy-done.6
  137.3 0.0 copy-done.11
  137.4 0.0 copy-done.14
  137.4 0.0 copy-done.18
  137.4 22.2 %decode.1 = f32[2048,256]{1,0:T(8,128)} custom-call(s32[16]{0:T(128)S(1)} %copy-done.18, s32[1]{0:T(128)} %bitcast.core_ref, bf16[2048,256]{1,0:T(8,128)(2,1)S(1)} %copy-done, f32[3,256]{1,0:T(4,128)S(1)} %copy-done.14, bf16[16,16,1024]{2,1,0:T(8,128)(2,1)S(1)} %all_to_all.16.own_ref, bf16[16,16,1024]{2,1,0:T(8,128)(2,1)S(1)} %collective-permute-done.11.other_ref, ...), custom_call_target="tpu_custom_call" | custom-call | tf_op jit(solution)/shard_map/decode/pallas_call | solution.py:601
  (12 shorter events, 0.0 us)
Async XLA Ops:
  0.0 81.7 %copy-start.15 = (f32[1024]{0:T(1024)S(1)}, f32[1024]{0:T(1024)}, u32[]{:S(2)}) copy-start(f32[1024]{0:T(1024)} %param.37) | copy-start | bytes 12292
  52.1 21.0 %copy-start.7 = (bf16[256,1024]{1,0:T(8,128)(2,1)S(1)}, bf16[256,1024]{1,0:T(8,128)(2,1)}, u32[]{:S(2)}) copy-start(bf16[256,1024]{1,0:T(8,128)(2,1)} %wo_ref.4) | copy-start | bytes 1572868
  52.1 2.8 %collective-permute-start = (bf16[256,384]{1,0:T(8,128)(2,1)}, bf16[256,384]{1,0:T(8,128)(2,1)S(1)}, u32[]{:S(2)}, u32[]{:S(2)}) collective-permute-start(bf16[256,384]{1,0:T(8,128)(2,1)} %get-tuple-element.26), channel_id=1, source_target_pairs={{0,4},{4,0},{8,12},{12,8},{16,20},{20,16},{24,28},{28,24},{32,36},... | collective-permute-start | bytes 589832 | tf_op jit(solution)/shard_map/ppermute | solution.py:642
  54.9 0.9 copy-start.10
  57.3 45.4 %copy-start.13 = (f32[4,16,512]{2,1,0:T(8,128)S(1)}, f32[4,16,512]{2,1,0:T(8,128)}, u32[]{:S(2)}) copy-start(f32[4,16,512]{2,1,0:T(8,128)} %bias_ref.5) | copy-start | bytes 393220
  57.3 15.7 %all-to-all-start = ((bf16[16,16,384]{2,1,0:T(8,128)(2,1)}), bf16[16,16,384]{2,1,0:T(8,128)(2,1)S(1)}, u32[]{:S(2)}, u32[]{:S(2)}) async-start(bf16[16,16,384]{2,1,0:T(8,128)(2,1)} %bitcast.3), calls=%async_computation | async-start | bytes 393216 | tf_op jit(solution)/shard_map/all_to_all | solution.py:638
  65.1 46.0 %copy-start.3 = (bf16[1024,1024]{1,0:T(8,128)(2,1)S(1)}, bf16[1024,1024]{1,0:T(8,128)(2,1)}, u32[]{:S(2)}) copy-start(bf16[1024,1024]{1,0:T(8,128)(2,1)} %w1_ref.1) | copy-start | bytes 6291460
  73.0 29.7 %copy-start.8 = (bf16[256,1024]{1,0:T(8,128)(2,1)S(1)}, bf16[256,1024]{1,0:T(8,128)(2,1)}, u32[]{:S(2)}) copy-start(bf16[256,1024]{1,0:T(8,128)(2,1)} %wo_ref.5) | copy-start | bytes 1572868
  73.0 38.0 %copy-start.16 = (f32[1024]{0:T(1024)S(1)}, f32[1024]{0:T(1024)}, u32[]{:S(2)}) copy-start(f32[1024]{0:T(1024)} %param.41) | copy-start | bytes 12292
  73.1 46.3 %copy-start.17 = (f32[1024]{0:T(1024)S(1)}, f32[1024]{0:T(1024)}, u32[]{:S(2)}) copy-start(f32[1024]{0:T(1024)} %param.44) | copy-start | bytes 12292
  73.1 64.2 %copy-start.9 = (bf16[2,512,128]{2,1,0:T(8,128)(2,1)S(1)}, bf16[2,512,128]{2,1,0:T(8,128)(2,1)}, u32[]{:S(2)}) copy-start(bf16[2,512,128]{2,1,0:T(8,128)(2,1)} %get-tuple-element.40.bias_ref) | copy-start | bytes 786436
  73.6 4.7 %collective-permute-start.3 = (f32[16,1024]{1,0:T(8,128)S(1)}, f32[16,1024]{1,0:T(8,128)S(1)}, u32[]{:S(2)}, u32[]{:S(2)}) collective-permute-start(f32[16,1024]{1,0:T(8,128)S(1)} %merge.1.a_ref), channel_id=1, source_target_pairs={{0,3},{1,0},{2,1},{3,2},{4,7},{5,4},{6,5},{7,6},{8,11},{9,8},{10,9... | collective-permute-start | bytes 196616 | tf_op jit(solution)/shard_map/ppermute | solution.py:648
  76.3 4.7 %collective-permute-start.2 = (f32[16,1024]{1,0:T(8,128)S(1)}, f32[16,1024]{1,0:T(8,128)S(1)}, u32[]{:S(2)}, u32[]{:S(2)}) collective-permute-start(f32[16,1024]{1,0:T(8,128)S(1)} %merge.1.a_ref), channel_id=1, source_target_pairs={{0,2},{1,3},{2,0},{3,1},{4,6},{5,7},{6,4},{7,5},{8,10},{9,11},{10,... | collective-permute-start | bytes 196616 | tf_op jit(solution)/shard_map/ppermute | solution.py:648
  76.7 4.9 %collective-permute-start.1 = (f32[16,1024]{1,0:T(8,128)S(1)}, f32[16,1024]{1,0:T(8,128)S(1)}, u32[]{:S(2)}, u32[]{:S(2)}) collective-permute-start(f32[16,1024]{1,0:T(8,128)S(1)} %merge.1.a_ref), channel_id=1, source_target_pairs={{0,1},{1,2},{2,3},{3,0},{4,5},{5,6},{6,7},{7,4},{8,9},{9,10},{10,1... | collective-permute-start | bytes 196616 | tf_op jit(solution)/shard_map/ppermute | solution.py:648
  77.4 59.9 %copy-start.12 = (f32[16,2048]{1,0:T(8,128)S(1)}, f32[16,2048]{1,0:T(8,128)}, u32[]{:S(2)}) copy-start(f32[16,2048]{1,0:T(8,128)} %get-tuple-element.43.top_ref) | copy-start | bytes 393220
  81.7 1.4 copy-start.5
  83.1 54.2 %copy-start.2 = (bf16[1024,2048]{1,0:T(8,128)(2,1)S(1)}, bf16[1024,2048]{1,0:T(8,128)(2,1)}, u32[]{:S(2)}) copy-start(bf16[1024,2048]{1,0:T(8,128)(2,1)} %get-tuple-element.41.qt_ref) | copy-start | bytes 12582916
  97.8 4.8 %collective-permute-start.4 = (bf16[16,16,512]{2,1,0:T(8,128)(2,1)S(1)}, bf16[16,16,512]{2,1,0:T(8,128)(2,1)S(1)}, u32[]{:S(2)}, u32[]{:S(2)}) collective-permute-start(bf16[16,16,512]{2,1,0:T(8,128)(2,1)S(1)} %all_to_all.15.own_ref), channel_id=1, source_target_pairs={{0,4},{4,0},{8,12},{12,8},{16,20},{20,16},{24,28},{28,24},{32,36},... | collective-permute-start | bytes 786440 | tf_op jit(solution)/shard_map/ppermute | solution.py:642
  104.2 3.1 %collective-permute-start.7 = (f32[16,1024]{1,0:T(8,128)S(1)}, f32[16,1024]{1,0:T(8,128)S(1)}, u32[]{:S(2)}, u32[]{:S(2)}) collective-permute-start(f32[16,1024]{1,0:T(8,128)S(1)} %attend.1.a_ref), channel_id=1, source_target_pairs={{0,3},{1,0},{2,1},{3,2},{4,7},{5,4},{6,5},{7,6},{8,11},{9,8},{10,9... | collective-permute-start | bytes 196616 | tf_op jit(solution)/shard_map/ppermute | solution.py:648
  104.5 4.6 %collective-permute-start.6 = (f32[16,1024]{1,0:T(8,128)S(1)}, f32[16,1024]{1,0:T(8,128)S(1)}, u32[]{:S(2)}, u32[]{:S(2)}) collective-permute-start(f32[16,1024]{1,0:T(8,128)S(1)} %attend.1.a_ref), channel_id=1, source_target_pairs={{0,2},{1,3},{2,0},{3,1},{4,6},{5,7},{6,4},{7,5},{8,10},{9,11},{10,... | collective-permute-start | bytes 196616 | tf_op jit(solution)/shard_map/ppermute | solution.py:648
  105.3 5.7 %collective-permute-start.5 = (f32[16,1024]{1,0:T(8,128)S(1)}, f32[16,1024]{1,0:T(8,128)S(1)}, u32[]{:S(2)}, u32[]{:S(2)}) collective-permute-start(f32[16,1024]{1,0:T(8,128)S(1)} %attend.1.a_ref), channel_id=1, source_target_pairs={{0,1},{1,2},{2,3},{3,0},{4,5},{5,6},{6,7},{7,4},{8,9},{9,10},{10,1... | collective-permute-start | bytes 196616 | tf_op jit(solution)/shard_map/ppermute | solution.py:648
  111.0 1.6 copy-start.4
  112.6 24.7 %copy-start = (bf16[2048,256]{1,0:T(8,128)(2,1)S(1)}, bf16[2048,256]{1,0:T(8,128)(2,1)}, u32[]{:S(2)}) copy-start(bf16[2048,256]{1,0:T(8,128)(2,1)} %x_ref.4) | copy-start | bytes 3145732
  112.6 24.7 %copy-start.1 = (bf16[2,1024,1024]{2,1,0:T(8,128)(2,1)S(1)}, bf16[2,1024,1024]{2,1,0:T(8,128)(2,1)}, u32[]{:S(2)}) copy-start(bf16[2,1024,1024]{2,1,0:T(8,128)(2,1)} %wkv_ref.3) | copy-start | bytes 12582916
  112.6 24.7 %copy-start.6 = (bf16[256,1024]{1,0:T(8,128)(2,1)S(1)}, bf16[256,1024]{1,0:T(8,128)(2,1)}, u32[]{:S(2)}) copy-start(bf16[256,1024]{1,0:T(8,128)(2,1)} %get-tuple-element.44.wot_ref) | copy-start | bytes 1572868
  112.6 24.7 %copy-start.11 = (f32[16,2048]{1,0:T(8,128)S(1)}, f32[16,2048]{1,0:T(8,128)}, u32[]{:S(2)}) copy-start(f32[16,2048]{1,0:T(8,128)} %get-tuple-element.42.norm_ref) | copy-start | bytes 393220
  112.6 24.7 %copy-start.14 = (f32[3,256]{1,0:T(4,128)S(1)}, f32[3,256]{1,0:T(4,128)}, u32[]{:S(2)}) copy-start(f32[3,256]{1,0:T(4,128)} %table_ref.5) | copy-start | bytes 9220
  112.7 24.7 %copy-start.18 = (s32[16]{0:T(128)S(1)}, s32[16]{0:T(128)}, u32[]{:S(2)}) copy-start(s32[16]{0:T(128)} %mod_ref.5) | copy-start | bytes 196
  113.5 3.1 %collective-permute-start.10 = (f32[16,1024]{1,0:T(8,128)S(1)}, f32[16,1024]{1,0:T(8,128)S(1)}, u32[]{:S(2)}, u32[]{:S(2)}) collective-permute-start(f32[16,1024]{1,0:T(8,128)S(1)} %get-tuple-element.38.a_ref), channel_id=1, source_target_pairs={{0,3},{1,0},{2,1},{3,2},{4,7},{5,4},{6,5},{7,6},{8,11},{9,8},{10,9... | collective-permute-start | bytes 196616 | tf_op jit(solution)/shard_map/ppermute | solution.py:648
  114.0 4.6 %collective-permute-start.9 = (f32[16,1024]{1,0:T(8,128)S(1)}, f32[16,1024]{1,0:T(8,128)S(1)}, u32[]{:S(2)}, u32[]{:S(2)}) collective-permute-start(f32[16,1024]{1,0:T(8,128)S(1)} %get-tuple-element.38.a_ref), channel_id=1, source_target_pairs={{0,2},{1,3},{2,0},{3,1},{4,6},{5,7},{6,4},{7,5},{8,10},{9,11},{10,... | collective-permute-start | bytes 196616 | tf_op jit(solution)/shard_map/ppermute | solution.py:648
  114.6 4.7 %collective-permute-start.8 = (f32[16,1024]{1,0:T(8,128)S(1)}, f32[16,1024]{1,0:T(8,128)S(1)}, u32[]{:S(2)}, u32[]{:S(2)}) collective-permute-start(f32[16,1024]{1,0:T(8,128)S(1)} %get-tuple-element.38.a_ref), channel_id=1, source_target_pairs={{0,1},{1,2},{2,3},{3,0},{4,5},{5,6},{6,7},{7,4},{8,9},{9,10},{10,1... | collective-permute-start | bytes 196616 | tf_op jit(solution)/shard_map/ppermute | solution.py:648
  131.2 6.1 %collective-permute-start.11 = (bf16[16,16,1024]{2,1,0:T(8,128)(2,1)S(1)}, bf16[16,16,1024]{2,1,0:T(8,128)(2,1)S(1)}, u32[]{:S(2)}, u32[]{:S(2)}) collective-permute-start(bf16[16,16,1024]{2,1,0:T(8,128)(2,1)S(1)} %all_to_all.16.own_ref), channel_id=1, source_target_pairs={{0,4},{4,0},{8,12},{12,8},{16,20},{20,16},{24,28},{28,24},{32,36},... | collective-permute-start | bytes 1572872 | tf_op jit(solution)/shard_map/ppermute | solution.py:642

commit v4 on v3

--- a/solution.py
+++ b/solution.py
@@ -71,16 +71,6 @@
     return layer_norm(embedded, gain).astype(BF)
 
 
-def part_rows(core, all_ref, own_ref, other_ref):
-    for held, refs in enumerate(((own_ref, other_ref), (other_ref, own_ref))):
-
-        @pl.when(core == held)
-        def _():
-            for block in range(all_ref.shape[0] // 16):
-                rows = slice(block // 2 * 16, block // 2 * 16 + 16)
-                refs[block % 2][rows, :] = all_ref[block * 16 : block * 16 + 16, :]
-
-
 def join_rows(core, own_ref, other_ref, all_ref):
     for held, refs in enumerate(((own_ref, other_ref), (other_ref, own_ref))):
 
@@ -93,7 +83,6 @@
 def encode_kernel(
     heads,
     mod_ref,
-    core_ref,
     x_ref,
     next_ref,
     table_ref,
@@ -103,8 +92,7 @@
     wq_ref,
     wkv_ref,
     bias_ref,
-    keep_ref,
-    send_ref,
+    out_ref,
     qx_ref,
     norm_ref,
     wvt_ref,
@@ -117,7 +105,6 @@
     shift_ref,
     m_ref,
     acc_ref,
-    out_ref,
 ):
     step = pl.program_id(0)
     last = pl.num_programs(0) - 1
@@ -235,10 +222,9 @@
             for part, piece in enumerate(three_parts(m_ref[h] + jnp.log2(total))):
                 extra = jnp.where(index == heads * part + h, piece, extra)
         out_ref[...] = jnp.concatenate(pieces + [extra], axis=0).T.astype(BF)
-        part_rows(core_ref[0], out_ref, keep_ref, send_ref)
-
-
-def encode(core, inputs, input_modality, table, gain, latents, lat_gain, wq, wkv, bias):
+
+
+def encode(inputs, input_modality, table, gain, latents, lat_gain, wq, wkv, bias):
     points, width = inputs.shape
     heads = bias.shape[1]
     lat_count, lat_width = latents.shape
@@ -249,7 +235,7 @@
     return pl.pallas_call(
         functools.partial(encode_kernel, heads),
         grid_spec=pltpu.PrefetchScalarGridSpec(
-            num_scalar_prefetch=2,
+            num_scalar_prefetch=1,
             grid=(steps,),
             in_specs=[
                 pl.BlockSpec((tile, width), lambda i, *_: (0, 0)),
@@ -262,7 +248,7 @@
                 whole(2, width, cols),
                 whole(MODS, heads, lat_count),
             ],
-            out_specs=[whole(lat_count // 2, cols + EXTRA)] * 2,
+            out_specs=whole(lat_count, cols + EXTRA),
             scratch_shapes=[
                 pltpu.VMEM((heads, 256, lat_count), BF),
                 pltpu.VMEM((heads, lat_count), F32),
@@ -276,17 +262,30 @@
                 pltpu.VMEM((2, heads, 1, lat_count), F32),
                 pltpu.VMEM((heads, 1, lat_count), F32),
                 pltpu.VMEM((heads, 128, lat_count), F32),
-                pltpu.VMEM((lat_count, cols + EXTRA), BF),
             ],
         ),
-        out_shape=[jax.ShapeDtypeStruct((lat_count // 2, cols + EXTRA), BF)] * 2,
+        out_shape=jax.ShapeDtypeStruct((lat_count, cols + EXTRA), BF),
         compiler_params=pltpu.CompilerParams(vmem_limit_bytes=58 * MIB),
+        cost_estimate=pl.CostEstimate(
+            flops=2 * points * lat_count * heads * (256 + 128),
+            transcendentals=points * lat_count * heads,
+            bytes_accessed=2 * inputs.nbytes + latents.nbytes + wq.nbytes + wkv.nbytes,
+        ),
         name="encode",
-    )(input_modality, core, inputs, inputs, table, gain, latents, lat_gain, wq, wkv, bias)
-
-
-def small_call(kernel, name, outs, *args, scratch=()):
-    space = lambda a: pltpu.SMEM if a.dtype == jnp.int32 else pltpu.VMEM
+    )(input_modality, inputs, inputs, table, gain, latents, lat_gain, wq, wkv, bias)
+
+
+def small_call(kernel, name, outs, *args, scratch=(), streamed=None):
+    def space(a):
+        if a is streamed:
+            return pltpu.HBM
+        return pltpu.SMEM if a.dtype == jnp.int32 else pltpu.VMEM
+
+    if streamed is not None:
+        scratch = (pltpu.VMEM(streamed.shape, streamed.dtype), pltpu.SemaphoreType.DMA(()))
+        far = pltpu.with_memory_space_constraint(streamed, pltpu.HBM)
+        args = [far if a is streamed else a for a in args]
+        streamed = far
     return pl.pallas_call(
         kernel,
         out_shape=outs,
@@ -313,25 +312,6 @@
     return spread
 
 
-def pair_kernel(heads, a_ref, b_ref, out_ref):
-    cols = heads * HSZ
-    rows = a_ref.shape[0]
-    first = log_totals(heads, a_ref[:, cols:].astype(F32))
-    second = log_totals(heads, b_ref[:, cols:].astype(F32))
-    top = jnp.maximum(first, second)
-    first, second = jnp.exp2(first - top), jnp.exp2(second - top)
-    total = first + second
-    joint = a_ref[:, :cols].astype(F32) * per_head(heads, first / total, (rows, cols))
-    joint = joint + b_ref[:, :cols].astype(F32) * per_head(heads, second / total, (rows, cols))
-    out_ref[:, :cols] = joint.astype(BF)
-    lane = lax.broadcasted_iota(jnp.int32, (rows, EXTRA), 1)
-    extra = jnp.zeros((rows, EXTRA), F32)
-    for part, piece in enumerate(three_parts(top + jnp.log2(total))):
-        for h in range(heads):
-            extra = jnp.where(lane == heads * part + h, piece[:, h : h + 1], extra)
-    out_ref[:, cols:] = extra.astype(BF)
-
-
 def merge_kernel(heads, part_ref, wo_ref, out_ref):
     cols = heads * HSZ
     lse = log_totals(heads, part_ref[:, :, cols:].astype(F32))
@@ -339,14 +319,24 @@
     factor = factor / jnp.sum(factor, axis=0, keepdims=True)
     spread = per_head(heads, factor, part_ref.shape[:2] + (cols,))
     attended = jnp.sum(part_ref[:, :, :cols].astype(F32) * spread, axis=0)
-    out_ref[...] = dot(attended.astype(BF), wo_ref[...])
-
-
-def project_kernel(a_ref, b_ref, c_ref, d_ref, lat_ref, gain_ref, w_ref, lat_out, q_out, kv_out):
-    lat = lat_ref[...] + ((a_ref[...] + b_ref[...]) + (c_ref[...] + d_ref[...]))
+    out_ref[...] = dot(attended.astype(BF), wo_ref[...]).astype(BF)
+
+
+def added(*refs):
+    a, b, c, d = [ref[...].astype(F32) for ref in refs]
+    return (a + b) + (c + d)
+
+
+def project_kernel(
+    a_ref, b_ref, c_ref, d_ref, lat_ref, gain_ref, far_ref, lat_out, q_out, kv_out, w_ref, sem
+):
+    copy = pltpu.make_async_copy(far_ref, w_ref, sem)
+    copy.start()
+    lat = lat_ref[...] + added(a_ref, b_ref, c_ref, d_ref)
     lat_out[...] = lat
     normed = layer_norm(lat, gain_ref[...]).astype(BF)
     cols = w_ref.shape[2]
+    copy.wait()
     q_out[...] = (dot(normed, w_ref[0]) * SCALE2).astype(BF)
     keys = dot(normed, w_ref[1]).astype(BF)
     values = dot(normed, w_ref[2]).astype(BF)
@@ -370,19 +360,24 @@
         weights = jnp.exp2(scores - jnp.max(scores, axis=1, keepdims=True))
         total = jnp.sum(weights, axis=1, keepdims=True)
         mixed = jnp.where(lane == h, dot(weights.astype(BF), values) / total, mixed)
-    out_ref[...] = dot(mixed.astype(BF), wo_ref[...])
-
-
-def mlp_kernel(a_ref, b_ref, c_ref, d_ref, lat_ref, gain_ref, w1_ref, w2_ref, lat_out, out_ref):
-    lat = lat_ref[...] + ((a_ref[...] + b_ref[...]) + (c_ref[...] + d_ref[...]))
+    out_ref[...] = dot(mixed.astype(BF), wo_ref[...]).astype(BF)
+
+
+def mlp_kernel(
+    a_ref, b_ref, c_ref, d_ref, lat_ref, gain_ref, w1_ref, far_ref, lat_out, out_ref, w2_ref, sem
+):
+    copy = pltpu.make_async_copy(far_ref, w2_ref, sem)
+    copy.start()
+    lat = lat_ref[...] + added(a_ref, b_ref, c_ref, d_ref)
     lat_out[...] = lat
     normed = layer_norm(lat, gain_ref[...]).astype(BF)
     hidden = jax.nn.gelu(dot(normed, w1_ref[...]), approximate=True).astype(BF)
-    out_ref[...] = dot(hidden, w2_ref[...])
+    copy.wait()
+    out_ref[...] = dot(hidden, w2_ref[...]).astype(BF)
 
 
 def last_kernel(a_ref, b_ref, c_ref, d_ref, lat_ref, gain_ref, out_ref):
-    lat = lat_ref[...] + ((a_ref[...] + b_ref[...]) + (c_ref[...] + d_ref[...]))
+    lat = lat_ref[...] + added(a_ref, b_ref, c_ref, d_ref)
     normed = layer_norm(lat, gain_ref[...]).astype(BF)
     for copy in range(out_ref.shape[0]):
         out_ref[copy] = normed
@@ -479,6 +474,11 @@
             jax.ShapeDtypeStruct((width, cols), BF),
         ],
         compiler_params=pltpu.CompilerParams(vmem_limit_bytes=58 * MIB),
+        cost_estimate=pl.CostEstimate(
+            flops=2 * count * width * cols,
+            transcendentals=count * heads,
+            bytes_accessed=queries.nbytes + wq.nbytes + wo.nbytes + 2 * count * cols,
+        ),
         name="queries",
     )(query_modality, queries, table, gain, wq, bias, wo)
 
@@ -628,6 +628,11 @@
         ),
         out_shape=jax.ShapeDtypeStruct((count, width), F32),
         compiler_params=pltpu.CompilerParams(vmem_limit_bytes=32 * MIB),
+        cost_estimate=pl.CostEstimate(
+            flops=2 * count * lat_count * heads * (256 + 128) + 2 * count * width * cols,
+            transcendentals=count * lat_count * heads,
+            bytes_accessed=queries.nbytes + wkv.nbytes + queries_t.nbytes + 4 * queries.size,
+        ),
         name="decode",
     )(query_modality, core, queries, table, own, other, wkv, bias, queries_t, norms, tops, wo_t)
 
@@ -688,8 +693,7 @@
 
     core = (lax.axis_index("inp") % 2).astype(jnp.int32).reshape(1)
     chips = lax.axis_size("inp") // 2
-    keep, send = encode(
-        core,
+    partial = encode(
         inputs,
         input_modality,
         modality_embed,
@@ -700,21 +704,14 @@
         enc_wkv,
         enc_bias,
     )
-    joint = small_call(
-        functools.partial(pair_kernel, heads),
-        "pair",
-        shape(keep.shape, BF),
-        keep,
-        other_core(send),
-    )
-    joint, early = lax.optimization_barrier((joint, queries))
-    parts = trade(joint.reshape(chips, lat_rows, joint.shape[1]))
+    partial, early = lax.optimization_barrier((partial, queries))
+    parts = lax.all_to_all(partial.reshape(-1, lat_rows, partial.shape[1]), "inp", 0, 0)
     prepared = prepare_queries(
         early, query_modality, modality_embed, row(query_gain), dec_wq, dec_bias, dec_wo
     )
     parts, prepared = lax.optimization_barrier((parts, prepared))
     enc_part = small_call(
-        functools.partial(merge_kernel, heads), "merge", shape((lat_rows, width), F32), parts, enc_wo
+        functools.partial(merge_kernel, heads), "merge", shape((lat_rows, width), BF), parts, enc_wo
     )
     latent_rows = lax.dynamic_slice_in_dim(latents, row_first, lat_rows, 0)
     lat_one, self_q, self_kv = small_call(
@@ -729,12 +726,13 @@
         latent_rows,
         row(self_gain),
         self_wqkv,
+        streamed=self_wqkv,
     )
     own_kv = trade(self_kv)
     self_part = small_call(
         functools.partial(attend_kernel, heads),
         "attend",
-        shape((lat_rows, width), F32),
+        shape((lat_rows, width), BF),
         core,
         self_q,
         own_kv,
@@ -746,12 +744,13 @@
     lat_two, mlp_part = small_call(
         mlp_kernel,
         "mlp",
-        [shape((lat_rows, width), F32), shape((lat_rows, width), F32)],
+        [shape((lat_rows, width), F32), shape((lat_rows, width), BF)],
         *head_parts(self_part),
         lat_one,
         row(mlp_gain),
         mlp_w1,
         mlp_w2,
+        streamed=mlp_w2,
     )
     normed = small_call(
         last_kernel,
@@ -762,6 +761,7 @@
         row(dec_gain),
     )
     own = trade(normed)
+    prepared = (pltpu.with_memory_space_constraint(prepared[0], pltpu.HBM), *prepared[1:])
     return decode(
         core, queries, query_modality, modality_embed, own, other_core(own), dec_wkv, prepared
     )

time: 160 us -> 157 us (0.981)
  local copies, waits for them, and re-layouts: 4.88 us -> 1.82 us
  Pallas kernels: 87.3 us -> 90 us
  blocking collectives: 25.9 us -> 23.8 us
    unnamed x38 -> x30, local copies, waits for them, and re-layouts: 4 us -> 0.97 us
    ppermute x9, waiting for transfers between devices: 12.6 us -> 10.4 us  [head_parts(): lax.ppermute(part, 'head', [(i, (i + k) % size) for i in range(size)])]
    all_to_all x1, waiting for transfers between devices: 0.01 us -> 2.22 us  [body(): lax.all_to_all(partial.reshape(-1, lat_rows, partial.shape[1]), 'inp', 0, 0)]
    all_to_all x2, blocking collectives: 25.9 us -> 23.8 us  [trade(): return lax.all_to_all(parts, 'inp', 0, 0, axis_index_groups=groups)]
    ppermute x3 -> x2, starting transfers between devices: 9.8 us -> 7.82 us  [other_core(): lax.ppermute(rows, 'inp', [(i, i ^ 1) for i in range(lax.axis_size('inp'))])]
    all_to_all x1, starting transfers between devices: 7.79 us -> 9.67 us  [body(): lax.all_to_all(partial.reshape(-1, lat_rows, partial.shape[1]), 'inp', 0, 0)]
    pallas_call x6 -> x5, Pallas kernels: 5.09 us -> 6.92 us  [small_call(): pl.pallas_call(kernel, out_shape=outs, in_specs=[pl.BlockSpec(memory_spac...]
    ppermute x3 -> x2, waiting for transfers between devices: 3.98 us -> 2.7 us  [other_core(): lax.ppermute(rows, 'inp', [(i, i ^ 1) for i in range(lax.axis_size('inp'))])]
  transfers between devices with their start and end apart: 13 -> 12, of which waited for: 11 -> 11; matrix products, arithmetic and copies ran while one was open for 1% -> 1% of each run, Pallas kernels for 5% -> 5%
where the time goes in v4:
time: 157 us; the launch traced here: 156 us
  Pallas kernels  90 us (57%)
  starting transfers between devices  25.2 us (16%)
  blocking collectives  23.8 us (15%)
  waiting for transfers between devices  15.3 us (10%)
  local copies, waits for them, and re-layouts  1.82 us (1%)
    pallas_call x1, Pallas kernels, encode(): pl.pallas_call(functools.partial(encode_kernel, heads), grid_spec=pltpu.P...  52.1 us
    all_to_all x2, blocking collectives, trade(): return lax.all_to_all(parts, 'inp', 0, 0, axis_index_groups=groups)  23.8 us
    pallas_call x1, Pallas kernels, decode(): pl.pallas_call(functools.partial(decode_kernel, heads), grid_spec=pltpu.P...  23.2 us
    ppermute x9, waiting for transfers between devices, head_parts(): lax.ppermute(part, 'head', [(i, (i + k) % size) for i in range(size)])  10.4 us
    all_to_all x1, starting transfers between devices, body(): lax.all_to_all(partial.reshape(-1, lat_rows, partial.shape[1]), 'inp', 0, 0)  9.67 us
    pallas_call x1, Pallas kernels, prepare_queries(): pl.pallas_call(functools.partial(query_kernel, heads), grid_spec=pltpu.Pr...  7.92 us
    ppermute x2, starting transfers between devices, other_core(): lax.ppermute(rows, 'inp', [(i, i ^ 1) for i in range(lax.axis_size('inp'))])  7.82 us
    ppermute x9, starting transfers between devices, head_parts(): lax.ppermute(part, 'head', [(i, (i + k) % size) for i in range(size)])  7.73 us
  transfers between devices with their start and end apart: 12, of which 11 were waited for; matrix products, arithmetic and copies ran while one was open for 1% of the time, Pallas kernels for 5%

profile of v4, /device:TPU:1, one launch (start us, length us, event | category | flops | bytes accessed | tf_op | source)
XLA Modules:
  0.0 156.3 jit_solution(16203088055948237386)
XLA Ops:
  0.0 52.1 %encode.1 = bf16[512,384]{1,0:T(8,128)(2,1)} custom-call(s32[64]{0:T(128)} %mod_ref.3, bf16[8192,256]{1,0:T(8,128)(2,1)} %next_ref.1, bf16[8192,256]{1,0:T(8,128)(2,1)} %next_ref.1, f32[3,256]{1,0:T(4,128)} %table_ref.5, f32[1,256]{1,0:T(1,128)} %bitcast.13, f32[512,1024]{1,0:T(8,128)} %lat_ref.1, f32[1,1024]{1,0:T(1,128)} %bitcast.12, ...), custom_call_target="tpu_custom_call" | custom-call | flops 12884901888 | bytes 11272192 | tf_op jit(solution)/shard_map/encode/pallas_call | solution.py:235
  52.1 9.7 %all-to-all-start = ((bf16[32,16,384]{2,1,0:T(8,128)(2,1)}), bf16[32,16,384]{2,1,0:T(8,128)(2,1)S(1)}, u32[]{:S(2)}, u32[]{:S(2)}) async-start(bf16[32,16,384]{2,1,0:T(8,128)(2,1)} %bitcast.11), calls=%async_computation | async-start | bytes 786432 | tf_op jit(solution)/shard_map/all_to_all | solution.py:708
  61.7 0.0 copy-start.1
  61.7 0.0 copy-start.4
  61.8 7.9 %queries.1 = (bf16[1024,2048]{1,0:T(8,128)(2,1)}, f32[16,2048]{1,0:T(8,128)}, f32[16,2048]{1,0:T(8,128)}, bf16[2,512,128]{2,1,0:T(8,128)(2,1)}, bf16[256,1024]{1,0:T(8,128)(2,1)}) custom-call(s32[16]{0:T(128)} %mod_ref.5, bf16[2048,256]{1,0:T(8,128)(2,1)} %x_ref.4, f32[3,256]{1,0:T(4,128)} %table_ref.5, f32[1,256]{1,0:T(1,128)} %bitcast.14, ...), custom_call_target="tpu_custom_call" | custom-call | flops 1073741824 | bytes 6291456 | tf_op jit(solution)/shard_map/queries/pallas_call | solution.py:443
  69.7 0.0 copy-start.2
  69.7 2.2 %all-to-all-done.part_ref = bf16[32,16,384]{2,1,0:T(8,128)(2,1)S(1)} async-done(((bf16[32,16,384]{2,1,0:T(8,128)(2,1)}), bf16[32,16,384]{2,1,0:T(8,128)(2,1)S(1)}, u32[]{:S(2)}, u32[]{:S(2)}) %all-to-all-start) | async-done | bytes 393248 | tf_op jit(solution)/shard_map/all_to_all | solution.py:708
  71.9 0.0 copy-done.1
  71.9 0.0 copy-start
  71.9 0.0 copy-start.5
  71.9 0.7 merge.1.a_ref
  72.6 2.7 %collective-permute-start.2 = (bf16[16,1024]{1,0:T(8,128)(2,1)S(1)}, bf16[16,1024]{1,0:T(8,128)(2,1)S(1)}, u32[]{:S(2)}, u32[]{:S(2)}) collective-permute-start(bf16[16,1024]{1,0:T(8,128)(2,1)S(1)} %merge.1.a_ref), channel_id=1, source_target_pairs={{0,3},{1,0},{2,1},{3,2},{4,7},{5,4},{6,5},{7,6},{8,11},{9,8},{10,9... | collective-permute-start | bytes 98312 | tf_op jit(solution)/shard_map/ppermute | solution.py:653
  75.4 0.3 collective-permute-start.1
  75.7 0.7 collective-permute-start
  76.4 0.8 constant_dynamic-slice_fusion.lat_ref
  77.2 0.0 collective-permute-done.2.d_ref
  77.2 2.4 %collective-permute-done.1.c_ref = bf16[16,1024]{1,0:T(8,128)(2,1)S(1)} collective-permute-done((bf16[16,1024]{1,0:T(8,128)(2,1)S(1)}, bf16[16,1024]{1,0:T(8,128)(2,1)S(1)}, u32[]{:S(2)}, u32[]{:S(2)}) %collective-permute-start.1) | collective-permute-done | bytes 32800 | tf_op jit(solution)/shard_map/ppermute | solution.py:653
  79.7 0.3 collective-permute-done.b_ref
  80.0 0.0 copy-done.4
  80.0 1.8 %project.1 = (f32[16,1024]{1,0:T(8,128)S(1)}, bf16[16,256]{1,0:T(8,128)(2,1)S(1)}, bf16[16,16,512]{2,1,0:T(8,128)(2,1)S(1)}) custom-call(bf16[16,1024]{1,0:T(8,128)(2,1)S(1)} %merge.1.a_ref, bf16[16,1024]{1,0:T(8,128)(2,1)S(1)} %collective-permute-done.b_ref, bf16[16,1024]{1,0:T(8,128)(2,1)S(1)} %collective-permute-done.1.c_ref, ...), custom_call_target="tpu_custom_call" | custom-call | tf_op jit(solution)/shard_map/project/pallas_call | solution.py:289
  81.8 11.8 %all_to_all.15.own_ref = bf16[16,16,512]{2,1,0:T(8,128)(2,1)S(1)} all-to-all(bf16[16,16,512]{2,1,0:T(8,128)(2,1)S(1)} %get-tuple-element.32), channel_id=1, replica_groups={{0,8,16,24,32,40,48,56,64,72,80,88,96,104,112,120},{4,12,20,28,36,44,52..., dimensions={0} | all-to-all | bytes 524288 | tf_op jit(solution)/shard_map/all_to_all | solution.py:643
  93.6 3.2 %collective-permute-start.3 = (bf16[16,16,512]{2,1,0:T(8,128)(2,1)S(1)}, bf16[16,16,512]{2,1,0:T(8,128)(2,1)S(1)}, u32[]{:S(2)}, u32[]{:S(2)}) collective-permute-start(bf16[16,16,512]{2,1,0:T(8,128)(2,1)S(1)} %all_to_all.15.own_ref), channel_id=1, source_target_pairs={{0,4},{4,0},{8,12},{12,8},{16,20},{20,16},{24,28},{28,24},{32,36},... | collective-permute-start | bytes 786440 | tf_op jit(solution)/shard_map/ppermute | solution.py:647
  96.8 1.2 collective-permute-done.3.other_ref
  98.0 0.0 copy-done.2
  98.0 0.0 copy-start.3
  98.0 0.9 copy-done.3
  98.9 0.0 copy-start.14
  98.9 1.5 attend.1.a_ref
  100.4 0.3 collective-permute-start.6
  100.7 1.2 collective-permute-start.5
  101.9 0.8 collective-permute-start.4
  102.7 0.5 collective-permute-done.6.d_ref
  103.2 1.8 %collective-permute-done.5.c_ref = bf16[16,1024]{1,0:T(8,128)(2,1)S(1)} collective-permute-done((bf16[16,1024]{1,0:T(8,128)(2,1)S(1)}, bf16[16,1024]{1,0:T(8,128)(2,1)S(1)}, u32[]{:S(2)}, u32[]{:S(2)}) %collective-permute-start.5) | collective-permute-done | bytes 32800 | tf_op jit(solution)/shard_map/ppermute | solution.py:653
  105.0 1.4 collective-permute-done.4.b_ref
  106.4 0.0 copy-done
  106.4 0.0 copy-done.5
  106.4 0.0 copy-start.6
  106.4 0.0 copy-start.8
  106.4 0.0 copy-start.9
  106.4 0.0 copy-start.10
  106.5 0.0 copy-start.11
  106.5 0.0 copy-start.12
  106.5 0.0 copy-start.13
  106.5 2.7 %mlp.1 = (f32[16,1024]{1,0:T(8,128)S(1)}, bf16[16,1024]{1,0:T(8,128)(2,1)S(1)}) custom-call(bf16[16,1024]{1,0:T(8,128)(2,1)S(1)} %attend.1.a_ref, bf16[16,1024]{1,0:T(8,128)(2,1)S(1)} %collective-permute-done.4.b_ref, bf16[16,1024]{1,0:T(8,128)(2,1)S(1)} %collective-permute-done.5.c_ref, bf16[16,1024]{1,0:T(8,128)(2,1)S(1)} %collective-permute-done.6.d_ref, ...), custom_call_target="tpu_custom_call" | custom-call | tf_op jit(solution)/shard_map/mlp/pallas_call | solution.py:289
  109.2 1.0 collective-permute-start.9
  110.2 0.6 collective-permute-start.8
  110.8 0.1 collective-permute-start.7
  110.9 1.1 collective-permute-done.9.d_ref
  112.0 2.5 %collective-permute-done.8.c_ref = bf16[16,1024]{1,0:T(8,128)(2,1)S(1)} collective-permute-done((bf16[16,1024]{1,0:T(8,128)(2,1)S(1)}, bf16[16,1024]{1,0:T(8,128)(2,1)S(1)}, u32[]{:S(2)}, u32[]{:S(2)}) %collective-permute-start.8) | collective-permute-done | bytes 32800 | tf_op jit(solution)/shard_map/ppermute | solution.py:653
  114.5 0.4 collective-permute-done.7.b_ref
  114.8 0.0 copy-done.6
  114.8 0.2 last.1
  115.1 11.9 %all_to_all.16.own_ref = bf16[16,16,1024]{2,1,0:T(8,128)(2,1)S(1)} all-to-all(bf16[16,16,1024]{2,1,0:T(8,128)(2,1)S(1)} %last.1), channel_id=1, replica_groups={{0,8,16,24,32,40,48,56,64,72,80,88,96,104,112,120},{4,12,20,28,36,44,52..., dimensions={0} | all-to-all | bytes 1048576 | tf_op jit(solution)/shard_map/all_to_all | solution.py:643
  127.0 4.6 %collective-permute-start.10 = (bf16[16,16,1024]{2,1,0:T(8,128)(2,1)S(1)}, bf16[16,16,1024]{2,1,0:T(8,128)(2,1)S(1)}, u32[]{:S(2)}, u32[]{:S(2)}) collective-permute-start(bf16[16,16,1024]{2,1,0:T(8,128)(2,1)S(1)} %all_to_all.16.own_ref), channel_id=1, source_target_pairs={{0,4},{4,0},{8,12},{12,8},{16,20},{20,16},{24,28},{28,24},{32,36},... | collective-permute-start | bytes 1572872 | tf_op jit(solution)/shard_map/ppermute | solution.py:647
  131.6 1.5 collective-permute-done.10.other_ref
  133.1 0.0 copy-done.14
  133.1 0.0 copy-done.7
  133.1 0.0 copy-done.8
  133.1 0.0 copy-done.9
  133.1 0.0 copy-done.10
  133.1 0.0 copy-done.11
  133.1 0.0 copy-done.12
  133.2 0.0 copy-done.13
  133.2 23.2 %decode.1 = f32[2048,256]{1,0:T(8,128)} custom-call(s32[16]{0:T(128)S(1)} %copy-done.10, s32[1]{0:T(128)} %bitcast.core_ref, bf16[2048,256]{1,0:T(8,128)(2,1)S(1)} %copy-done.8, f32[3,256]{1,0:T(4,128)S(1)} %copy-done.9, bf16[16,16,1024]{2,1,0:T(8,128)(2,1)S(1)} %all_to_all.16.own_ref, bf16[16,16,1024]{2,1,0:T(8,128)(2,1)S(1)} %collective-permute-done.10.other_ref, ...), custom_call_target="tpu_custom_call" | custom-call | flops 13958643712 | bytes 11534336 | tf_op jit(solution)/shard_map/decode/pallas_call | solution.py:601
  (1 shorter events, 0.0 us)
Async XLA Ops:
  52.1 19.8 %all-to-all-start = ((bf16[32,16,384]{2,1,0:T(8,128)(2,1)}), bf16[32,16,384]{2,1,0:T(8,128)(2,1)S(1)}, u32[]{:S(2)}, u32[]{:S(2)}) async-start(bf16[32,16,384]{2,1,0:T(8,128)(2,1)} %bitcast.11), calls=%async_computation | async-start | bytes 786432 | tf_op jit(solution)/shard_map/all_to_all | solution.py:708
  61.7 10.2 %copy-start.1 = (bf16[256,1024]{1,0:T(8,128)(2,1)S(1)}, bf16[256,1024]{1,0:T(8,128)(2,1)}, u32[]{:S(2)}) copy-start(bf16[256,1024]{1,0:T(8,128)(2,1)} %wo_ref.4) | copy-start | bytes 1572868
  61.7 18.2 %copy-start.4 = (f32[1024]{0:T(1024)S(1)}, f32[1024]{0:T(1024)}, u32[]{:S(2)}) copy-start(f32[1024]{0:T(1024)} %param.37) | copy-start | bytes 12292
  69.7 28.3 %copy-start.2 = (bf16[256,1024]{1,0:T(8,128)(2,1)S(1)}, bf16[256,1024]{1,0:T(8,128)(2,1)}, u32[]{:S(2)}) copy-start(bf16[256,1024]{1,0:T(8,128)(2,1)} %wo_ref.5) | copy-start | bytes 1572868
  71.9 34.5 %copy-start = (bf16[1024,1024]{1,0:T(8,128)(2,1)S(1)}, bf16[1024,1024]{1,0:T(8,128)(2,1)}, u32[]{:S(2)}) copy-start(bf16[1024,1024]{1,0:T(8,128)(2,1)} %w1_ref.1) | copy-start | bytes 6291460
  71.9 34.5 %copy-start.5 = (f32[1024]{0:T(1024)S(1)}, f32[1024]{0:T(1024)}, u32[]{:S(2)}) copy-start(f32[1024]{0:T(1024)} %param.41) | copy-start | bytes 12292
  72.6 4.6 %collective-permute-start.2 = (bf16[16,1024]{1,0:T(8,128)(2,1)S(1)}, bf16[16,1024]{1,0:T(8,128)(2,1)S(1)}, u32[]{:S(2)}, u32[]{:S(2)}) collective-permute-start(bf16[16,1024]{1,0:T(8,128)(2,1)S(1)} %merge.1.a_ref), channel_id=1, source_target_pairs={{0,3},{1,0},{2,1},{3,2},{4,7},{5,4},{6,5},{7,6},{8,11},{9,8},{10,9... | collective-permute-start | bytes 98312 | tf_op jit(solution)/shard_map/ppermute | solution.py:653
  75.4 4.3 %collective-permute-start.1 = (bf16[16,1024]{1,0:T(8,128)(2,1)S(1)}, bf16[16,1024]{1,0:T(8,128)(2,1)S(1)}, u32[]{:S(2)}, u32[]{:S(2)}) collective-permute-start(bf16[16,1024]{1,0:T(8,128)(2,1)S(1)} %merge.1.a_ref), channel_id=1, source_target_pairs={{0,2},{1,3},{2,0},{3,1},{4,6},{5,7},{6,4},{7,5},{8,10},{9,11},{10,... | collective-permute-start | bytes 98312 | tf_op jit(solution)/shard_map/ppermute | solution.py:653
  75.7 4.3 %collective-permute-start = (bf16[16,1024]{1,0:T(8,128)(2,1)S(1)}, bf16[16,1024]{1,0:T(8,128)(2,1)S(1)}, u32[]{:S(2)}, u32[]{:S(2)}) collective-permute-start(bf16[16,1024]{1,0:T(8,128)(2,1)S(1)} %merge.1.a_ref), channel_id=1, source_target_pairs={{0,1},{1,2},{2,3},{3,0},{4,5},{5,6},{6,7},{7,4},{8,9},{9,10},{10,1... | collective-permute-start | bytes 98312 | tf_op jit(solution)/shard_map/ppermute | solution.py:653
  93.6 4.4 %collective-permute-start.3 = (bf16[16,16,512]{2,1,0:T(8,128)(2,1)S(1)}, bf16[16,16,512]{2,1,0:T(8,128)(2,1)S(1)}, u32[]{:S(2)}, u32[]{:S(2)}) collective-permute-start(bf16[16,16,512]{2,1,0:T(8,128)(2,1)S(1)} %all_to_all.15.own_ref), channel_id=1, source_target_pairs={{0,4},{4,0},{8,12},{12,8},{16,20},{20,16},{24,28},{28,24},{32,36},... | collective-permute-start | bytes 786440 | tf_op jit(solution)/shard_map/ppermute | solution.py:647
  98.0 0.9 copy-start.3
  98.9 34.2 %copy-start.14 = (f32[16,2048]{1,0:T(8,128)S(1)}, f32[16,2048]{1,0:T(8,128)}, u32[]{:S(2)}) copy-start(f32[16,2048]{1,0:T(8,128)} %get-tuple-element.39.top_ref) | copy-start | bytes 393220
  100.4 2.8 %collective-permute-start.6 = (bf16[16,1024]{1,0:T(8,128)(2,1)S(1)}, bf16[16,1024]{1,0:T(8,128)(2,1)S(1)}, u32[]{:S(2)}, u32[]{:S(2)}) collective-permute-start(bf16[16,1024]{1,0:T(8,128)(2,1)S(1)} %attend.1.a_ref), channel_id=1, source_target_pairs={{0,3},{1,0},{2,1},{3,2},{4,7},{5,4},{6,5},{7,6},{8,11},{9,8},{10,9... | collective-permute-start | bytes 98312 | tf_op jit(solution)/shard_map/ppermute | solution.py:653
  100.7 4.3 %collective-permute-start.5 = (bf16[16,1024]{1,0:T(8,128)(2,1)S(1)}, bf16[16,1024]{1,0:T(8,128)(2,1)S(1)}, u32[]{:S(2)}, u32[]{:S(2)}) collective-permute-start(bf16[16,1024]{1,0:T(8,128)(2,1)S(1)} %attend.1.a_ref), channel_id=1, source_target_pairs={{0,2},{1,3},{2,0},{3,1},{4,6},{5,7},{6,4},{7,5},{8,10},{9,11},{10,... | collective-permute-start | bytes 98312 | tf_op jit(solution)/shard_map/ppermute | solution.py:653
  101.9 4.5 %collective-permute-start.4 = (bf16[16,1024]{1,0:T(8,128)(2,1)S(1)}, bf16[16,1024]{1,0:T(8,128)(2,1)S(1)}, u32[]{:S(2)}, u32[]{:S(2)}) collective-permute-start(bf16[16,1024]{1,0:T(8,128)(2,1)S(1)} %attend.1.a_ref), channel_id=1, source_target_pairs={{0,1},{1,2},{2,3},{3,0},{4,5},{5,6},{6,7},{7,4},{8,9},{9,10},{10,1... | collective-permute-start | bytes 98312 | tf_op jit(solution)/shard_map/ppermute | solution.py:653
  106.4 8.4 %copy-start.6 = (f32[1024]{0:T(1024)S(1)}, f32[1024]{0:T(1024)}, u32[]{:S(2)}) copy-start(f32[1024]{0:T(1024)} %param.44) | copy-start | bytes 12292
  106.4 26.7 %copy-start.7 = (bf16[2,1024,1024]{2,1,0:T(8,128)(2,1)S(1)}, bf16[2,1024,1024]{2,1,0:T(8,128)(2,1)}, u32[]{:S(2)}) copy-start(bf16[2,1024,1024]{2,1,0:T(8,128)(2,1)} %wkv_ref.3) | copy-start | bytes 12582916
  106.4 26.7 %copy-start.8 = (bf16[2048,256]{1,0:T(8,128)(2,1)S(1)}, bf16[2048,256]{1,0:T(8,128)(2,1)}, u32[]{:S(2)}) copy-start(bf16[2048,256]{1,0:T(8,128)(2,1)} %x_ref.4) | copy-start | bytes 3145732
  106.4 26.7 %copy-start.9 = (f32[3,256]{1,0:T(4,128)S(1)}, f32[3,256]{1,0:T(4,128)}, u32[]{:S(2)}) copy-start(f32[3,256]{1,0:T(4,128)} %table_ref.5) | copy-start | bytes 9220
  106.4 26.7 %copy-start.10 = (s32[16]{0:T(128)S(1)}, s32[16]{0:T(128)}, u32[]{:S(2)}) copy-start(s32[16]{0:T(128)} %mod_ref.5) | copy-start | bytes 196
  106.5 26.7 %copy-start.11 = (bf16[256,1024]{1,0:T(8,128)(2,1)S(1)}, bf16[256,1024]{1,0:T(8,128)(2,1)}, u32[]{:S(2)}) copy-start(bf16[256,1024]{1,0:T(8,128)(2,1)} %get-tuple-element.40.wot_ref) | copy-start | bytes 1572868
  106.5 26.7 %copy-start.12 = (bf16[2,512,128]{2,1,0:T(8,128)(2,1)S(1)}, bf16[2,512,128]{2,1,0:T(8,128)(2,1)}, u32[]{:S(2)}) copy-start(bf16[2,512,128]{2,1,0:T(8,128)(2,1)} %get-tuple-element.36.bias_ref) | copy-start | bytes 786436
  106.5 26.7 %copy-start.13 = (f32[16,2048]{1,0:T(8,128)S(1)}, f32[16,2048]{1,0:T(8,128)}, u32[]{:S(2)}) copy-start(f32[16,2048]{1,0:T(8,128)} %get-tuple-element.38.norm_ref) | copy-start | bytes 393220
  109.2 2.8 %collective-permute-start.9 = (bf16[16,1024]{1,0:T(8,128)(2,1)S(1)}, bf16[16,1024]{1,0:T(8,128)(2,1)S(1)}, u32[]{:S(2)}, u32[]{:S(2)}) collective-permute-start(bf16[16,1024]{1,0:T(8,128)(2,1)S(1)} %get-tuple-element.34.a_ref), channel_id=1, source_target_pairs={{0,3},{1,0},{2,1},{3,2},{4,7},{5,4},{6,5},{7,6},{8,11},{9,8},{10,9... | collective-permute-start | bytes 98312 | tf_op jit(solution)/shard_map/ppermute | solution.py:653
  110.2 4.3 %collective-permute-start.8 = (bf16[16,1024]{1,0:T(8,128)(2,1)S(1)}, bf16[16,1024]{1,0:T(8,128)(2,1)S(1)}, u32[]{:S(2)}, u32[]{:S(2)}) collective-permute-start(bf16[16,1024]{1,0:T(8,128)(2,1)S(1)} %get-tuple-element.34.a_ref), channel_id=1, source_target_pairs={{0,2},{1,3},{2,0},{3,1},{4,6},{5,7},{6,4},{7,5},{8,10},{9,11},{10,... | collective-permute-start | bytes 98312 | tf_op jit(solution)/shard_map/ppermute | solution.py:653
  110.8 4.0 %collective-permute-start.7 = (bf16[16,1024]{1,0:T(8,128)(2,1)S(1)}, bf16[16,1024]{1,0:T(8,128)(2,1)S(1)}, u32[]{:S(2)}, u32[]{:S(2)}) collective-permute-start(bf16[16,1024]{1,0:T(8,128)(2,1)S(1)} %get-tuple-element.34.a_ref), channel_id=1, source_target_pairs={{0,1},{1,2},{2,3},{3,0},{4,5},{5,6},{6,7},{7,4},{8,9},{9,10},{10,1... | collective-permute-start | bytes 98312 | tf_op jit(solution)/shard_map/ppermute | solution.py:653
  127.0 6.1 %collective-permute-start.10 = (bf16[16,16,1024]{2,1,0:T(8,128)(2,1)S(1)}, bf16[16,16,1024]{2,1,0:T(8,128)(2,1)S(1)}, u32[]{:S(2)}, u32[]{:S(2)}) collective-permute-start(bf16[16,16,1024]{2,1,0:T(8,128)(2,1)S(1)} %all_to_all.16.own_ref), channel_id=1, source_target_pairs={{0,4},{4,0},{8,12},{12,8},{16,20},{20,16},{24,28},{28,24},{32,36},... | collective-permute-start | bytes 1572872 | tf_op jit(solution)/shard_map/ppermute | solution.py:647

commit v5 on v4

--- a/solution.py
+++ b/solution.py
@@ -275,17 +275,8 @@
     )(input_modality, inputs, inputs, table, gain, latents, lat_gain, wq, wkv, bias)
 
 
-def small_call(kernel, name, outs, *args, scratch=(), streamed=None):
-    def space(a):
-        if a is streamed:
-            return pltpu.HBM
-        return pltpu.SMEM if a.dtype == jnp.int32 else pltpu.VMEM
-
-    if streamed is not None:
-        scratch = (pltpu.VMEM(streamed.shape, streamed.dtype), pltpu.SemaphoreType.DMA(()))
-        far = pltpu.with_memory_space_constraint(streamed, pltpu.HBM)
-        args = [far if a is streamed else a for a in args]
-        streamed = far
+def small_call(kernel, name, outs, *args, scratch=()):
+    space = lambda a: pltpu.SMEM if a.dtype == jnp.int32 else pltpu.VMEM
     return pl.pallas_call(
         kernel,
         out_shape=outs,
@@ -327,16 +318,11 @@
     return (a + b) + (c + d)
 
 
-def project_kernel(
-    a_ref, b_ref, c_ref, d_ref, lat_ref, gain_ref, far_ref, lat_out, q_out, kv_out, w_ref, sem
-):
-    copy = pltpu.make_async_copy(far_ref, w_ref, sem)
-    copy.start()
+def project_kernel(a_ref, b_ref, c_ref, d_ref, lat_ref, gain_ref, w_ref, lat_out, q_out, kv_out):
     lat = lat_ref[...] + added(a_ref, b_ref, c_ref, d_ref)
     lat_out[...] = lat
     normed = layer_norm(lat, gain_ref[...]).astype(BF)
     cols = w_ref.shape[2]
-    copy.wait()
     q_out[...] = (dot(normed, w_ref[0]) * SCALE2).astype(BF)
     keys = dot(normed, w_ref[1]).astype(BF)
     values = dot(normed, w_ref[2]).astype(BF)
@@ -363,16 +349,11 @@
     out_ref[...] = dot(mixed.astype(BF), wo_ref[...]).astype(BF)
 
 
-def mlp_kernel(
-    a_ref, b_ref, c_ref, d_ref, lat_ref, gain_ref, w1_ref, far_ref, lat_out, out_ref, w2_ref, sem
-):
-    copy = pltpu.make_async_copy(far_ref, w2_ref, sem)
-    copy.start()
+def mlp_kernel(a_ref, b_ref, c_ref, d_ref, lat_ref, gain_ref, w1_ref, w2_ref, lat_out, out_ref):
     lat = lat_ref[...] + added(a_ref, b_ref, c_ref, d_ref)
     lat_out[...] = lat
     normed = layer_norm(lat, gain_ref[...]).astype(BF)
     hidden = jax.nn.gelu(dot(normed, w1_ref[...]), approximate=True).astype(BF)
-    copy.wait()
     out_ref[...] = dot(hidden, w2_ref[...]).astype(BF)
 
 
@@ -637,6 +618,35 @@
     )(query_modality, core, queries, table, own, other, wkv, bias, queries_t, norms, tops, wo_t)
 
 
+def fetch_kernel(count, *refs):
+    sems = refs[-1]
+    copies = [
+        pltpu.make_async_copy(refs[i], refs[count + i], sems.at[i]) for i in range(count)
+    ]
+    for copy in copies:
+        copy.start()
+    for copy in copies:
+        copy.wait()
+
+
+def fetch(after, *arrays):
+    after, *arrays = lax.optimization_barrier((after, *arrays))
+    arrays = [pltpu.with_memory_space_constraint(a, pltpu.HBM) for a in arrays]
+    near = pl.pallas_call(
+        functools.partial(fetch_kernel, len(arrays)),
+        out_shape=[jax.ShapeDtypeStruct(a.shape, a.dtype) for a in arrays],
+        in_specs=[pl.BlockSpec(memory_space=pltpu.HBM)] * len(arrays),
+        out_specs=[pl.BlockSpec(memory_space=pltpu.VMEM)] * len(arrays),
+        scratch_shapes=[pltpu.SemaphoreType.DMA((len(arrays),))],
+        compiler_params=pltpu.CompilerParams(vmem_limit_bytes=14 * MIB),
+        cost_estimate=pl.CostEstimate(
+            flops=0, transcendentals=0, bytes_accessed=2 * sum(a.nbytes for a in arrays)
+        ),
+        name="fetch",
+    )(*arrays)
+    return after, *near
+
+
 def trade(parts):
     size = lax.axis_size("inp")
     groups = [list(range(core, size, 2)) for core in range(2)]
@@ -713,6 +723,7 @@
     enc_part = small_call(
         functools.partial(merge_kernel, heads), "merge", shape((lat_rows, width), BF), parts, enc_wo
     )
+    enc_part, weights, near_bias = fetch(enc_part, self_wqkv, self_bias)
     latent_rows = lax.dynamic_slice_in_dim(latents, row_first, lat_rows, 0)
     lat_one, self_q, self_kv = small_call(
         project_kernel,
@@ -725,8 +736,7 @@
         *head_parts(enc_part),
         latent_rows,
         row(self_gain),
-        self_wqkv,
-        streamed=self_wqkv,
+        weights,
     )
     own_kv = trade(self_kv)
     self_part = small_call(
@@ -737,10 +747,11 @@
         self_q,
         own_kv,
         other_core(own_kv),
-        self_bias,
+        near_bias,
         self_wo,
         scratch=[pltpu.VMEM((lat_count, 2 * cols), BF)],
     )
+    self_part, weights = fetch(self_part, mlp_w2)
     lat_two, mlp_part = small_call(
         mlp_kernel,
         "mlp",
@@ -749,8 +760,7 @@
         lat_one,
         row(mlp_gain),
         mlp_w1,
-        mlp_w2,
-        streamed=mlp_w2,
+        weights,
     )
     normed = small_call(
         last_kernel,

time: 157 us -> 153 us (0.975)
  waiting for transfers between devices: 15.3 us -> 12.2 us
    pallas_call x5, Pallas kernels: 6.92 us -> 3.8 us  [small_call(): pl.pallas_call(kernel, out_shape=outs, in_specs=[pl.BlockSpec(memory_spac...]
    ppermute x9, waiting for transfers between devices: 10.4 us -> 7.27 us  [head_parts(): lax.ppermute(part, 'head', [(i, (i + k) % size) for i in range(size)])]
    pallas_call x0 -> x2, Pallas kernels: none -> 3.06 us  [fetch(): pl.pallas_call(functools.partial(fetch_kernel, len(arrays)), out_shape=[j...]
  transfers between devices with their start and end apart: 12 -> 12, of which waited for: 11 -> 10; matrix products, arithmetic and copies ran while one was open for 1% -> 1% of each run, Pallas kernels for 5% -> 7%
where the time goes in v5:
time: 153 us; the launch traced here: 152 us
  Pallas kernels  89.9 us (59%)
  starting transfers between devices  25.2 us (16%)
  blocking collectives  23.7 us (15%)
  waiting for transfers between devices  12.2 us (8%)
    pallas_call x1, Pallas kernels, encode(): pl.pallas_call(functools.partial(encode_kernel, heads), grid_spec=pltpu.P...  52 us
    all_to_all x2, blocking collectives, trade(): return lax.all_to_all(parts, 'inp', 0, 0, axis_index_groups=groups)  23.7 us
    pallas_call x1, Pallas kernels, decode(): pl.pallas_call(functools.partial(decode_kernel, heads), grid_spec=pltpu.P...  23.1 us
    all_to_all x1, starting transfers between devices, body(): lax.all_to_all(partial.reshape(-1, lat_rows, partial.shape[1]), 'inp', 0, 0)  9.65 us
    pallas_call x1, Pallas kernels, prepare_queries(): pl.pallas_call(functools.partial(query_kernel, heads), grid_spec=pltpu.Pr...  7.91 us
    ppermute x2, starting transfers between devices, other_core(): lax.ppermute(rows, 'inp', [(i, i ^ 1) for i in range(lax.axis_size('inp'))])  7.83 us
    ppermute x9, starting transfers between devices, head_parts(): lax.ppermute(part, 'head', [(i, (i + k) % size) for i in range(size)])  7.72 us
    ppermute x9, waiting for transfers between devices, head_parts(): lax.ppermute(part, 'head', [(i, (i + k) % size) for i in range(size)])  7.27 us
  transfers between devices with their start and end apart: 12, of which 10 were waited for; matrix products, arithmetic and copies ran while one was open for 1% of the time, Pallas kernels for 7%

profile of v5, /device:TPU:1, one launch (start us, length us, event | category | flops | bytes accessed | tf_op | source)
XLA Modules:
  0.0 152.1 jit_solution(7579682299478737001)
XLA Ops:
  0.0 52.0 %encode.1 = bf16[512,384]{1,0:T(8,128)(2,1)} custom-call(s32[64]{0:T(128)} %mod_ref.3, bf16[8192,256]{1,0:T(8,128)(2,1)} %next_ref.1, bf16[8192,256]{1,0:T(8,128)(2,1)} %next_ref.1, f32[3,256]{1,0:T(4,128)} %table_ref.5, f32[1,256]{1,0:T(1,128)} %bitcast.13, f32[512,1024]{1,0:T(8,128)} %lat_ref.1, f32[1,1024]{1,0:T(1,128)} %bitcast.12, ...), custom_call_target="tpu_custom_call" | custom-call | flops 12884901888 | bytes 11272192 | tf_op jit(solution)/shard_map/encode/pallas_call | solution.py:235
  52.0 9.6 %all-to-all-start = ((bf16[32,16,384]{2,1,0:T(8,128)(2,1)}), bf16[32,16,384]{2,1,0:T(8,128)(2,1)S(1)}, u32[]{:S(2)}, u32[]{:S(2)}) async-start(bf16[32,16,384]{2,1,0:T(8,128)(2,1)} %bitcast.11), calls=%async_computation | async-start | bytes 786432 | tf_op jit(solution)/shard_map/all_to_all | solution.py:718
  61.7 0.0 copy-start.1
  61.7 7.9 %queries.1 = (bf16[1024,2048]{1,0:T(8,128)(2,1)}, f32[16,2048]{1,0:T(8,128)}, f32[16,2048]{1,0:T(8,128)}, bf16[2,512,128]{2,1,0:T(8,128)(2,1)}, bf16[256,1024]{1,0:T(8,128)(2,1)}) custom-call(s32[16]{0:T(128)} %mod_ref.5, bf16[2048,256]{1,0:T(8,128)(2,1)} %x_ref.4, f32[3,256]{1,0:T(4,128)} %table_ref.5, f32[1,256]{1,0:T(1,128)} %bitcast.14, ...), custom_call_target="tpu_custom_call" | custom-call | flops 1073741824 | bytes 6291456 | tf_op jit(solution)/shard_map/queries/pallas_call | solution.py:424
  69.6 0.0 copy-start.3
  69.6 2.2 %all-to-all-done.part_ref = bf16[32,16,384]{2,1,0:T(8,128)(2,1)S(1)} async-done(((bf16[32,16,384]{2,1,0:T(8,128)(2,1)}), bf16[32,16,384]{2,1,0:T(8,128)(2,1)S(1)}, u32[]{:S(2)}, u32[]{:S(2)}) %all-to-all-start) | async-done | bytes 393248 | tf_op jit(solution)/shard_map/all_to_all | solution.py:718
  71.8 0.0 copy-done.1
  71.8 0.7 merge.1.a_ref
  72.6 0.0 copy-start.2
  72.6 2.7 %collective-permute-start.2 = (bf16[16,1024]{1,0:T(8,128)(2,1)S(1)}, bf16[16,1024]{1,0:T(8,128)(2,1)S(1)}, u32[]{:S(2)}, u32[]{:S(2)}) collective-permute-start(bf16[16,1024]{1,0:T(8,128)(2,1)S(1)} %merge.1.a_ref), channel_id=1, source_target_pairs={{0,3},{1,0},{2,1},{3,2},{4,7},{5,4},{6,5},{7,6},{8,11},{9,8},{10,9... | collective-permute-start | bytes 98312 | tf_op jit(solution)/shard_map/ppermute | solution.py:663
  75.3 0.4 collective-permute-start.1
  75.6 0.7 collective-permute-start
  76.3 0.8 constant_dynamic-slice_fusion.lat_ref
  77.2 1.4 fetch.2
  78.6 0.0 collective-permute-done.2.d_ref
  78.6 1.0 collective-permute-done.1.c_ref
  79.6 0.3 collective-permute-done.b_ref
  79.9 0.0 copy-done.3
  79.9 0.5 project.1
  80.4 11.8 %all_to_all.15.own_ref = bf16[16,16,512]{2,1,0:T(8,128)(2,1)S(1)} all-to-all(bf16[16,16,512]{2,1,0:T(8,128)(2,1)S(1)} %get-tuple-element.43), channel_id=1, replica_groups={{0,8,16,24,32,40,48,56,64,72,80,88,96,104,112,120},{4,12,20,28,36,44,52..., dimensions={0} | all-to-all | bytes 524288 | tf_op jit(solution)/shard_map/all_to_all | solution.py:653
  92.2 3.2 %collective-permute-start.3 = (bf16[16,16,512]{2,1,0:T(8,128)(2,1)S(1)}, bf16[16,16,512]{2,1,0:T(8,128)(2,1)S(1)}, u32[]{:S(2)}, u32[]{:S(2)}) collective-permute-start(bf16[16,16,512]{2,1,0:T(8,128)(2,1)S(1)} %all_to_all.15.own_ref), channel_id=1, source_target_pairs={{0,4},{4,0},{8,12},{12,8},{16,20},{20,16},{24,28},{28,24},{32,36},... | collective-permute-start | bytes 786440 | tf_op jit(solution)/shard_map/ppermute | solution.py:657
  95.5 1.2 collective-permute-done.3.other_ref
  96.6 0.0 copy-done.2
  96.6 1.5 attend.1.a_ref
  98.1 0.0 copy-start
  98.1 0.3 collective-permute-start.6
  98.5 1.3 collective-permute-start.5
  99.7 0.7 collective-permute-start.4
  100.4 0.0 copy-start.13
  100.4 1.6 %fetch.3.w2_ref = bf16[1024,1024]{1,0:T(8,128)(2,1)S(1)} custom-call(bf16[1024,1024]{1,0:T(8,128)(2,1)} %refs_0_.1), custom_call_target="tpu_custom_call" | custom-call | bytes 4194304 | tf_op jit(solution)/shard_map/fetch/pallas_call | solution.py:635
  102.1 0.0 collective-permute-done.6.d_ref
  102.1 0.6 collective-permute-done.5.c_ref
  102.7 1.4 collective-permute-done.4.b_ref
  104.1 0.0 copy-done
  104.1 0.0 copy-done.4
  104.2 0.0 copy-start.5
  104.2 0.0 copy-start.6
  104.2 0.0 copy-start.7
  104.2 0.0 copy-start.8
  104.2 0.0 copy-start.9
  104.2 0.0 copy-start.10
  104.2 0.0 copy-start.11
  104.2 0.0 copy-start.12
  104.2 0.9 mlp.1
  105.1 1.0 collective-permute-start.9
  106.1 0.6 collective-permute-start.8
  106.7 0.1 collective-permute-start.7
  106.7 1.1 collective-permute-done.9.d_ref
  107.9 2.5 %collective-permute-done.8.c_ref = bf16[16,1024]{1,0:T(8,128)(2,1)S(1)} collective-permute-done((bf16[16,1024]{1,0:T(8,128)(2,1)S(1)}, bf16[16,1024]{1,0:T(8,128)(2,1)S(1)}, u32[]{:S(2)}, u32[]{:S(2)}) %collective-permute-start.8) | collective-permute-done | bytes 32800 | tf_op jit(solution)/shard_map/ppermute | solution.py:663
  110.3 0.4 collective-permute-done.7.b_ref
  110.7 0.0 copy-done.5
  110.7 0.2 last.1
  110.9 11.9 %all_to_all.16.own_ref = bf16[16,16,1024]{2,1,0:T(8,128)(2,1)S(1)} all-to-all(bf16[16,16,1024]{2,1,0:T(8,128)(2,1)S(1)} %last.1), channel_id=1, replica_groups={{0,8,16,24,32,40,48,56,64,72,80,88,96,104,112,120},{4,12,20,28,36,44,52..., dimensions={0} | all-to-all | bytes 1048576 | tf_op jit(solution)/shard_map/all_to_all | solution.py:653
  122.8 4.6 %collective-permute-start.10 = (bf16[16,16,1024]{2,1,0:T(8,128)(2,1)S(1)}, bf16[16,16,1024]{2,1,0:T(8,128)(2,1)S(1)}, u32[]{:S(2)}, u32[]{:S(2)}) collective-permute-start(bf16[16,16,1024]{2,1,0:T(8,128)(2,1)S(1)} %all_to_all.16.own_ref), channel_id=1, source_target_pairs={{0,4},{4,0},{8,12},{12,8},{16,20},{20,16},{24,28},{28,24},{32,36},... | collective-permute-start | bytes 1572872 | tf_op jit(solution)/shard_map/ppermute | solution.py:657
  127.4 1.5 %collective-permute-done.10.other_ref = bf16[16,16,1024]{2,1,0:T(8,128)(2,1)S(1)} collective-permute-done((bf16[16,16,1024]{2,1,0:T(8,128)(2,1)S(1)}, bf16[16,16,1024]{2,1,0:T(8,128)(2,1)S(1)}, u32[]{:S(2)}, u32[]{:S(2)}) %collective-permute-start.10) | collective-permute-done | bytes 524320 | tf_op jit(solution)/shard_map/ppermute | solution.py:657
  129.0 0.0 copy-done.13
  129.0 0.0 copy-done.6
  129.0 0.0 copy-done.7
  129.0 0.0 copy-done.8
  129.0 0.0 copy-done.9
  129.0 0.0 copy-done.10
  129.0 0.0 copy-done.11
  129.0 0.0 copy-done.12
  129.0 23.1 %decode.1 = f32[2048,256]{1,0:T(8,128)} custom-call(s32[16]{0:T(128)S(1)} %copy-done.9, s32[1]{0:T(128)} %bitcast.core_ref, bf16[2048,256]{1,0:T(8,128)(2,1)S(1)} %copy-done.7, f32[3,256]{1,0:T(4,128)S(1)} %copy-done.8, bf16[16,16,1024]{2,1,0:T(8,128)(2,1)S(1)} %all_to_all.16.own_ref, bf16[16,16,1024]{2,1,0:T(8,128)(2,1)S(1)} %collective-permute-done.10.other_ref, ...), custom_call_target="tpu_custom_call" | custom-call | flops 13958643712 | bytes 11534336 | tf_op jit(solution)/shard_map/decode/pallas_call | solution.py:582
  (1 shorter events, 0.0 us)
Async XLA Ops:
  52.0 19.8 %all-to-all-start = ((bf16[32,16,384]{2,1,0:T(8,128)(2,1)}), bf16[32,16,384]{2,1,0:T(8,128)(2,1)S(1)}, u32[]{:S(2)}, u32[]{:S(2)}) async-start(bf16[32,16,384]{2,1,0:T(8,128)(2,1)} %bitcast.11), calls=%async_computation | async-start | bytes 786432 | tf_op jit(solution)/shard_map/all_to_all | solution.py:718
  61.7 10.2 %copy-start.1 = (bf16[256,1024]{1,0:T(8,128)(2,1)S(1)}, bf16[256,1024]{1,0:T(8,128)(2,1)}, u32[]{:S(2)}) copy-start(bf16[256,1024]{1,0:T(8,128)(2,1)} %wo_ref.4) | copy-start | bytes 1572868
  69.6 10.3 %copy-start.3 = (f32[1024]{0:T(1024)S(1)}, f32[1024]{0:T(1024)}, u32[]{:S(2)}) copy-start(f32[1024]{0:T(1024)} %param.37) | copy-start | bytes 12292
  72.6 24.1 %copy-start.2 = (bf16[256,1024]{1,0:T(8,128)(2,1)S(1)}, bf16[256,1024]{1,0:T(8,128)(2,1)}, u32[]{:S(2)}) copy-start(bf16[256,1024]{1,0:T(8,128)(2,1)} %wo_ref.5) | copy-start | bytes 1572868
  72.6 6.0 %collective-permute-start.2 = (bf16[16,1024]{1,0:T(8,128)(2,1)S(1)}, bf16[16,1024]{1,0:T(8,128)(2,1)S(1)}, u32[]{:S(2)}, u32[]{:S(2)}) collective-permute-start(bf16[16,1024]{1,0:T(8,128)(2,1)S(1)} %merge.1.a_ref), channel_id=1, source_target_pairs={{0,3},{1,0},{2,1},{3,2},{4,7},{5,4},{6,5},{7,6},{8,11},{9,8},{10,9... | collective-permute-start | bytes 98312 | tf_op jit(solution)/shard_map/ppermute | solution.py:663
  75.3 4.3 %collective-permute-start.1 = (bf16[16,1024]{1,0:T(8,128)(2,1)S(1)}, bf16[16,1024]{1,0:T(8,128)(2,1)S(1)}, u32[]{:S(2)}, u32[]{:S(2)}) collective-permute-start(bf16[16,1024]{1,0:T(8,128)(2,1)S(1)} %merge.1.a_ref), channel_id=1, source_target_pairs={{0,2},{1,3},{2,0},{3,1},{4,6},{5,7},{6,4},{7,5},{8,10},{9,11},{10,... | collective-permute-start | bytes 98312 | tf_op jit(solution)/shard_map/ppermute | solution.py:663
  75.6 4.2 %collective-permute-start = (bf16[16,1024]{1,0:T(8,128)(2,1)S(1)}, bf16[16,1024]{1,0:T(8,128)(2,1)S(1)}, u32[]{:S(2)}, u32[]{:S(2)}) collective-permute-start(bf16[16,1024]{1,0:T(8,128)(2,1)S(1)} %merge.1.a_ref), channel_id=1, source_target_pairs={{0,1},{1,2},{2,3},{3,0},{4,5},{5,6},{6,7},{7,4},{8,9},{9,10},{10,1... | collective-permute-start | bytes 98312 | tf_op jit(solution)/shard_map/ppermute | solution.py:663
  92.2 4.4 %collective-permute-start.3 = (bf16[16,16,512]{2,1,0:T(8,128)(2,1)S(1)}, bf16[16,16,512]{2,1,0:T(8,128)(2,1)S(1)}, u32[]{:S(2)}, u32[]{:S(2)}) collective-permute-start(bf16[16,16,512]{2,1,0:T(8,128)(2,1)S(1)} %all_to_all.15.own_ref), channel_id=1, source_target_pairs={{0,4},{4,0},{8,12},{12,8},{16,20},{20,16},{24,28},{28,24},{32,36},... | collective-permute-start | bytes 786440 | tf_op jit(solution)/shard_map/ppermute | solution.py:657
  98.1 6.0 %copy-start = (bf16[1024,1024]{1,0:T(8,128)(2,1)S(1)}, bf16[1024,1024]{1,0:T(8,128)(2,1)}, u32[]{:S(2)}) copy-start(bf16[1024,1024]{1,0:T(8,128)(2,1)} %w1_ref.1) | copy-start | bytes 6291460
  98.1 6.0 %copy-start.4 = (f32[1024]{0:T(1024)S(1)}, f32[1024]{0:T(1024)}, u32[]{:S(2)}) copy-start(f32[1024]{0:T(1024)} %param.41) | copy-start | bytes 12292
  98.1 4.0 %collective-permute-start.6 = (bf16[16,1024]{1,0:T(8,128)(2,1)S(1)}, bf16[16,1024]{1,0:T(8,128)(2,1)S(1)}, u32[]{:S(2)}, u32[]{:S(2)}) collective-permute-start(bf16[16,1024]{1,0:T(8,128)(2,1)S(1)} %attend.1.a_ref), channel_id=1, source_target_pairs={{0,3},{1,0},{2,1},{3,2},{4,7},{5,4},{6,5},{7,6},{8,11},{9,8},{10,9... | collective-permute-start | bytes 98312 | tf_op jit(solution)/shard_map/ppermute | solution.py:663
  98.5 4.3 %collective-permute-start.5 = (bf16[16,1024]{1,0:T(8,128)(2,1)S(1)}, bf16[16,1024]{1,0:T(8,128)(2,1)S(1)}, u32[]{:S(2)}, u32[]{:S(2)}) collective-permute-start(bf16[16,1024]{1,0:T(8,128)(2,1)S(1)} %attend.1.a_ref), channel_id=1, source_target_pairs={{0,2},{1,3},{2,0},{3,1},{4,6},{5,7},{6,4},{7,5},{8,10},{9,11},{10,... | collective-permute-start | bytes 98312 | tf_op jit(solution)/shard_map/ppermute | solution.py:663
  99.7 4.4 %collective-permute-start.4 = (bf16[16,1024]{1,0:T(8,128)(2,1)S(1)}, bf16[16,1024]{1,0:T(8,128)(2,1)S(1)}, u32[]{:S(2)}, u32[]{:S(2)}) collective-permute-start(bf16[16,1024]{1,0:T(8,128)(2,1)S(1)} %attend.1.a_ref), channel_id=1, source_target_pairs={{0,1},{1,2},{2,3},{3,0},{4,5},{5,6},{6,7},{7,4},{8,9},{9,10},{10,1... | collective-permute-start | bytes 98312 | tf_op jit(solution)/shard_map/ppermute | solution.py:663
  100.4 28.5 %copy-start.13 = (f32[16,2048]{1,0:T(8,128)S(1)}, f32[16,2048]{1,0:T(8,128)}, u32[]{:S(2)}) copy-start(f32[16,2048]{1,0:T(8,128)} %get-tuple-element.53.top_ref) | copy-start | bytes 393220
  104.2 6.5 %copy-start.5 = (f32[1024]{0:T(1024)S(1)}, f32[1024]{0:T(1024)}, u32[]{:S(2)}) copy-start(f32[1024]{0:T(1024)} %param.44) | copy-start | bytes 12292
  104.2 24.8 %copy-start.6 = (bf16[2,1024,1024]{2,1,0:T(8,128)(2,1)S(1)}, bf16[2,1024,1024]{2,1,0:T(8,128)(2,1)}, u32[]{:S(2)}) copy-start(bf16[2,1024,1024]{2,1,0:T(8,128)(2,1)} %wkv_ref.3) | copy-start | bytes 12582916
  104.2 24.8 %copy-start.7 = (bf16[2048,256]{1,0:T(8,128)(2,1)S(1)}, bf16[2048,256]{1,0:T(8,128)(2,1)}, u32[]{:S(2)}) copy-start(bf16[2048,256]{1,0:T(8,128)(2,1)} %x_ref.4) | copy-start | bytes 3145732
  104.2 24.8 %copy-start.8 = (f32[3,256]{1,0:T(4,128)S(1)}, f32[3,256]{1,0:T(4,128)}, u32[]{:S(2)}) copy-start(f32[3,256]{1,0:T(4,128)} %table_ref.5) | copy-start | bytes 9220
  104.2 24.8 %copy-start.9 = (s32[16]{0:T(128)S(1)}, s32[16]{0:T(128)}, u32[]{:S(2)}) copy-start(s32[16]{0:T(128)} %mod_ref.5) | copy-start | bytes 196
  104.2 24.8 %copy-start.10 = (bf16[256,1024]{1,0:T(8,128)(2,1)S(1)}, bf16[256,1024]{1,0:T(8,128)(2,1)}, u32[]{:S(2)}) copy-start(bf16[256,1024]{1,0:T(8,128)(2,1)} %get-tuple-element.54.wot_ref) | copy-start | bytes 1572868
  104.2 24.8 %copy-start.11 = (bf16[2,512,128]{2,1,0:T(8,128)(2,1)S(1)}, bf16[2,512,128]{2,1,0:T(8,128)(2,1)}, u32[]{:S(2)}) copy-start(bf16[2,512,128]{2,1,0:T(8,128)(2,1)} %get-tuple-element.50.bias_ref) | copy-start | bytes 786436
  104.2 24.8 %copy-start.12 = (f32[16,2048]{1,0:T(8,128)S(1)}, f32[16,2048]{1,0:T(8,128)}, u32[]{:S(2)}) copy-start(f32[16,2048]{1,0:T(8,128)} %get-tuple-element.52.norm_ref) | copy-start | bytes 393220
  105.1 2.8 %collective-permute-start.9 = (bf16[16,1024]{1,0:T(8,128)(2,1)S(1)}, bf16[16,1024]{1,0:T(8,128)(2,1)S(1)}, u32[]{:S(2)}, u32[]{:S(2)}) collective-permute-start(bf16[16,1024]{1,0:T(8,128)(2,1)S(1)} %get-tuple-element.48.a_ref), channel_id=1, source_target_pairs={{0,3},{1,0},{2,1},{3,2},{4,7},{5,4},{6,5},{7,6},{8,11},{9,8},{10,9... | collective-permute-start | bytes 98312 | tf_op jit(solution)/shard_map/ppermute | solution.py:663
  106.1 4.3 %collective-permute-start.8 = (bf16[16,1024]{1,0:T(8,128)(2,1)S(1)}, bf16[16,1024]{1,0:T(8,128)(2,1)S(1)}, u32[]{:S(2)}, u32[]{:S(2)}) collective-permute-start(bf16[16,1024]{1,0:T(8,128)(2,1)S(1)} %get-tuple-element.48.a_ref), channel_id=1, source_target_pairs={{0,2},{1,3},{2,0},{3,1},{4,6},{5,7},{6,4},{7,5},{8,10},{9,11},{10,... | collective-permute-start | bytes 98312 | tf_op jit(solution)/shard_map/ppermute | solution.py:663
  106.7 4.0 %collective-permute-start.7 = (bf16[16,1024]{1,0:T(8,128)(2,1)S(1)}, bf16[16,1024]{1,0:T(8,128)(2,1)S(1)}, u32[]{:S(2)}, u32[]{:S(2)}) collective-permute-start(bf16[16,1024]{1,0:T(8,128)(2,1)S(1)} %get-tuple-element.48.a_ref), channel_id=1, source_target_pairs={{0,1},{1,2},{2,3},{3,0},{4,5},{5,6},{6,7},{7,4},{8,9},{9,10},{10,1... | collective-permute-start | bytes 98312 | tf_op jit(solution)/shard_map/ppermute | solution.py:663
  122.8 6.1 %collective-permute-start.10 = (bf16[16,16,1024]{2,1,0:T(8,128)(2,1)S(1)}, bf16[16,16,1024]{2,1,0:T(8,128)(2,1)S(1)}, u32[]{:S(2)}, u32[]{:S(2)}) collective-permute-start(bf16[16,16,1024]{2,1,0:T(8,128)(2,1)S(1)} %all_to_all.16.own_ref), channel_id=1, source_target_pairs={{0,4},{4,0},{8,12},{12,8},{16,20},{20,16},{24,28},{28,24},{32,36},... | collective-permute-start | bytes 1572872 | tf_op jit(solution)/shard_map/ppermute | solution.py:657

commit v6 on v5

--- a/solution.py
+++ b/solution.py
@@ -762,16 +762,18 @@
         mlp_w1,
         weights,
     )
+    mlp_part, near_queries = fetch(mlp_part, prepared[0])
+    mlp_parts, near_queries = lax.optimization_barrier((head_parts(mlp_part), near_queries))
+    prepared = (near_queries, *prepared[1:])
     normed = small_call(
         last_kernel,
         "last",
         shape((chips, lat_rows, width), BF),
-        *head_parts(mlp_part),
+        *mlp_parts,
         lat_two,
         row(dec_gain),
     )
     own = trade(normed)
-    prepared = (pltpu.with_memory_space_constraint(prepared[0], pltpu.HBM), *prepared[1:])
     return decode(
         core, queries, query_modality, modality_embed, own, other_core(own), dec_wkv, prepared
     )

time: 153 us -> 152 us (level)
  waiting for transfers between devices: 12.2 us -> 9.9 us
    pallas_call x2 -> x3, Pallas kernels: 3.06 us -> 5.37 us  [fetch(): pl.pallas_call(functools.partial(fetch_kernel, len(arrays)), out_shape=[j...]
    ppermute x9, waiting for transfers between devices: 7.27 us -> 4.97 us  [head_parts(): lax.ppermute(part, 'head', [(i, (i + k) % size) for i in range(size)])]
  transfers between devices with their start and end apart: 12 -> 12, of which waited for: 10 -> 9; matrix products, arithmetic and copies ran while one was open for 1% -> 1% of each run, Pallas kernels for 7% -> 9%
where the time goes in v6:
time: 152 us; the launch traced here: 151 us
  Pallas kernels  91.4 us (60%)
  starting transfers between devices  25.2 us (17%)
  blocking collectives  23.7 us (16%)
  waiting for transfers between devices  9.9 us (7%)
    pallas_call x1, Pallas kernels, encode(): pl.pallas_call(functools.partial(encode_kernel, heads), grid_spec=pltpu.P...  52 us
    all_to_all x2, blocking collectives, trade(): return lax.all_to_all(parts, 'inp', 0, 0, axis_index_groups=groups)  23.7 us
    pallas_call x1, Pallas kernels, decode(): pl.pallas_call(functools.partial(decode_kernel, heads), grid_spec=pltpu.P...  22.2 us
    all_to_all x1, starting transfers between devices, body(): lax.all_to_all(partial.reshape(-1, lat_rows, partial.shape[1]), 'inp', 0, 0)  9.62 us
    pallas_call x1, Pallas kernels, prepare_queries(): pl.pallas_call(functools.partial(query_kernel, heads), grid_spec=pltpu.Pr...  7.91 us
    ppermute x2, starting transfers between devices, other_core(): lax.ppermute(rows, 'inp', [(i, i ^ 1) for i in range(lax.axis_size('inp'))])  7.82 us
    ppermute x9, starting transfers between devices, head_parts(): lax.ppermute(part, 'head', [(i, (i + k) % size) for i in range(size)])  7.77 us
    pallas_call x3, Pallas kernels, fetch(): pl.pallas_call(functools.partial(fetch_kernel, len(arrays)), out_shape=[j...  5.37 us
  transfers between devices with their start and end apart: 12, of which 9 were waited for; matrix products, arithmetic and copies ran while one was open for 1% of the time, Pallas kernels for 9%

profile of v6, /device:TPU:1, one launch (start us, length us, event | category | flops | bytes accessed | tf_op | source)
XLA Modules:
  0.0 151.3 jit_solution(8446712860206686450)
XLA Ops:
  0.0 52.0 %encode.1 = bf16[512,384]{1,0:T(8,128)(2,1)} custom-call(s32[64]{0:T(128)} %mod_ref.3, bf16[8192,256]{1,0:T(8,128)(2,1)} %next_ref.1, bf16[8192,256]{1,0:T(8,128)(2,1)} %next_ref.1, f32[3,256]{1,0:T(4,128)} %table_ref.5, f32[1,256]{1,0:T(1,128)} %bitcast.13, f32[512,1024]{1,0:T(8,128)} %lat_ref.1, f32[1,1024]{1,0:T(1,128)} %bitcast.12, ...), custom_call_target="tpu_custom_call" | custom-call | flops 12884901888 | bytes 11272192 | tf_op jit(solution)/shard_map/encode/pallas_call | solution.py:235
  52.0 9.6 %all-to-all-start = ((bf16[32,16,384]{2,1,0:T(8,128)(2,1)}), bf16[32,16,384]{2,1,0:T(8,128)(2,1)S(1)}, u32[]{:S(2)}, u32[]{:S(2)}) async-start(bf16[32,16,384]{2,1,0:T(8,128)(2,1)} %bitcast.11), calls=%async_computation | async-start | bytes 786432 | tf_op jit(solution)/shard_map/all_to_all | solution.py:718
  61.7 0.0 copy-start.1
  61.7 7.9 %queries.1 = (bf16[1024,2048]{1,0:T(8,128)(2,1)}, f32[16,2048]{1,0:T(8,128)}, f32[16,2048]{1,0:T(8,128)}, bf16[2,512,128]{2,1,0:T(8,128)(2,1)}, bf16[256,1024]{1,0:T(8,128)(2,1)}) custom-call(s32[16]{0:T(128)} %mod_ref.5, bf16[2048,256]{1,0:T(8,128)(2,1)} %x_ref.4, f32[3,256]{1,0:T(4,128)} %table_ref.5, f32[1,256]{1,0:T(1,128)} %bitcast.14, ...), custom_call_target="tpu_custom_call" | custom-call | flops 1073741824 | bytes 6291456 | tf_op jit(solution)/shard_map/queries/pallas_call | solution.py:424
  69.6 0.0 copy-start.3
  69.6 2.2 %all-to-all-done.part_ref = bf16[32,16,384]{2,1,0:T(8,128)(2,1)S(1)} async-done(((bf16[32,16,384]{2,1,0:T(8,128)(2,1)}), bf16[32,16,384]{2,1,0:T(8,128)(2,1)S(1)}, u32[]{:S(2)}, u32[]{:S(2)}) %all-to-all-start) | async-done | bytes 393248 | tf_op jit(solution)/shard_map/all_to_all | solution.py:718
  71.8 0.0 copy-done.1
  71.8 0.7 merge.1.a_ref
  72.6 0.0 copy-start.2
  72.6 2.7 %collective-permute-start.2 = (bf16[16,1024]{1,0:T(8,128)(2,1)S(1)}, bf16[16,1024]{1,0:T(8,128)(2,1)S(1)}, u32[]{:S(2)}, u32[]{:S(2)}) collective-permute-start(bf16[16,1024]{1,0:T(8,128)(2,1)S(1)} %merge.1.a_ref), channel_id=1, source_target_pairs={{0,3},{1,0},{2,1},{3,2},{4,7},{5,4},{6,5},{7,6},{8,11},{9,8},{10,9... | collective-permute-start | bytes 98312 | tf_op jit(solution)/shard_map/ppermute | solution.py:663
  75.3 0.3 collective-permute-start.1
  75.6 0.7 collective-permute-start
  76.3 0.8 constant_dynamic-slice_fusion.lat_ref
  77.2 1.4 fetch.3
  78.6 0.0 collective-permute-done.2.d_ref
  78.6 1.0 collective-permute-done.1.c_ref
  79.6 0.3 collective-permute-done.b_ref
  79.9 0.0 copy-done.3
  79.9 0.5 project.1
  80.4 11.8 %all_to_all.15.own_ref = bf16[16,16,512]{2,1,0:T(8,128)(2,1)S(1)} all-to-all(bf16[16,16,512]{2,1,0:T(8,128)(2,1)S(1)} %get-tuple-element.50), channel_id=1, replica_groups={{0,8,16,24,32,40,48,56,64,72,80,88,96,104,112,120},{4,12,20,28,36,44,52..., dimensions={0} | all-to-all | bytes 524288 | tf_op jit(solution)/shard_map/all_to_all | solution.py:653
  92.2 3.2 %collective-permute-start.3 = (bf16[16,16,512]{2,1,0:T(8,128)(2,1)S(1)}, bf16[16,16,512]{2,1,0:T(8,128)(2,1)S(1)}, u32[]{:S(2)}, u32[]{:S(2)}) collective-permute-start(bf16[16,16,512]{2,1,0:T(8,128)(2,1)S(1)} %all_to_all.15.own_ref), channel_id=1, source_target_pairs={{0,4},{4,0},{8,12},{12,8},{16,20},{20,16},{24,28},{28,24},{32,36},... | collective-permute-start | bytes 786440 | tf_op jit(solution)/shard_map/ppermute | solution.py:657
  95.5 1.2 collective-permute-done.3.other_ref
  96.6 0.0 copy-done.2
  96.6 1.5 attend.1.a_ref
  98.1 0.0 copy-start
  98.1 0.0 copy-start.4
  98.1 0.3 collective-permute-start.6
  98.5 1.3 collective-permute-start.5
  99.7 0.7 collective-permute-start.4
  100.4 1.6 %fetch.4.w2_ref = bf16[1024,1024]{1,0:T(8,128)(2,1)S(1)} custom-call(bf16[1024,1024]{1,0:T(8,128)(2,1)} %refs_0_.1), custom_call_target="tpu_custom_call" | custom-call | bytes 4194304 | tf_op jit(solution)/shard_map/fetch/pallas_call | solution.py:635
  102.1 0.0 collective-permute-done.6.d_ref
  102.1 0.7 collective-permute-done.5.c_ref
  102.7 1.4 collective-permute-done.4.b_ref
  104.2 0.0 copy-done
  104.2 0.0 copy-done.4
  104.2 0.8 mlp.1
  105.0 0.0 copy-start.7
  105.0 0.0 copy-start.8
  105.0 0.0 copy-start.9
  105.0 0.0 copy-start.10
  105.1 0.0 copy-start.11
  105.1 0.0 copy-start.12
  105.1 0.0 copy-start.13
  105.1 1.0 collective-permute-start.9
  106.1 0.6 collective-permute-start.8
  106.7 0.1 collective-permute-start.7
  106.8 2.3 %fetch.5.qt_ref = bf16[1024,2048]{1,0:T(8,128)(2,1)S(1)} custom-call(bf16[1024,2048]{1,0:T(8,128)(2,1)} %get-tuple-element.58.refs_0_), custom_call_target="tpu_custom_call" | custom-call | bytes 8388608 | tf_op jit(solution)/shard_map/fetch/pallas_call | solution.py:635
  109.1 0.0 collective-permute-done.9.d_ref
  109.2 1.2 collective-permute-done.8.c_ref
  110.4 0.4 collective-permute-done.7.b_ref
  110.7 0.0 copy-done.5
  110.7 0.2 last.1
  111.0 11.9 %all_to_all.16.own_ref = bf16[16,16,1024]{2,1,0:T(8,128)(2,1)S(1)} all-to-all(bf16[16,16,1024]{2,1,0:T(8,128)(2,1)S(1)} %last.1), channel_id=1, replica_groups={{0,8,16,24,32,40,48,56,64,72,80,88,96,104,112,120},{4,12,20,28,36,44,52..., dimensions={0} | all-to-all | bytes 1048576 | tf_op jit(solution)/shard_map/all_to_all | solution.py:653
  122.9 4.6 %collective-permute-start.10 = (bf16[16,16,1024]{2,1,0:T(8,128)(2,1)S(1)}, bf16[16,16,1024]{2,1,0:T(8,128)(2,1)S(1)}, u32[]{:S(2)}, u32[]{:S(2)}) collective-permute-start(bf16[16,16,1024]{2,1,0:T(8,128)(2,1)S(1)} %all_to_all.16.own_ref), channel_id=1, source_target_pairs={{0,4},{4,0},{8,12},{12,8},{16,20},{20,16},{24,28},{28,24},{32,36},... | collective-permute-start | bytes 1572872 | tf_op jit(solution)/shard_map/ppermute | solution.py:657
  127.5 1.5 %collective-permute-done.10.other_ref = bf16[16,16,1024]{2,1,0:T(8,128)(2,1)S(1)} collective-permute-done((bf16[16,16,1024]{2,1,0:T(8,128)(2,1)S(1)}, bf16[16,16,1024]{2,1,0:T(8,128)(2,1)S(1)}, u32[]{:S(2)}, u32[]{:S(2)}) %collective-permute-start.10) | collective-permute-done | bytes 524320 | tf_op jit(solution)/shard_map/ppermute | solution.py:657
  129.0 0.0 copy-done.6
  129.0 0.0 copy-done.7
  129.0 0.0 copy-done.8
  129.0 0.0 copy-done.9
  129.0 0.0 copy-done.10
  129.0 0.0 copy-done.11
  129.1 0.0 copy-done.12
  129.1 0.0 copy-done.13
  129.1 22.2 %decode.1 = f32[2048,256]{1,0:T(8,128)} custom-call(s32[16]{0:T(128)S(1)} %copy-done.9, s32[1]{0:T(128)} %bitcast.core_ref, bf16[2048,256]{1,0:T(8,128)(2,1)S(1)} %copy-done.7, f32[3,256]{1,0:T(4,128)S(1)} %copy-done.8, bf16[16,16,1024]{2,1,0:T(8,128)(2,1)S(1)} %all_to_all.16.own_ref, bf16[16,16,1024]{2,1,0:T(8,128)(2,1)S(1)} %collective-permute-done.10.other_ref, ...), custom_call_target="tpu_custom_call" | custom-call | flops 13958643712 | bytes 11534336 | tf_op jit(solution)/shard_map/decode/pallas_call | solution.py:582
  (2 shorter events, 0.0 us)
Async XLA Ops:
  52.0 19.8 %all-to-all-start = ((bf16[32,16,384]{2,1,0:T(8,128)(2,1)}), bf16[32,16,384]{2,1,0:T(8,128)(2,1)S(1)}, u32[]{:S(2)}, u32[]{:S(2)}) async-start(bf16[32,16,384]{2,1,0:T(8,128)(2,1)} %bitcast.11), calls=%async_computation | async-start | bytes 786432 | tf_op jit(solution)/shard_map/all_to_all | solution.py:718
  61.7 10.2 %copy-start.1 = (bf16[256,1024]{1,0:T(8,128)(2,1)S(1)}, bf16[256,1024]{1,0:T(8,128)(2,1)}, u32[]{:S(2)}) copy-start(bf16[256,1024]{1,0:T(8,128)(2,1)} %wo_ref.4) | copy-start | bytes 1572868
  69.6 10.3 %copy-start.3 = (f32[1024]{0:T(1024)S(1)}, f32[1024]{0:T(1024)}, u32[]{:S(2)}) copy-start(f32[1024]{0:T(1024)} %param.37) | copy-start | bytes 12292
  72.6 24.1 %copy-start.2 = (bf16[256,1024]{1,0:T(8,128)(2,1)S(1)}, bf16[256,1024]{1,0:T(8,128)(2,1)}, u32[]{:S(2)}) copy-start(bf16[256,1024]{1,0:T(8,128)(2,1)} %wo_ref.5) | copy-start | bytes 1572868
  72.6 6.0 %collective-permute-start.2 = (bf16[16,1024]{1,0:T(8,128)(2,1)S(1)}, bf16[16,1024]{1,0:T(8,128)(2,1)S(1)}, u32[]{:S(2)}, u32[]{:S(2)}) collective-permute-start(bf16[16,1024]{1,0:T(8,128)(2,1)S(1)} %merge.1.a_ref), channel_id=1, source_target_pairs={{0,3},{1,0},{2,1},{3,2},{4,7},{5,4},{6,5},{7,6},{8,11},{9,8},{10,9... | collective-permute-start | bytes 98312 | tf_op jit(solution)/shard_map/ppermute | solution.py:663
  75.3 4.3 %collective-permute-start.1 = (bf16[16,1024]{1,0:T(8,128)(2,1)S(1)}, bf16[16,1024]{1,0:T(8,128)(2,1)S(1)}, u32[]{:S(2)}, u32[]{:S(2)}) collective-permute-start(bf16[16,1024]{1,0:T(8,128)(2,1)S(1)} %merge.1.a_ref), channel_id=1, source_target_pairs={{0,2},{1,3},{2,0},{3,1},{4,6},{5,7},{6,4},{7,5},{8,10},{9,11},{10,... | collective-permute-start | bytes 98312 | tf_op jit(solution)/shard_map/ppermute | solution.py:663
  75.6 4.3 %collective-permute-start = (bf16[16,1024]{1,0:T(8,128)(2,1)S(1)}, bf16[16,1024]{1,0:T(8,128)(2,1)S(1)}, u32[]{:S(2)}, u32[]{:S(2)}) collective-permute-start(bf16[16,1024]{1,0:T(8,128)(2,1)S(1)} %merge.1.a_ref), channel_id=1, source_target_pairs={{0,1},{1,2},{2,3},{3,0},{4,5},{5,6},{6,7},{7,4},{8,9},{9,10},{10,1... | collective-permute-start | bytes 98312 | tf_op jit(solution)/shard_map/ppermute | solution.py:663
  92.2 4.4 %collective-permute-start.3 = (bf16[16,16,512]{2,1,0:T(8,128)(2,1)S(1)}, bf16[16,16,512]{2,1,0:T(8,128)(2,1)S(1)}, u32[]{:S(2)}, u32[]{:S(2)}) collective-permute-start(bf16[16,16,512]{2,1,0:T(8,128)(2,1)S(1)} %all_to_all.15.own_ref), channel_id=1, source_target_pairs={{0,4},{4,0},{8,12},{12,8},{16,20},{20,16},{24,28},{28,24},{32,36},... | collective-permute-start | bytes 786440 | tf_op jit(solution)/shard_map/ppermute | solution.py:657
  98.1 6.0 %copy-start = (bf16[1024,1024]{1,0:T(8,128)(2,1)S(1)}, bf16[1024,1024]{1,0:T(8,128)(2,1)}, u32[]{:S(2)}) copy-start(bf16[1024,1024]{1,0:T(8,128)(2,1)} %w1_ref.1) | copy-start | bytes 6291460
  98.1 6.0 %copy-start.4 = (f32[1024]{0:T(1024)S(1)}, f32[1024]{0:T(1024)}, u32[]{:S(2)}) copy-start(f32[1024]{0:T(1024)} %param.41) | copy-start | bytes 12292
  98.1 3.9 %collective-permute-start.6 = (bf16[16,1024]{1,0:T(8,128)(2,1)S(1)}, bf16[16,1024]{1,0:T(8,128)(2,1)S(1)}, u32[]{:S(2)}, u32[]{:S(2)}) collective-permute-start(bf16[16,1024]{1,0:T(8,128)(2,1)S(1)} %attend.1.a_ref), channel_id=1, source_target_pairs={{0,3},{1,0},{2,1},{3,2},{4,7},{5,4},{6,5},{7,6},{8,11},{9,8},{10,9... | collective-permute-start | bytes 98312 | tf_op jit(solution)/shard_map/ppermute | solution.py:663
  98.5 4.3 %collective-permute-start.5 = (bf16[16,1024]{1,0:T(8,128)(2,1)S(1)}, bf16[16,1024]{1,0:T(8,128)(2,1)S(1)}, u32[]{:S(2)}, u32[]{:S(2)}) collective-permute-start(bf16[16,1024]{1,0:T(8,128)(2,1)S(1)} %attend.1.a_ref), channel_id=1, source_target_pairs={{0,2},{1,3},{2,0},{3,1},{4,6},{5,7},{6,4},{7,5},{8,10},{9,11},{10,... | collective-permute-start | bytes 98312 | tf_op jit(solution)/shard_map/ppermute | solution.py:663
  99.7 4.4 %collective-permute-start.4 = (bf16[16,1024]{1,0:T(8,128)(2,1)S(1)}, bf16[16,1024]{1,0:T(8,128)(2,1)S(1)}, u32[]{:S(2)}, u32[]{:S(2)}) collective-permute-start(bf16[16,1024]{1,0:T(8,128)(2,1)S(1)} %attend.1.a_ref), channel_id=1, source_target_pairs={{0,1},{1,2},{2,3},{3,0},{4,5},{5,6},{6,7},{7,4},{8,9},{9,10},{10,1... | collective-permute-start | bytes 98312 | tf_op jit(solution)/shard_map/ppermute | solution.py:663
  105.0 5.7 %copy-start.5 = (f32[1024]{0:T(1024)S(1)}, f32[1024]{0:T(1024)}, u32[]{:S(2)}) copy-start(f32[1024]{0:T(1024)} %param.44) | copy-start | bytes 12292
  105.0 24.0 %copy-start.6 = (bf16[2,1024,1024]{2,1,0:T(8,128)(2,1)S(1)}, bf16[2,1024,1024]{2,1,0:T(8,128)(2,1)}, u32[]{:S(2)}) copy-start(bf16[2,1024,1024]{2,1,0:T(8,128)(2,1)} %wkv_ref.3) | copy-start | bytes 12582916
  105.0 24.0 %copy-start.7 = (bf16[2048,256]{1,0:T(8,128)(2,1)S(1)}, bf16[2048,256]{1,0:T(8,128)(2,1)}, u32[]{:S(2)}) copy-start(bf16[2048,256]{1,0:T(8,128)(2,1)} %x_ref.4) | copy-start | bytes 3145732
  105.0 24.0 %copy-start.8 = (f32[3,256]{1,0:T(4,128)S(1)}, f32[3,256]{1,0:T(4,128)}, u32[]{:S(2)}) copy-start(f32[3,256]{1,0:T(4,128)} %table_ref.5) | copy-start | bytes 9220
  105.0 24.0 %copy-start.9 = (s32[16]{0:T(128)S(1)}, s32[16]{0:T(128)}, u32[]{:S(2)}) copy-start(s32[16]{0:T(128)} %mod_ref.5) | copy-start | bytes 196
  105.0 24.0 %copy-start.10 = (bf16[256,1024]{1,0:T(8,128)(2,1)S(1)}, bf16[256,1024]{1,0:T(8,128)(2,1)}, u32[]{:S(2)}) copy-start(bf16[256,1024]{1,0:T(8,128)(2,1)} %get-tuple-element.68.wot_ref) | copy-start | bytes 1572868
  105.1 24.0 %copy-start.11 = (bf16[2,512,128]{2,1,0:T(8,128)(2,1)S(1)}, bf16[2,512,128]{2,1,0:T(8,128)(2,1)}, u32[]{:S(2)}) copy-start(bf16[2,512,128]{2,1,0:T(8,128)(2,1)} %get-tuple-element.64.bias_ref) | copy-start | bytes 786436
  105.1 24.0 %copy-start.12 = (f32[16,2048]{1,0:T(8,128)S(1)}, f32[16,2048]{1,0:T(8,128)}, u32[]{:S(2)}) copy-start(f32[16,2048]{1,0:T(8,128)} %get-tuple-element.66.norm_ref) | copy-start | bytes 393220
  105.1 24.0 %copy-start.13 = (f32[16,2048]{1,0:T(8,128)S(1)}, f32[16,2048]{1,0:T(8,128)}, u32[]{:S(2)}) copy-start(f32[16,2048]{1,0:T(8,128)} %get-tuple-element.67.top_ref) | copy-start | bytes 393220
  105.1 4.1 %collective-permute-start.9 = (bf16[16,1024]{1,0:T(8,128)(2,1)S(1)}, bf16[16,1024]{1,0:T(8,128)(2,1)S(1)}, u32[]{:S(2)}, u32[]{:S(2)}) collective-permute-start(bf16[16,1024]{1,0:T(8,128)(2,1)S(1)} %get-tuple-element.59.a_ref), channel_id=1, source_target_pairs={{0,3},{1,0},{2,1},{3,2},{4,7},{5,4},{6,5},{7,6},{8,11},{9,8},{10,9... | collective-permute-start | bytes 98312 | tf_op jit(solution)/shard_map/ppermute | solution.py:663
  106.1 4.3 %collective-permute-start.8 = (bf16[16,1024]{1,0:T(8,128)(2,1)S(1)}, bf16[16,1024]{1,0:T(8,128)(2,1)S(1)}, u32[]{:S(2)}, u32[]{:S(2)}) collective-permute-start(bf16[16,1024]{1,0:T(8,128)(2,1)S(1)} %get-tuple-element.59.a_ref), channel_id=1, source_target_pairs={{0,2},{1,3},{2,0},{3,1},{4,6},{5,7},{6,4},{7,5},{8,10},{9,11},{10,... | collective-permute-start | bytes 98312 | tf_op jit(solution)/shard_map/ppermute | solution.py:663
  106.7 4.0 %collective-permute-start.7 = (bf16[16,1024]{1,0:T(8,128)(2,1)S(1)}, bf16[16,1024]{1,0:T(8,128)(2,1)S(1)}, u32[]{:S(2)}, u32[]{:S(2)}) collective-permute-start(bf16[16,1024]{1,0:T(8,128)(2,1)S(1)} %get-tuple-element.59.a_ref), channel_id=1, source_target_pairs={{0,1},{1,2},{2,3},{3,0},{4,5},{5,6},{6,7},{7,4},{8,9},{9,10},{10,1... | collective-permute-start | bytes 98312 | tf_op jit(solution)/shard_map/ppermute | solution.py:663
  122.9 6.1 %collective-permute-start.10 = (bf16[16,16,1024]{2,1,0:T(8,128)(2,1)S(1)}, bf16[16,16,1024]{2,1,0:T(8,128)(2,1)S(1)}, u32[]{:S(2)}, u32[]{:S(2)}) collective-permute-start(bf16[16,16,1024]{2,1,0:T(8,128)(2,1)S(1)} %all_to_all.16.own_ref), channel_id=1, source_target_pairs={{0,4},{4,0},{8,12},{12,8},{16,20},{20,16},{24,28},{28,24},{32,36},... | collective-permute-start | bytes 1572872 | tf_op jit(solution)/shard_map/ppermute | solution.py:657
